TPU v7x, 32 devices: a whole 2x2x4 slice. The times are simulated.
32 devices in a mesh: gx: 4 (over x, core), gy: 4 (over z), gz: 2 (over y).
Axes of the slice: x: 2, y: 2, z: 4, core: 2. Of those that a mesh axis runs over, the one named last changes fastest.
Arguments:
- iterate: float32 [64, 128, 256], P('gx', 'gy', 'gz'), may hold values from -6 to 6
- residual: float32 [64, 128, 256], P('gx', 'gy', 'gz'), may hold values from -6 to 6
- direction: float32 [64, 128, 256], P('gx', 'gy', 'gz'), may hold values from -1.5 to 1.5
- permeability: float32 [64, 128, 256], P('gx', 'gy', 'gz'), may hold values from 1 to 16
- unfixed_node_mask: int32 [64, 128, 256], P('gx', 'gy', 'gz'), may hold values 0 or 1
- rz_prev: float32 [1], replicated, may hold values from 26214.4 to 104857.6
Outputs:
- updated_potential_values: float32 [64, 128, 256], P('gx', 'gy', 'gz')
- new_residual: float32 [64, 128, 256], P('gx', 'gy', 'gz')
- new_direction: float32 [64, 128, 256], P('gx', 'gy', 'gz')
All inputs are finite; a program needn't handle non-finite values. No bound on the sum of `unfixed_node_mask` on one device may be relied on, other than what follows from the above.
Results may differ from a plain program's by a relative error of at most 0.0003.
Values sent between devices are 32-bit elements; how exact they have to be, the bound alone decides.
No kernel may reach another device: no remote copies, remote signals or barrier semaphores. Data moves between devices by JAX's collectives and lax.ppermute only.
A program may use at most 64 MiB of HBM per device.

v0:
```python
import jax
import jax.numpy as jnp
from jax import lax
from jax.sharding import PartitionSpec as P


def extended(cells, sides, width):
    for axis, dim in sides:
        count = lax.axis_size(axis)
        ends = count - 1
        head = lax.slice_in_dim(cells, 0, width, axis=dim)
        tail = lax.slice_in_dim(cells, cells.shape[dim] - width, cells.shape[dim], axis=dim)
        cells = jnp.concatenate(
            [
                lax.ppermute(tail, axis, [(i, (i + 1) % count) for i in range(ends)]),
                cells,
                lax.ppermute(head, axis, [((i + 1) % count, i) for i in range(ends)]),
            ],
            axis=dim,
        )
    return cells


def tables(n):
    idx = jnp.arange(n).astype(jnp.float32) + 1.0
    basis = jnp.sqrt(2.0 / (n + 1)) * jnp.sin(jnp.pi * idx[:, None] * idx[None, :] / (n + 1))
    values = 2.0 - 2.0 * jnp.cos(jnp.pi * idx / (n + 1))
    return (basis, values)


def rim_masks(ex, ey, ez):

    def along(n):
        ids = jnp.arange(n)
        return ((ids == 0) | (ids == n - 1), (ids >= 2) & (ids <= n - 3))

    onx, inx = along(ex)
    ony, iny = along(ey)
    onz, inz = along(ez)
    onx, inx = (onx[:, None, None], inx[:, None, None])
    ony, iny = (ony[None, :, None], iny[None, :, None])
    onz, inz = (onz[None, None, :], inz[None, None, :])
    count = onx.astype(jnp.int32) + ony.astype(jnp.int32) + onz.astype(jnp.int32)
    outer = (count <= 1).astype(jnp.float32)
    kept = (count == 0) | onx & iny & inz | ony & inx & inz | onz & inx & iny
    return (outer, kept.astype(jnp.float32))


def fdm_solve(box, coef):
    high = lax.Precision.HIGHEST
    sx, lx = tables(box.shape[0])
    sy, ly = tables(box.shape[1])
    sz, lz = tables(box.shape[2])
    work = jnp.einsum("ia,ijk->ajk", sx, box, precision=high)
    work = jnp.einsum("jb,ajk->abk", sy, work, precision=high)
    work = jnp.einsum("kc,abk->abc", sz, work, precision=high)
    work = work / (coef * (lx[:, None, None] + ly[None, :, None] + lz[None, None, :]))
    work = jnp.einsum("ia,abc->ibc", sx, work, precision=high)
    work = jnp.einsum("jb,ibc->ijc", sy, work, precision=high)
    return jnp.einsum("kc,ijc->ijk", sz, work, precision=high)


def stencil(fpad, mpad):
    center = fpad[1:-1, 1:-1, 1:-1]
    mcent = mpad[1:-1, 1:-1, 1:-1]
    pairs = [
        (fpad[2:, 1:-1, 1:-1], mpad[2:, 1:-1, 1:-1]),
        (fpad[:-2, 1:-1, 1:-1], mpad[:-2, 1:-1, 1:-1]),
        (fpad[1:-1, 2:, 1:-1], mpad[1:-1, 2:, 1:-1]),
        (fpad[1:-1, :-2, 1:-1], mpad[1:-1, :-2, 1:-1]),
        (fpad[1:-1, 1:-1, 2:], mpad[1:-1, 1:-1, 2:]),
        (fpad[1:-1, 1:-1, :-2], mpad[1:-1, 1:-1, :-2]),
    ]
    total = jnp.zeros_like(center)
    for near_f, near_m in pairs:
        total = total + 0.5 * (mcent + near_m) * (center - near_f)
    return total


def boundary_planes(stacked):
    return extended(stacked, (("gx", 1), ("gy", 2), ("gz", 3)), 1)


def build_halo_message(subdomain_parts):
    halo_message = jnp.zeros(
        (subdomain_parts.shape[0] - 2, subdomain_parts.shape[1] - 2, subdomain_parts.shape[2] - 2),
        jnp.float32,
    )
    halo_message = halo_message.at[0, 1:-1, 1:-1].set(subdomain_parts[0, 2:-2, 2:-2])
    halo_message = halo_message.at[-1, 1:-1, 1:-1].set(subdomain_parts[-1, 2:-2, 2:-2])
    halo_message = halo_message.at[1:-1, 0, 1:-1].set(subdomain_parts[2:-2, 0, 2:-2])
    halo_message = halo_message.at[1:-1, -1, 1:-1].set(subdomain_parts[2:-2, -1, 2:-2])
    halo_message = halo_message.at[1:-1, 1:-1, 0].set(subdomain_parts[2:-2, 2:-2, 0])
    halo_message = halo_message.at[1:-1, 1:-1, -1].set(subdomain_parts[2:-2, 2:-2, -1])
    return halo_message


def collect(owned, received_planes):
    owned = owned.at[0, 1:-1, 1:-1].add(received_planes[0, 2:-2, 2:-2])
    owned = owned.at[-1, 1:-1, 1:-1].add(received_planes[-1, 2:-2, 2:-2])
    owned = owned.at[1:-1, 0, 1:-1].add(received_planes[2:-2, 0, 2:-2])
    owned = owned.at[1:-1, -1, 1:-1].add(received_planes[2:-2, -1, 2:-2])
    owned = owned.at[1:-1, 1:-1, 0].add(received_planes[2:-2, 2:-2, 0])
    owned = owned.at[1:-1, 1:-1, -1].add(received_planes[2:-2, 2:-2, -1])
    return owned


def shards(iterate, residual, direction, permeability, unfixed_node_mask, rz_prev):
    extent_along_x, size_y, size_z = residual.shape
    maskf = unfixed_node_mask.astype(jnp.float32)
    masked = maskf * residual
    outer, kept = rim_masks(extent_along_x + 2, size_y + 2, size_z + 2)
    coef = jnp.mean(permeability)
    box = boundary_planes(masked[None])[0] * outer
    subdomain_parts = fdm_solve(box, coef) * kept
    halo_message = build_halo_message(subdomain_parts)
    own_part = subdomain_parts[1:-1, 1:-1, 1:-1]
    received_planes = boundary_planes(halo_message[None])[0]
    precond = collect(own_part, received_planes)
    rz = lax.psum(jnp.sum(masked * precond), ("gx", "gy", "gz"))
    beta = rz / rz_prev[0]
    new_direction = maskf * (precond + beta * direction)
    third = boundary_planes(jnp.stack([new_direction, permeability]))
    dir_ext = third[0]
    perm_ext = third[1]
    image = maskf * stencil(dir_ext, perm_ext)
    curve = lax.psum(jnp.sum(new_direction * image), ("gx", "gy", "gz"))
    alpha = rz / curve
    return (iterate + alpha * new_direction, residual - alpha * image, new_direction)


def solution(mesh):
    in_specs = (
        P("gx", "gy", "gz"),
        P("gx", "gy", "gz"),
        P("gx", "gy", "gz"),
        P("gx", "gy", "gz"),
        P("gx", "gy", "gz"),
        P(),
    )
    out_specs = (P("gx", "gy", "gz"), P("gx", "gy", "gz"), P("gx", "gy", "gz"))
    return jax.shard_map(shards, mesh=mesh, in_specs=in_specs, out_specs=out_specs, check_vma=False)
```

profile of v0, /device:TPU:0, one launch (start us, length us, event | category | flops | bytes accessed | tf_op | source)
XLA Modules:
  0.0 200.4 jit_solution(18307225097064954946)
XLA Ops:
  1.7 2.5 %collective-permute-start = (f32[1,1,32,128]{3,2,1,0:T(8,128)S(1)}, f32[1,1,32,128]{3,2,1,0:T(8,128)S(1)}, u32[]{:S(2)}, u32[]{:S(2)}) collective-permute-start(f32[1,1,32,128]{3,2,1,0:T(8,128)S(1)} %get-tuple-element.173), channel_id=1, source_target_pairs={{0,8},{8,16},{16,24},{1,9},{9,17},{17,25},{2,10},{10,18},{18,26},{... | collective-permute-start | bytes 49160 | tf_op jit(solution)/shard_map/ppermute | solution.py:15
  6.1 3.3 %collective-permute-done.1 = f32[1,1,32,128]{3,2,1,0:T(8,128)S(1)} collective-permute-done((f32[1,1,32,128]{3,2,1,0:T(8,128)S(1)}, f32[1,1,32,128]{3,2,1,0:T(8,128)S(1)}, u32[]{:S(2)}, u32[]{:S(2)}) %collective-permute-start.1) | collective-permute-done | bytes 16416 | tf_op jit(solution)/shard_map/ppermute | solution.py:17
  9.4 3.5 %collective-permute-start.2 = (f32[1,18,1,128]{3,2,1,0:T(1,128)S(1)}, f32[1,18,1,128]{3,2,1,0:T(1,128)S(1)}, u32[]{:S(2)}, u32[]{:S(2)}) collective-permute-start(f32[1,18,1,128]{3,2,1,0:T(1,128)S(1)} %get-tuple-element.169), channel_id=1, source_target_pairs={{0,2},{2,4},{4,6},{1,3},{3,5},{5,7},{8,10},{10,12},{12,14},{9,11},... | collective-permute-start | bytes 27656 | tf_op jit(solution)/shard_map/ppermute | solution.py:15
  14.3 4.2 %collective-permute-done.3 = f32[1,18,1,128]{3,2,1,0:T(1,128)S(1)} collective-permute-done((f32[1,18,1,128]{3,2,1,0:T(1,128)S(1)}, f32[1,18,1,128]{3,2,1,0:T(1,128)S(1)}, u32[]{:S(2)}, u32[]{:S(2)}) %collective-permute-start.3) | collective-permute-done | bytes 9248 | tf_op jit(solution)/shard_map/ppermute | solution.py:17
  18.7 3.4 %collective-permute-start.4 = (f32[1,18,34,1]{3,2,1,0:T(8,128)S(1)}, f32[1,18,34,1]{3,2,1,0:T(8,128)S(1)}, u32[]{:S(2)}, u32[]{:S(2)}) collective-permute-start(f32[1,18,34,1]{3,2,1,0:T(8,128)S(1)} %get-tuple-element.165), channel_id=1, source_target_pairs={{0,1},{2,3},{4,5},{6,7},{8,9},{10,11},{12,13},{14,15},{16,17},{18,... | collective-permute-start | bytes 7352 | tf_op jit(solution)/shard_map/ppermute | solution.py:15
  22.1 1.3 collective-permute-start.5
  24.8 6.2 %collective-permute-done.4 = f32[1,18,34,1]{3,2,1,0:T(8,128)S(1)} collective-permute-done((f32[1,18,34,1]{3,2,1,0:T(8,128)S(1)}, f32[1,18,34,1]{3,2,1,0:T(8,128)S(1)}, u32[]{:S(2)}, u32[]{:S(2)}) %collective-permute-start.4) | collective-permute-done | bytes 2480 | tf_op jit(solution)/shard_map/ppermute | solution.py:15
  31.0 4.3 %collective-permute-done.5 = f32[1,18,34,1]{3,2,1,0:T(8,128)S(1)} collective-permute-done((f32[1,18,34,1]{3,2,1,0:T(8,128)S(1)}, f32[1,18,34,1]{3,2,1,0:T(8,128)S(1)}, u32[]{:S(2)}, u32[]{:S(2)}) %collective-permute-start.5) | collective-permute-done | bytes 2480 | tf_op jit(solution)/shard_map/ppermute | solution.py:17
  41.4 1.3 convolution_select_fusion
  43.9 2.2 %scatter.24 = f32[1,16,32,128]{3,2,1,0:T(8,128)S(1)} dynamic-update-slice(f32[1,16,32,128]{3,2,1,0:T(8,128)S(1)} %scatter.21, f32[1,14,1,126]{3,2,1,0:T(1,128)S(1)} %get-tuple-element.156, s32[]{:T(128)} %constant.338.clone.1, s32[]{:T(128)} %constant.350.clone.1, s32[]{:T(128)} %constant.338.clone.1, s32[]{:T(128)} %constant.350.clone.1) | dynamic-update-slice | bytes 14116 | tf_op jit(solution)/shard_map/scatter | solution.py:91
  46.2 2.2 %scatter.25 = f32[1,16,32,128]{3,2,1,0:T(8,128)S(1)} dynamic-update-slice(f32[1,16,32,128]{3,2,1,0:T(8,128)S(1)} %scatter.24, f32[1,14,1,126]{3,2,1,0:T(1,128)S(1)} %get-tuple-element.155, s32[]{:T(128)} %constant.338.clone.1, s32[]{:T(128)} %constant.350.clone.1, s32[]{:T(128)} %constant.343.clone.1, s32[]{:T(128)} %constant.350.clone.1) | dynamic-update-slice | bytes 14116 | tf_op jit(solution)/shard_map/scatter | solution.py:92
  48.9 2.5 %scatter.29 = f32[1,16,32,128]{3,2,1,0:T(8,128)S(1)} dynamic-update-slice(f32[1,16,32,128]{3,2,1,0:T(8,128)S(1)} %scatter.26, f32[1,14,30,1]{3,2,1,0:T(8,128)S(1)} %get-tuple-element.153, s32[]{:T(128)} %constant.338.clone.1, s32[]{:T(128)} %constant.350.clone.1, s32[]{:T(128)} %constant.350.clone.1, s32[]{:T(128)} %constant.344.clone.1) | dynamic-update-slice | bytes 3364 | tf_op jit(solution)/shard_map/scatter | solution.py:94
  51.4 1.8 collective-permute-start.6
  54.6 1.8 collective-permute-done.7
  56.4 3.5 %collective-permute-start.8 = (f32[1,18,1,128]{3,2,1,0:T(1,128)S(1)}, f32[1,18,1,128]{3,2,1,0:T(1,128)S(1)}, u32[]{:S(2)}, u32[]{:S(2)}) collective-permute-start(f32[1,18,1,128]{3,2,1,0:T(1,128)S(1)} %get-tuple-element.167), channel_id=1, source_target_pairs={{0,2},{2,4},{4,6},{1,3},{3,5},{5,7},{8,10},{10,12},{12,14},{9,11},... | collective-permute-start | bytes 27656 | tf_op jit(solution)/shard_map/ppermute | solution.py:15
  59.8 1.3 collective-permute-start.9
  61.2 4.2 %collective-permute-done.9 = f32[1,18,1,128]{3,2,1,0:T(1,128)S(1)} collective-permute-done((f32[1,18,1,128]{3,2,1,0:T(1,128)S(1)}, f32[1,18,1,128]{3,2,1,0:T(1,128)S(1)}, u32[]{:S(2)}, u32[]{:S(2)}) %collective-permute-start.9) | collective-permute-done | bytes 9248 | tf_op jit(solution)/shard_map/ppermute | solution.py:17
  65.6 1.5 collective-permute-start.10
  67.1 1.5 collective-permute-start.11
  68.7 7.0 %collective-permute-done.10 = f32[1,18,34,1]{3,2,1,0:T(8,128)S(1)} collective-permute-done((f32[1,18,34,1]{3,2,1,0:T(8,128)S(1)}, f32[1,18,34,1]{3,2,1,0:T(8,128)S(1)}, u32[]{:S(2)}, u32[]{:S(2)}) %collective-permute-start.10) | collective-permute-done | bytes 2480 | tf_op jit(solution)/shard_map/ppermute | solution.py:15
  75.7 4.1 %collective-permute-done.11 = f32[1,18,34,1]{3,2,1,0:T(8,128)S(1)} collective-permute-done((f32[1,18,34,1]{3,2,1,0:T(8,128)S(1)}, f32[1,18,34,1]{3,2,1,0:T(8,128)S(1)}, u32[]{:S(2)}, u32[]{:S(2)}) %collective-permute-start.11) | collective-permute-done | bytes 2480 | tf_op jit(solution)/shard_map/ppermute | solution.py:17
  82.1 2.2 %scatter-add.24 = f32[16,32,128]{2,1,0:T(8,128)S(1)} dynamic-update-slice(f32[16,32,128]{2,1,0:T(8,128)S(1)} %scatter-add.21, f32[14,1,126]{2,1,0:T(1,128)S(1)} %slice_add_fusion.11, s32[]{:T(128)} %constant.350.clone.1, s32[]{:T(128)} %constant.338.clone.1, s32[]{:T(128)} %constant.350.clone.1) | dynamic-update-slice | bytes 14116 | tf_op jit(solution)/shard_map/scatter-add | solution.py:101
  84.5 2.2 %scatter-add.25 = f32[16,32,128]{2,1,0:T(8,128)S(1)} dynamic-update-slice(f32[16,32,128]{2,1,0:T(8,128)S(1)} %scatter-add.24, f32[14,1,126]{2,1,0:T(1,128)S(1)} %slice_add_fusion.10, s32[]{:T(128)} %constant.350.clone.1, s32[]{:T(128)} %constant.343.clone.1, s32[]{:T(128)} %constant.350.clone.1) | dynamic-update-slice | bytes 14116 | tf_op jit(solution)/shard_map/scatter-add | solution.py:102
  87.5 2.5 %scatter-add.29 = f32[16,32,128]{2,1,0:T(8,128)S(1)} dynamic-update-slice(f32[16,32,128]{2,1,0:T(8,128)S(1)} %scatter-add.26, f32[14,30,1]{2,1,0:T(8,128)S(1)} %slice_add_fusion.6, s32[]{:T(128)} %constant.350.clone.1, s32[]{:T(128)} %constant.350.clone.1, s32[]{:T(128)} %constant.344.clone.1) | dynamic-update-slice | bytes 3364 | tf_op jit(solution)/shard_map/scatter-add | solution.py:104
  91.3 39.6 %psum.14 = f32[]{:T(128)} all-reduce(f32[]{:T(128)} %multiply_reduce_fusion.1), channel_id=1, replica_groups=mesh['gx'=4,'gy'=4,'gz'=2] {'gx','gy','gz'}, use_global_device_ids=true, to_apply=%region_2.0 | all-reduce | flops 1 | bytes 8 | tf_op jit(solution)/shard_map/psum | solution.py:120
  134.3 4.3 %collective-permute-done.13 = f32[2,1,32,128]{3,2,1,0:T(8,128)S(1)} collective-permute-done((f32[2,1,32,128]{3,2,1,0:T(8,128)S(1)}, f32[2,1,32,128]{3,2,1,0:T(8,128)S(1)}, u32[]{:S(2)}, u32[]{:S(2)}) %collective-permute-start.13) | collective-permute-done | bytes 32800 | tf_op jit(solution)/shard_map/ppermute | solution.py:17
  138.6 2.3 %collective-permute-start.14 = (f32[2,18,1,128]{3,2,1,0:T(1,128)S(1)}, f32[2,18,1,128]{3,2,1,0:T(1,128)S(1)}, u32[]{:S(2)}, u32[]{:S(2)}) collective-permute-start(f32[2,18,1,128]{3,2,1,0:T(1,128)S(1)} %get-tuple-element.159), channel_id=1, source_target_pairs={{0,2},{2,4},{4,6},{1,3},{3,5},{5,7},{8,10},{10,12},{12,14},{9,11},... | collective-permute-start | bytes 55304 | tf_op jit(solution)/shard_map/ppermute | solution.py:15
  142.4 4.2 %collective-permute-done.15 = f32[2,18,1,128]{3,2,1,0:T(1,128)S(1)} collective-permute-done((f32[2,18,1,128]{3,2,1,0:T(1,128)S(1)}, f32[2,18,1,128]{3,2,1,0:T(1,128)S(1)}, u32[]{:S(2)}, u32[]{:S(2)}) %collective-permute-start.15) | collective-permute-done | bytes 18464 | tf_op jit(solution)/shard_map/ppermute | solution.py:17
  147.3 2.1 %collective-permute-start.16 = (f32[2,18,34,1]{2,0,3,1:T(2,128)S(1)}, f32[2,18,34,1]{2,0,3,1:T(2,128)S(1)}, u32[]{:S(2)}, u32[]{:S(2)}) collective-permute-start(f32[2,18,34,1]{2,0,3,1:T(2,128)S(1)} %copy.21), channel_id=1, source_target_pairs={{0,1},{2,3},{4,5},{6,7},{8,9},{10,11},{12,13},{14,15},{16,17},{18,... | collective-permute-start | bytes 14696 | tf_op jit(solution)/shard_map/ppermute | solution.py:15
  151.5 4.1 %collective-permute-done.17 = f32[2,18,34,1]{2,0,3,1:T(2,128)S(1)} collective-permute-done((f32[2,18,34,1]{2,0,3,1:T(2,128)S(1)}, f32[2,18,34,1]{2,0,3,1:T(2,128)S(1)}, u32[]{:S(2)}, u32[]{:S(2)}) %collective-permute-start.17) | collective-permute-done | bytes 4928 | tf_op jit(solution)/shard_map/ppermute | solution.py:17
  156.9 1.5 multiply_reduce_fusion
  158.4 39.2 %psum.15 = f32[]{:T(128)} all-reduce(f32[]{:T(128)} %get-tuple-element.147), channel_id=1, replica_groups=mesh['gx'=4,'gy'=4,'gz'=2] {'gx','gy','gz'}, use_global_device_ids=true, to_apply=%region_4.0 | all-reduce | flops 1 | bytes 8 | tf_op jit(solution)/shard_map/psum | solution.py:127
  (94 shorter events, 27.8 us)
Async XLA Ops:
  1.7 21.8 %copy-start.1 = (f32[16,32,128]{2,1,0:T(8,128)S(1)}, f32[16,32,128]{2,1,0:T(8,128)}, u32[]{:S(2)}) copy-start(f32[16,32,128]{2,1,0:T(8,128)} %param.33) | copy-start | bytes 786436
  1.7 4.4 %collective-permute-start = (f32[1,1,32,128]{3,2,1,0:T(8,128)S(1)}, f32[1,1,32,128]{3,2,1,0:T(8,128)S(1)}, u32[]{:S(2)}, u32[]{:S(2)}) collective-permute-start(f32[1,1,32,128]{3,2,1,0:T(8,128)S(1)} %get-tuple-element.173), channel_id=1, source_target_pairs={{0,8},{8,16},{16,24},{1,9},{9,17},{17,25},{2,10},{10,18},{18,26},{... | collective-permute-start | bytes 49160 | tf_op jit(solution)/shard_map/ppermute | solution.py:15
  4.2 5.2 %collective-permute-start.1 = (f32[1,1,32,128]{3,2,1,0:T(8,128)S(1)}, f32[1,1,32,128]{3,2,1,0:T(8,128)S(1)}, u32[]{:S(2)}, u32[]{:S(2)}) collective-permute-start(f32[1,1,32,128]{3,2,1,0:T(8,128)S(1)} %get-tuple-element.174), channel_id=1, source_target_pairs={{8,0},{16,8},{24,16},{9,1},{17,9},{25,17},{10,2},{18,10},{26,18},{... | collective-permute-start | bytes 49160 | tf_op jit(solution)/shard_map/ppermute | solution.py:17
  9.4 4.8 %collective-permute-start.2 = (f32[1,18,1,128]{3,2,1,0:T(1,128)S(1)}, f32[1,18,1,128]{3,2,1,0:T(1,128)S(1)}, u32[]{:S(2)}, u32[]{:S(2)}) collective-permute-start(f32[1,18,1,128]{3,2,1,0:T(1,128)S(1)} %get-tuple-element.169), channel_id=1, source_target_pairs={{0,2},{2,4},{4,6},{1,3},{3,5},{5,7},{8,10},{10,12},{12,14},{9,11},... | collective-permute-start | bytes 27656 | tf_op jit(solution)/shard_map/ppermute | solution.py:15
  12.9 5.6 %collective-permute-start.3 = (f32[1,18,1,128]{3,2,1,0:T(1,128)S(1)}, f32[1,18,1,128]{3,2,1,0:T(1,128)S(1)}, u32[]{:S(2)}, u32[]{:S(2)}) collective-permute-start(f32[1,18,1,128]{3,2,1,0:T(1,128)S(1)} %get-tuple-element.170), channel_id=1, source_target_pairs={{2,0},{4,2},{6,4},{3,1},{5,3},{7,5},{10,8},{12,10},{14,12},{11,9},... | collective-permute-start | bytes 27656 | tf_op jit(solution)/shard_map/ppermute | solution.py:17
  18.7 12.3 %collective-permute-start.4 = (f32[1,18,34,1]{3,2,1,0:T(8,128)S(1)}, f32[1,18,34,1]{3,2,1,0:T(8,128)S(1)}, u32[]{:S(2)}, u32[]{:S(2)}) collective-permute-start(f32[1,18,34,1]{3,2,1,0:T(8,128)S(1)} %get-tuple-element.165), channel_id=1, source_target_pairs={{0,1},{2,3},{4,5},{6,7},{8,9},{10,11},{12,13},{14,15},{16,17},{18,... | collective-permute-start | bytes 7352 | tf_op jit(solution)/shard_map/ppermute | solution.py:15
  22.1 13.2 %collective-permute-start.5 = (f32[1,18,34,1]{3,2,1,0:T(8,128)S(1)}, f32[1,18,34,1]{3,2,1,0:T(8,128)S(1)}, u32[]{:S(2)}, u32[]{:S(2)}) collective-permute-start(f32[1,18,34,1]{3,2,1,0:T(8,128)S(1)} %get-tuple-element.166), channel_id=1, source_target_pairs={{1,0},{3,2},{5,4},{7,6},{9,8},{11,10},{13,12},{15,14},{17,16},{19,... | collective-permute-start | bytes 7352 | tf_op jit(solution)/shard_map/ppermute | solution.py:17
  51.4 3.1 %collective-permute-start.6 = (f32[1,1,32,128]{3,2,1,0:T(8,128)S(1)}, f32[1,1,32,128]{3,2,1,0:T(8,128)S(1)}, u32[]{:S(2)}, u32[]{:S(2)}) collective-permute-start(f32[1,1,32,128]{3,2,1,0:T(8,128)S(1)} %get-tuple-element.171), channel_id=1, source_target_pairs={{0,8},{8,16},{16,24},{1,9},{9,17},{17,25},{2,10},{10,18},{18,26},{... | collective-permute-start | bytes 49160 | tf_op jit(solution)/shard_map/ppermute | solution.py:15
  53.3 3.1 %collective-permute-start.7 = (f32[1,1,32,128]{3,2,1,0:T(8,128)S(1)}, f32[1,1,32,128]{3,2,1,0:T(8,128)S(1)}, u32[]{:S(2)}, u32[]{:S(2)}) collective-permute-start(f32[1,1,32,128]{3,2,1,0:T(8,128)S(1)} %get-tuple-element.172), channel_id=1, source_target_pairs={{8,0},{16,8},{24,16},{9,1},{17,9},{25,17},{10,2},{18,10},{26,18},{... | collective-permute-start | bytes 49160 | tf_op jit(solution)/shard_map/ppermute | solution.py:17
  56.4 4.8 %collective-permute-start.8 = (f32[1,18,1,128]{3,2,1,0:T(1,128)S(1)}, f32[1,18,1,128]{3,2,1,0:T(1,128)S(1)}, u32[]{:S(2)}, u32[]{:S(2)}) collective-permute-start(f32[1,18,1,128]{3,2,1,0:T(1,128)S(1)} %get-tuple-element.167), channel_id=1, source_target_pairs={{0,2},{2,4},{4,6},{1,3},{3,5},{5,7},{8,10},{10,12},{12,14},{9,11},... | collective-permute-start | bytes 27656 | tf_op jit(solution)/shard_map/ppermute | solution.py:15
  59.8 5.6 %collective-permute-start.9 = (f32[1,18,1,128]{3,2,1,0:T(1,128)S(1)}, f32[1,18,1,128]{3,2,1,0:T(1,128)S(1)}, u32[]{:S(2)}, u32[]{:S(2)}) collective-permute-start(f32[1,18,1,128]{3,2,1,0:T(1,128)S(1)} %get-tuple-element.168), channel_id=1, source_target_pairs={{2,0},{4,2},{6,4},{3,1},{5,3},{7,5},{10,8},{12,10},{14,12},{11,9},... | collective-permute-start | bytes 27656 | tf_op jit(solution)/shard_map/ppermute | solution.py:17
  65.6 10.1 %collective-permute-start.10 = (f32[1,18,34,1]{3,2,1,0:T(8,128)S(1)}, f32[1,18,34,1]{3,2,1,0:T(8,128)S(1)}, u32[]{:S(2)}, u32[]{:S(2)}) collective-permute-start(f32[1,18,34,1]{3,2,1,0:T(8,128)S(1)} %get-tuple-element.163), channel_id=1, source_target_pairs={{0,1},{2,3},{4,5},{6,7},{8,9},{10,11},{12,13},{14,15},{16,17},{18,... | collective-permute-start | bytes 7352 | tf_op jit(solution)/shard_map/ppermute | solution.py:15
  67.1 12.8 %collective-permute-start.11 = (f32[1,18,34,1]{3,2,1,0:T(8,128)S(1)}, f32[1,18,34,1]{3,2,1,0:T(8,128)S(1)}, u32[]{:S(2)}, u32[]{:S(2)}) collective-permute-start(f32[1,18,34,1]{3,2,1,0:T(8,128)S(1)} %get-tuple-element.164), channel_id=1, source_target_pairs={{1,0},{3,2},{5,4},{7,6},{9,8},{11,10},{13,12},{15,14},{17,16},{19,... | collective-permute-start | bytes 7352 | tf_op jit(solution)/shard_map/ppermute | solution.py:17
  80.3 9.7 %copy-start.2 = (s32[16,32,128]{2,1,0:T(8,128)S(1)}, s32[16,32,128]{2,1,0:T(8,128)}, u32[]{:S(2)}) copy-start(s32[16,32,128]{2,1,0:T(8,128)} %param.34) | copy-start | bytes 786436
  80.3 9.7 %copy-start.3 = (f32[16,32,128]{2,1,0:T(8,128)S(1)}, f32[16,32,128]{2,1,0:T(8,128)}, u32[]{:S(2)}) copy-start(f32[16,32,128]{2,1,0:T(8,128)} %param.31) | copy-start | bytes 786436
  86.7 44.8 %copy-start.4 = (f32[16,32,128]{2,1,0:T(8,128)S(1)}, f32[16,32,128]{2,1,0:T(8,128)}, u32[]{:S(2)}) copy-start(f32[16,32,128]{2,1,0:T(8,128)} %param.32) | copy-start | bytes 786436
  131.7 68.0 %copy-start = (f32[16,32,128]{2,1,0:T(8,128)}, f32[16,32,128]{2,1,0:T(8,128)S(1)}, u32[]{:S(2)}) copy-start(f32[16,32,128]{2,1,0:T(8,128)S(1)} %add_multiply_fusion) | copy-start | bytes 786436
  131.7 2.6 %collective-permute-start.12 = (f32[2,1,32,128]{3,2,1,0:T(8,128)S(1)}, f32[2,1,32,128]{3,2,1,0:T(8,128)S(1)}, u32[]{:S(2)}, u32[]{:S(2)}) collective-permute-start(f32[2,1,32,128]{3,2,1,0:T(8,128)S(1)} %get-tuple-element.161), channel_id=1, source_target_pairs={{0,8},{8,16},{16,24},{1,9},{9,17},{17,25},{2,10},{10,18},{18,26},{... | collective-permute-start | bytes 98312 | tf_op jit(solution)/shard_map/ppermute | solution.py:15
  133.0 5.6 %collective-permute-start.13 = (f32[2,1,32,128]{3,2,1,0:T(8,128)S(1)}, f32[2,1,32,128]{3,2,1,0:T(8,128)S(1)}, u32[]{:S(2)}, u32[]{:S(2)}) collective-permute-start(f32[2,1,32,128]{3,2,1,0:T(8,128)S(1)} %get-tuple-element.162), channel_id=1, source_target_pairs={{8,0},{16,8},{24,16},{9,1},{17,9},{25,17},{10,2},{18,10},{26,18},{... | collective-permute-start | bytes 98312 | tf_op jit(solution)/shard_map/ppermute | solution.py:17
  138.6 3.8 %collective-permute-start.14 = (f32[2,18,1,128]{3,2,1,0:T(1,128)S(1)}, f32[2,18,1,128]{3,2,1,0:T(1,128)S(1)}, u32[]{:S(2)}, u32[]{:S(2)}) collective-permute-start(f32[2,18,1,128]{3,2,1,0:T(1,128)S(1)} %get-tuple-element.159), channel_id=1, source_target_pairs={{0,2},{2,4},{4,6},{1,3},{3,5},{5,7},{8,10},{10,12},{12,14},{9,11},... | collective-permute-start | bytes 55304 | tf_op jit(solution)/shard_map/ppermute | solution.py:15
  141.0 5.7 %collective-permute-start.15 = (f32[2,18,1,128]{3,2,1,0:T(1,128)S(1)}, f32[2,18,1,128]{3,2,1,0:T(1,128)S(1)}, u32[]{:S(2)}, u32[]{:S(2)}) collective-permute-start(f32[2,18,1,128]{3,2,1,0:T(1,128)S(1)} %get-tuple-element.160), channel_id=1, source_target_pairs={{2,0},{4,2},{6,4},{3,1},{5,3},{7,5},{10,8},{12,10},{14,12},{11,9},... | collective-permute-start | bytes 55304 | tf_op jit(solution)/shard_map/ppermute | solution.py:17
  147.3 3.8 %collective-permute-start.16 = (f32[2,18,34,1]{2,0,3,1:T(2,128)S(1)}, f32[2,18,34,1]{2,0,3,1:T(2,128)S(1)}, u32[]{:S(2)}, u32[]{:S(2)}) collective-permute-start(f32[2,18,34,1]{2,0,3,1:T(2,128)S(1)} %copy.21), channel_id=1, source_target_pairs={{0,1},{2,3},{4,5},{6,7},{8,9},{10,11},{12,13},{14,15},{16,17},{18,... | collective-permute-start | bytes 14696 | tf_op jit(solution)/shard_map/ppermute | solution.py:15
  149.8 5.8 %collective-permute-start.17 = (f32[2,18,34,1]{2,0,3,1:T(2,128)S(1)}, f32[2,18,34,1]{2,0,3,1:T(2,128)S(1)}, u32[]{:S(2)}, u32[]{:S(2)}) collective-permute-start(f32[2,18,34,1]{2,0,3,1:T(2,128)S(1)} %copy.22), channel_id=1, source_target_pairs={{1,0},{3,2},{5,4},{7,6},{9,8},{11,10},{13,12},{15,14},{17,16},{19,... | collective-permute-start | bytes 14696 | tf_op jit(solution)/shard_map/ppermute | solution.py:17
  156.9 42.8 %copy-start.5 = (f32[16,32,128]{2,1,0:T(8,128)S(1)}, f32[16,32,128]{2,1,0:T(8,128)}, u32[]{:S(2)}) copy-start(f32[16,32,128]{2,1,0:T(8,128)} %param.30) | copy-start | bytes 786436
where the time goes:
time: 201 us; the launch traced here: 200 us
  blocking collectives  78.7 us (39%)
  waiting for transfers between devices  48 us (24%)
  starting transfers between devices  33.7 us (17%)
  local copies, waits for them, and re-layouts  19.9 us (10%)
  other arithmetic  8.53 us (4%)
  matrix products  6.87 us (3%)
  between operations  4.56 us (2%)
    psum x1, blocking collectives, shards(): rz = lax.psum(jnp.sum(masked * precond), ('gx', 'gy', 'gz'))  39.6 us
    psum x1, blocking collectives, shards(): curve = lax.psum(jnp.sum(new_direction * image), ('gx', 'gy', 'gz'))  39.2 us
    ppermute x9, waiting for transfers between devices, extended(): lax.ppermute(head, axis, [((i + 1) % count, i) for i in range(ends)])  34.5 us
    ppermute x9, starting transfers between devices, extended(): lax.ppermute(tail, axis, [(i, (i + 1) % count) for i in range(ends)])  21.9 us
    ppermute x9, waiting for transfers between devices, extended(): lax.ppermute(tail, axis, [(i, (i + 1) % count) for i in range(ends)])  13.5 us
    ppermute x9, starting transfers between devices, extended(): lax.ppermute(head, axis, [((i + 1) % count, i) for i in range(ends)])  11.8 us
  transfers between devices with their start and end apart: 18, of which 13 were waited for; matrix products, arithmetic and copies ran while one was open for 1% of the time, Pallas kernels for 0%

commit v1 on v0

v1 whole, which is shorter than its diff:
```python
import functools

import jax
import jax.numpy as jnp
import ml_dtypes
import numpy as np
from jax import lax
from jax.experimental import pallas as pl
from jax.experimental.pallas import tpu as pltpu
from jax.sharding import PartitionSpec as P

AXES = ("gx", "gy", "gz")
F32 = jnp.float32
BF16 = jnp.bfloat16
HIGHEST = lax.Precision.HIGHEST
VMEM = pl.BlockSpec(memory_space=pltpu.VMEM)
SMEM = pl.BlockSpec(memory_space=pltpu.SMEM)
LANES = 256


def swaps(axis, turn):
    count = lax.axis_size(axis)
    return [(i, (i + 1 if (i + turn) % 2 == 0 else i - 1) % count) for i in range(count)]


def swap(block, axis, turn):
    return lax.ppermute(block, axis, swaps(axis, turn))


def place(axis):
    index = lax.axis_index(axis)
    return index % 2 == 0, index > 0, index < lax.axis_size(axis) - 1


def sides(turn0, turn1, where):
    even, below, above = where
    low = jnp.where(below, jnp.where(even, turn1, turn0), 0.0)
    high = jnp.where(above, jnp.where(even, turn0, turn1), 0.0)
    return low, high


def halves(value):
    high = value.astype(BF16)
    return high, (value - high.astype(F32)).astype(BF16)


def dot(a, b):
    return lax.dot_general(a, b, (((1,), (0,)), ((), ())), preferred_element_type=F32)


def iota(shape, dim):
    return lax.broadcasted_iota(jnp.int32, shape, dim)


def basis(n):
    idx = np.arange(n, dtype=np.float64) + 1.0
    values = 2.0 - 2.0 * np.cos(np.pi * idx / (n + 1))
    return np.sqrt(2.0 / (n + 1)) * np.sin(np.pi * idx[:, None] * idx[None, :] / (n + 1)), values


def np_halves(table):
    high = table.astype(np.float32).astype(ml_dtypes.bfloat16)
    return high, (table - high.astype(np.float64)).astype(np.float32).astype(ml_dtypes.bfloat16)


@functools.cache
def solve_tables(size_x, size_y, size_z):
    qx, lx = basis(size_x + 2)
    qy, ly = basis(size_y + 2)
    qz, lz = basis(size_z + 2)
    nx, ny, nz = size_x + 2, size_y + 2, size_z + 2
    own = [(i, j) for i in range(1, nx - 1) for j in range(1, ny - 1)]
    rim = [(i, j) for i in (0, nx - 1) for j in range(1, ny - 1)]
    rim += [(i, j) for j in (0, ny - 1) for i in range(1, nx - 1)]
    place_x, place_y = (np.array(v) for v in zip(*(own + rim)))
    modes = nx * ny
    padded = -(-modes // 16) * 16
    cross = np.zeros((padded, len(place_x)))
    cross[:modes] = (qx[:, None, place_x] * qy[None, :, place_y]).reshape(modes, -1)
    inverse = np.zeros((padded, LANES))
    inverse[:modes, :nz] = 1.0 / ((lx[:, None] + ly[None, :]).reshape(modes, 1) + lz[None, :])
    forward = np.zeros((size_z, LANES))
    forward[:, :nz] = qz[1:-1]
    ends = np.zeros((8, LANES))
    ends[0, :nz] = qz[0]
    ends[1, :nz] = qz[-1]
    fh, fl = np_halves(forward)
    ch, cl = np_halves(cross)
    return dict(
        fwd_hh=np.concatenate([fh, fh]),
        fwd_l=fl,
        ends=ends.astype(np.float32),
        cross_h=ch,
        cross_l=cl,
        inverse=inverse.astype(np.float32),
        back_h=np.ascontiguousarray(ch.T),
        back_l=np.ascontiguousarray(cl.T),
        out_hl=np.concatenate([np.ascontiguousarray(fh.T), np.ascontiguousarray(fl.T)], axis=1),
    )


def lane_rows(fields, lane):
    depth = fields[0].shape[1]
    total = None
    for f, field in enumerate(fields):
        pick = jnp.where((iota((8, depth), 0) == f) & (iota((8, depth), 1) == lane), 1.0, 0.0)
        rows = lax.dot_general(pick, field, (((1,), (1,)), ((), ())), precision=HIGHEST, preferred_element_type=F32)
        total = rows if total is None else total + rows
    return total


def lane_ends(row, even, depth):
    pick = jnp.where((iota((8, depth), 0) == 0) & (iota((8, depth), 1) == jnp.where(even, depth - 1, 0)), 1.0, 0.0)
    rows = jnp.broadcast_to(row, (8, row.shape[1]))
    return lax.dot_general(rows, pick, (((0,), (0,)), ((), ())), precision=HIGHEST, preferred_element_type=F32)


def pack_kernel(res, direction, mu, msk, sx0, sx1, sy0, sy1, sz):
    size_x, size_y, size_z = res.shape
    even_x, even_y, even_z = (place(axis)[0] for axis in AXES)
    mask = msk[...].astype(F32)
    fields = (mask * res[...], mask, mask * direction[...], mu[...])
    for f, field in enumerate(fields):
        low, high = field[0], field[size_x - 1]
        sx0[f] = jnp.where(even_x, high, low)
        sx1[f] = jnp.where(even_x, low, high)
        low, high = field[:, 0], field[:, size_y - 1]
        sy0[f] = jnp.where(even_y, high, low)
        sy1[f] = jnp.where(even_y, low, high)
    flat = [field.reshape(size_x * size_y, size_z) for field in fields]
    sz[...] = lane_rows(flat, jnp.where(even_z, size_z - 1, 0))


def solve_kernel(
    res, mu, msk, rx0, rx1, ry0, ry1, rz,
    fwd_hh, fwd_l, ends, cross_h, cross_l, inverse, back_h, back_l, out_hl,
    own, tx0, tx1, ty0, ty1, tz,
):
    size_x, size_y, size_z = res.shape
    rows = size_x * size_y
    where_x, where_y, where_z = (place(axis) for axis in AXES)
    even_z = where_z[0]
    mask = msk[...].astype(F32).reshape(rows, size_z)
    masked = mask * res[...].reshape(rows, size_z)
    x_low, x_high = sides(rx0[...], rx1[...], where_x)
    y_low, y_high = sides(ry0[...], ry1[...], where_y)
    box = jnp.concatenate([masked, x_low[0], x_high[0], y_low[0], y_high[0]], axis=0)
    box_h, box_l = halves(box)
    work = dot(jnp.concatenate([box_h, box_l], axis=1), fwd_hh[...]) + dot(box_h, fwd_l[...])
    face = jnp.broadcast_to(rz[0:1], (8, rows))
    face = jnp.where(iota((8, rows), 0) == jnp.where(even_z, 1, 0), face, 0.0)
    face = lax.dot_general(face, ends[...], (((0,), (0,)), ((), ())), precision=HIGHEST, preferred_element_type=F32)
    work = jnp.concatenate([work[:rows] + face, work[rows:]], axis=0)
    work_h, work_l = halves(work)
    work = dot(cross_h[...], work_h) + dot(cross_l[...], work_h) + dot(cross_h[...], work_l)
    coef = jnp.sum(mu[...]) * (1.0 / (rows * size_z))
    work = work * (inverse[...] / coef)
    work_h, work_l = halves(work)
    work = dot(back_h[...], work_h) + dot(back_l[...], work_h) + dot(back_h[...], work_l)
    work_h, work_l = halves(work)
    both = dot(work_h, out_hl[...])
    local = both[:, :size_z] + both[:, size_z:] + dot(work_l, out_hl[:, :size_z])
    face = lax.dot_general(ends[...], work[:rows], (((1,), (1,)), ((), ())), precision=HIGHEST, preferred_element_type=F32)

    def inner(shape, dim):
        at = iota(shape, dim)
        return (at >= 1) & (at <= shape[dim] - 2)

    own_flat = mask * local[:rows]
    own_box = own_flat.reshape(size_x, size_y, size_z)
    own[...] = own_box
    at = rows
    shape = (size_y, size_z)
    kept = inner(shape, 0) & inner(shape, 1)
    g_low = jnp.where(kept, local[at : at + size_y] * x_low[1], 0.0)
    g_high = jnp.where(kept, local[at + size_y : at + 2 * size_y] * x_high[1], 0.0)
    at += 2 * size_y
    even = where_x[0]
    low, high = own_box[0], own_box[size_x - 1]
    tx0[0] = jnp.where(even, high, low)
    tx0[1] = jnp.where(even, g_high, g_low)
    tx1[0] = jnp.where(even, low, high)
    tx1[1] = jnp.where(even, g_low, g_high)
    shape = (size_x, size_z)
    kept = inner(shape, 0) & inner(shape, 1)
    g_low = jnp.where(kept, local[at : at + size_x] * y_low[1], 0.0)
    g_high = jnp.where(kept, local[at + size_x : at + 2 * size_x] * y_high[1], 0.0)
    even = where_y[0]
    low, high = own_box[:, 0], own_box[:, size_y - 1]
    ty0[0] = jnp.where(even, high, low)
    ty0[1] = jnp.where(even, g_high, g_low)
    ty1[0] = jnp.where(even, low, high)
    ty1[1] = jnp.where(even, g_low, g_high)
    mine = lane_rows([own_flat], jnp.where(even_z, size_z - 1, 0))
    ids = iota((1, rows), 1)
    x_at, y_at = ids // size_y, ids % size_y
    kept = (x_at >= 1) & (x_at <= size_x - 2) & (y_at >= 1) & (y_at <= size_y - 2)
    ghost = jnp.where(kept, jnp.where(even_z, face[1:2], face[0:1]) * rz[1:2], 0.0)
    tz[...] = jnp.where(iota((8, rows), 0) == 1, jnp.broadcast_to(ghost, (8, rows)), mine)


def flux(value, x_sides, y_sides, face, mu, mu_x, mu_y, mu_face, even_z):
    size_x = y_sides[0].shape[0]
    rows, size_z = value.shape
    size_y = rows // size_x
    box = (size_x, size_y, size_z)
    value_b, mu_b = value.reshape(box), mu.reshape(box)
    ext = jnp.concatenate([x_sides[0][None], value_b, x_sides[1][None]], axis=0)
    mu_ext = jnp.concatenate([mu_x[0][None], mu_b, mu_x[1][None]], axis=0)
    flow = 0.5 * (mu_ext[1:] + mu_ext[:-1]) * (ext[1:] - ext[:-1])
    total = (flow[:-1] - flow[1:]).reshape(rows, size_z)

    def wide(side):
        return jnp.broadcast_to(side[:, None, :], box).reshape(rows, size_z)

    at = iota((rows, size_z), 0) % size_y
    next_v = jnp.where(at == size_y - 1, wide(y_sides[1]), pltpu.roll(value, rows - 1, 0))
    next_m = jnp.where(at == size_y - 1, wide(mu_y[1]), pltpu.roll(mu, rows - 1, 0))
    flow = 0.5 * (mu + next_m) * (next_v - value)
    first = 0.5 * (mu + wide(mu_y[0])) * (value - wide(y_sides[0]))
    total = total + jnp.where(at == 0, first, pltpu.roll(flow, 1, 0)) - flow
    at = iota((rows, size_z), 1)
    next_v = jnp.where(at == size_z - 1, face, pltpu.roll(value, size_z - 1, 1))
    next_m = jnp.where(at == size_z - 1, mu_face, pltpu.roll(mu, size_z - 1, 1))
    flow = 0.5 * (mu + next_m) * (next_v - value)
    first = 0.5 * (mu + mu_face) * (value - face)
    return total + jnp.where(at == 0, first, pltpu.roll(flow, 1, 1)) - flow


def image_kernel(
    res, direction, mu, msk, own, rx0, rx1, ry0, ry1, rz, tx0, tx1, ty0, ty1, tz, qx0, qx1, qy0, qy1, qz,
    z_out, az_out, ad_out, sums,
):
    size_x, size_y, size_z = res.shape
    rows = size_x * size_y
    box = (size_x, size_y, size_z)
    where_x, where_y, where_z = (place(axis) for axis in AXES)
    even_z = where_z[0]
    x_near = sides(rx0[...], rx1[...], where_x)
    y_near = sides(ry0[...], ry1[...], where_y)
    x_sent = sides(tx0[...], tx1[...], where_x)
    y_sent = sides(ty0[...], ty1[...], where_y)
    x_got = sides(qx0[...], qx1[...], where_x)
    y_got = sides(qy0[...], qy1[...], where_y)
    mask = msk[...].astype(F32).reshape(rows, size_z)
    mu_own = mu[...].reshape(rows, size_z)
    mu_x, mu_y = [v[3] for v in x_near], [v[3] for v in y_near]
    mu_face = lane_ends(rz[3:4], even_z, size_z)
    d = mask * direction[...].reshape(rows, size_z)
    d_face = lane_ends(rz[2:3], even_z, size_z)
    ad = mask * flux(d, [v[2] for v in x_near], [v[2] for v in y_near], d_face, mu_own, mu_x, mu_y, mu_face, even_z)
    own_box = own[...]
    z = jnp.concatenate(
        [own_box[:1] + x_got[0][1][None], own_box[1:-1], own_box[-1:] + x_got[1][1][None]], axis=0
    )
    at = iota(box, 1)
    z = z + jnp.where(at == 0, y_got[0][1][:, None, :], 0.0) + jnp.where(at == size_y - 1, y_got[1][1][:, None, :], 0.0)
    z = z.reshape(rows, size_z) + lane_ends(qz[1:2], even_z, size_z)
    z_face = lane_ends(qz[0:1] + tz[1:2], even_z, size_z)
    az = mask * flux(
        z,
        [x_got[s][0] + x_sent[s][1] for s in (0, 1)],
        [y_got[s][0] + y_sent[s][1] for s in (0, 1)],
        z_face, mu_own, mu_x, mu_y, mu_face, even_z,
    )
    z_out[...] = z.reshape(box)
    az_out[...] = az.reshape(box)
    ad_out[...] = ad.reshape(box)
    parts = (
        jnp.sum(res[...].reshape(rows, size_z) * z),
        jnp.sum(z * az),
        jnp.sum(z * ad + d * az),
        jnp.sum(d * ad),
    )
    at = iota(sums.shape, 2)
    line = jnp.zeros(sums.shape, F32)
    for k, part in enumerate(parts):
        line = jnp.where(at == k, part, line)
    sums[...] = line


def update_kernel(rz_prev, sums, iterate, res, direction, msk, z, az, ad, new_iterate, new_res, new_direction):
    line = jnp.sum(sums[...], axis=0)
    rz, zaz, zad, dad = (line[:, k : k + 1] for k in range(4))
    beta = rz / rz_prev[0]
    alpha = rz / (zaz + beta * (zad + beta * dad))
    alpha, beta = (v.reshape(1, 1, 1) for v in (alpha, beta))
    p = z[...] + beta * (msk[...].astype(F32) * direction[...])
    new_direction[...] = p
    new_iterate[...] = iterate[...] + alpha * p
    new_res[...] = res[...] - alpha * (az[...] + beta * ad[...])


def call(kernel, args, outs, specs=None):
    return pl.pallas_call(
        kernel,
        out_shape=[jax.ShapeDtypeStruct(shape, F32) for shape in outs],
        in_specs=specs or [VMEM] * len(args),
        out_specs=[VMEM] * len(outs),
        compiler_params=pltpu.CompilerParams(vmem_limit_bytes=48 * 1024 * 1024),
    )(*args)


def exchange(sx0, sx1, sy0, sy1, sz):
    return (
        swap(sx0, "gx", 0),
        swap(sx1, "gx", 1),
        swap(sy0, "gy", 0),
        swap(sy1, "gy", 1),
        swap(sz, "gz", 0),
    )


def shards(iterate, residual, direction, permeability, unfixed_node_mask, rz_prev):
    size_x, size_y, size_z = residual.shape
    box = residual.shape
    rows = size_x * size_y
    devices = lax.axis_size(AXES)

    def faces(count):
        return [(count, size_y, size_z)] * 2 + [(count, size_x, size_z)] * 2 + [(8, rows)]

    table = solve_tables(size_x, size_y, size_z)
    with jax.named_scope("pack"):
        sent = call(pack_kernel, (residual, direction, permeability, unfixed_node_mask), faces(4))
    with jax.named_scope("faces_in"):
        near = exchange(*sent)
    with jax.named_scope("solve"):
        own, *made = call(
            solve_kernel,
            (residual, permeability, unfixed_node_mask, *near, *map(jnp.asarray, table.values())),
            [box] + faces(2),
        )
    with jax.named_scope("faces_out"):
        got = exchange(*made)
    with jax.named_scope("image"):
        z, az, ad, sums = call(
            image_kernel,
            (residual, direction, permeability, unfixed_node_mask, own, *near, *made, *got),
            [box, box, box, (devices, 1, 128)],
        )
    with jax.named_scope("sums"):
        sums = lax.all_to_all(sums, AXES, 0, 0, tiled=True)
    with jax.named_scope("update"):
        args = (rz_prev, sums, iterate, residual, direction, unfixed_node_mask, z, az, ad)
        return tuple(call(update_kernel, args, [box] * 3, [SMEM] + [VMEM] * 8))


def solution(mesh):
    in_specs = (P(*AXES),) * 5 + (P(),)
    out_specs = (P(*AXES),) * 3
    return jax.shard_map(shards, mesh=mesh, in_specs=in_specs, out_specs=out_specs, check_vma=False)
```

time: 201 us -> 50.6 us (0.25)
  blocking collectives: 78.7 us -> 0 us
  waiting for transfers between devices: 48 us -> 11.4 us
  starting transfers between devices: 33.7 us -> 17 us
  Pallas kernels: 0 us -> 9.33 us
  local copies, waits for them, and re-layouts: 19.9 us -> 11 us
  other arithmetic: 8.53 us -> 0 us
  matrix products: 6.87 us -> 0 us
  between operations: 4.56 us -> 1.39 us
    psum x2 -> x0, blocking collectives: 78.7 us -> none  [the longest x1 39.6 us: shards(): rz = lax.psum(jnp.sum(masked * precond), ('gx', 'gy', 'gz'))]
    ppermute x18 -> x10, waiting for transfers between devices: 48 us -> 4.98 us  [swap(): return lax.ppermute(block, axis, swaps(axis, turn))]
    ppermute x18 -> x10, starting transfers between devices: 33.7 us -> 12.8 us  [swap(): return lax.ppermute(block, axis, swaps(axis, turn))]
    unnamed x12 -> x34, local copies, waits for them, and re-layouts: 0.04 us -> 11 us
    pallas_call x0 -> x4, Pallas kernels: none -> 9.33 us  [call(): pl.pallas_call(kernel, out_shape=[jax.ShapeDtypeStruct(shape, F32) for sh...]
    scatter-add x6 -> x0, local copies, waits for them, and re-layouts: 8.99 us -> none  [the longest x1 2.53 us: collect(): owned = owned.at[1:-1, 1:-1, -1].add(received_planes[2:-2, 2:-2, -1])]
    scatter x5 -> x0, local copies, waits for them, and re-layouts: 8.24 us -> none  [the longest x1 2.53 us: build_halo_message(): halo_message.at[1:-1, 1:-1, -1].set(subdomain_parts[2:-2, 2:-2, -1])]
    dot_general x6 -> x0, matrix products: 6.87 us -> none  [the longest x1 1.31 us: fdm_solve(): return jnp.einsum('kc,ijc->ijk', sz, work, precision=high)]
  transfers between devices with their start and end apart: 18 -> 11, of which waited for: 13 -> 4; matrix products, arithmetic and copies ran while one was open for 1% -> 0% of each run, Pallas kernels for 0% -> 0%
where the time goes in v1:
time: 50.6 us; the launch traced here: 50.1 us
  starting transfers between devices  17 us (34%)
  waiting for transfers between devices  11.4 us (23%)
  local copies, waits for them, and re-layouts  11 us (22%)
  Pallas kernels  9.33 us (18%)
  between operations  1.39 us (3%)
    ppermute x10, starting transfers between devices, swap(): return lax.ppermute(block, axis, swaps(axis, turn))  12.8 us
    unnamed x34, local copies, waits for them, and re-layouts  11 us
    pallas_call x4, Pallas kernels, call(): pl.pallas_call(kernel, out_shape=[jax.ShapeDtypeStruct(shape, F32) for sh...  9.33 us
    all_to_all x1, waiting for transfers between devices, shards(): sums = lax.all_to_all(sums, AXES, 0, 0, tiled=True)  6.39 us
    ppermute x10, waiting for transfers between devices, swap(): return lax.ppermute(block, axis, swaps(axis, turn))  4.98 us
    all_to_all x1, starting transfers between devices, shards(): sums = lax.all_to_all(sums, AXES, 0, 0, tiled=True)  4.26 us
  transfers between devices with their start and end apart: 11, of which 4 were waited for; matrix products, arithmetic and copies ran while one was open for 0% of the time, Pallas kernels for 0%

profile of v1, /device:TPU:0, one launch (start us, length us, event | category | flops | bytes accessed | tf_op | source)
XLA Modules:
  0.0 50.1 jit_solution(16627520871893405004)
XLA Ops:
  0.6 0.9 %copy-done = f32[16,32,128]{2,1,0:T(8,128)S(1)} copy-done((f32[16,32,128]{2,1,0:T(8,128)S(1)}, f32[16,32,128]{2,1,0:T(8,128)}, u32[]{:S(2)}) %copy-start) | copy-done | bytes 262168
  1.6 0.9 %copy-done.2 = s32[16,32,128]{2,1,0:T(8,128)S(1)} copy-done((s32[16,32,128]{2,1,0:T(8,128)S(1)}, s32[16,32,128]{2,1,0:T(8,128)}, u32[]{:S(2)}) %copy-start.2) | copy-done | bytes 262168
  2.5 0.9 %copy-done.4 = f32[16,32,128]{2,1,0:T(8,128)S(1)} copy-done((f32[16,32,128]{2,1,0:T(8,128)S(1)}, f32[16,32,128]{2,1,0:T(8,128)}, u32[]{:S(2)}) %copy-start.4) | copy-done | bytes 262168
  3.5 0.9 %copy-done.5 = f32[16,32,128]{2,1,0:T(8,128)S(1)} copy-done((f32[16,32,128]{2,1,0:T(8,128)S(1)}, f32[16,32,128]{2,1,0:T(8,128)}, u32[]{:S(2)}) %copy-start.5) | copy-done | bytes 262168
  4.4 0.9 %pack.1 = (f32[4,32,128]{2,1,0:T(8,128)S(1)}, f32[4,32,128]{2,1,0:T(8,128)S(1)}, f32[4,16,128]{2,1,0:T(8,128)S(1)}, f32[4,16,128]{2,1,0:T(8,128)S(1)}, f32[8,512]{1,0:T(8,128)S(1)}) custom-call(f32[16,32,128]{2,1,0:T(8,128)S(1)} %copy-done, f32[16,32,128]{2,1,0:T(8,128)S(1)} %copy-done.5, f32[16,32,128]{2,1,0:T(8,128)S(1)} %copy-done.4, ...), custom_call_target="tpu_custom_call" | custom-call | tf_op jit(solution)/shard_map/pack/pallas_call | solution.py:295
  5.4 0.5 collective-permute-start
  5.9 2.6 %collective-permute-start.1 = (f32[4,32,128]{2,1,0:T(8,128)S(1)}, f32[4,32,128]{2,1,0:T(8,128)S(1)}, u32[]{:S(2)}, u32[]{:S(2)}) collective-permute-start(f32[4,32,128]{2,1,0:T(8,128)S(1)} %get-tuple-element.19), channel_id=1, source_target_pairs={{0,24},{8,16},{16,8},{24,0},{1,25},{9,17},{17,9},{25,1},{2,26},{10... | collective-permute-start | bytes 196616 | tf_op jit(solution)/shard_map/faces_in/ppermute | solution.py:27
  8.5 1.6 %collective-permute-start.2 = (f32[4,16,128]{2,1,0:T(8,128)S(1)}, f32[4,16,128]{2,1,0:T(8,128)S(1)}, u32[]{:S(2)}, u32[]{:S(2)}) collective-permute-start(f32[4,16,128]{2,1,0:T(8,128)S(1)} %get-tuple-element.20), channel_id=1, source_target_pairs={{0,2},{2,0},{4,6},{6,4},{1,3},{3,1},{5,7},{7,5},{8,10},{10,8},{12,... | collective-permute-start | bytes 98312 | tf_op jit(solution)/shard_map/faces_in/ppermute | solution.py:27
  10.0 2.5 %collective-permute-start.3 = (f32[4,16,128]{2,1,0:T(8,128)S(1)}, f32[4,16,128]{2,1,0:T(8,128)S(1)}, u32[]{:S(2)}, u32[]{:S(2)}) collective-permute-start(f32[4,16,128]{2,1,0:T(8,128)S(1)} %get-tuple-element.21), channel_id=1, source_target_pairs={{0,6},{2,4},{4,2},{6,0},{1,7},{3,5},{5,3},{7,1},{8,14},{10,12},{12... | collective-permute-start | bytes 98312 | tf_op jit(solution)/shard_map/faces_in/ppermute | solution.py:27
  12.5 1.5 %collective-permute-start.4 = (f32[8,512]{1,0:T(8,128)S(1)}, f32[8,512]{1,0:T(8,128)S(1)}, u32[]{:S(2)}, u32[]{:S(2)}) collective-permute-start(f32[8,512]{1,0:T(8,128)S(1)} %get-tuple-element.22), channel_id=1, source_target_pairs={{0,1},{1,0},{2,3},{3,2},{4,5},{5,4},{6,7},{7,6},{8,9},{9,8},{10,11... | collective-permute-start | bytes 49160 | tf_op jit(solution)/shard_map/faces_in/ppermute | solution.py:27
  14.0 2.2 %collective-permute-done.4.rz = f32[8,512]{1,0:T(8,128)S(1)} collective-permute-done((f32[8,512]{1,0:T(8,128)S(1)}, f32[8,512]{1,0:T(8,128)S(1)}, u32[]{:S(2)}, u32[]{:S(2)}) %collective-permute-start.4) | collective-permute-done | bytes 16416 | tf_op jit(solution)/shard_map/faces_in/ppermute | solution.py:27
  16.3 0.0 copy-start.7
  16.3 1.1 %copy-done.7 = bf16[624,608]{1,0:T(8,128)(2,1)S(1)} copy-done((bf16[624,608]{1,0:T(8,128)(2,1)S(1)}, bf16[624,608]{1,0:T(8,128)(2,1)}, u32[]{:S(2)}) %copy-start.7) | copy-done | bytes 758808
  17.4 1.1 %copy-done.8 = bf16[624,608]{1,0:T(8,128)(2,1)S(1)} copy-done((bf16[624,608]{1,0:T(8,128)(2,1)S(1)}, bf16[624,608]{1,0:T(8,128)(2,1)}, u32[]{:S(2)}) %copy-start.8) | copy-done | bytes 758808
  18.6 1.1 %copy-done.10 = bf16[608,624]{1,0:T(8,128)(2,1)S(1)} copy-done((bf16[608,624]{1,0:T(8,128)(2,1)S(1)}, bf16[608,624]{1,0:T(8,128)(2,1)}, u32[]{:S(2)}) %copy-start.10) | copy-done | bytes 758808
  19.7 1.1 %copy-done.11 = f32[624,256]{1,0:T(8,128)S(1)} copy-done((f32[624,256]{1,0:T(8,128)S(1)}, f32[624,256]{1,0:T(8,128)}, u32[]{:S(2)}) %copy-start.11) | copy-done | bytes 639000
  20.8 0.9 %copy-done.13 = bf16[256,256]{1,0:T(8,128)(2,1)S(1)} copy-done((bf16[256,256]{1,0:T(8,128)(2,1)S(1)}, bf16[256,256]{1,0:T(8,128)(2,1)}, u32[]{:S(2)}) %copy-start.13) | copy-done | bytes 131096
  21.7 0.9 %copy-done.14 = bf16[256,256]{1,0:T(8,128)(2,1)S(1)} copy-done((bf16[256,256]{1,0:T(8,128)(2,1)S(1)}, bf16[256,256]{1,0:T(8,128)(2,1)}, u32[]{:S(2)}) %copy-start.14) | copy-done | bytes 131096
  22.6 0.8 %copy-done.15 = bf16[128,256]{1,0:T(8,128)(2,1)S(1)} copy-done((bf16[128,256]{1,0:T(8,128)(2,1)S(1)}, bf16[128,256]{1,0:T(8,128)(2,1)}, u32[]{:S(2)}) %copy-start.15) | copy-done | bytes 65560
  23.4 4.8 %solve.1 = (f32[16,32,128]{2,1,0:T(8,128)S(1)}, f32[2,32,128]{2,1,0:T(8,128)S(1)}, f32[2,32,128]{2,1,0:T(8,128)S(1)}, f32[2,16,128]{2,1,0:T(8,128)S(1)}, f32[2,1...) custom-call(f32[16,32,128]{2,1,0:T(8,128)S(1)} %copy-done, f32[16,32,128]{2,1,0:T(8,128)S(1)} %copy-done.4, ...), custom_call_target="tpu_custom_call" | custom-call | tf_op jit(solution)/shard_map/solve/pallas_call | solution.py:295
  28.3 0.7 %collective-permute-start.6 = (f32[2,32,128]{2,1,0:T(8,128)S(1)}, f32[2,32,128]{2,1,0:T(8,128)S(1)}, u32[]{:S(2)}, u32[]{:S(2)}) collective-permute-start(f32[2,32,128]{2,1,0:T(8,128)S(1)} %get-tuple-element.25.tx1), channel_id=1, source_target_pairs={{0,24},{8,16},{16,8},{24,0},{1,25},{9,17},{17,9},{25,1},{2,26},{10... | collective-permute-start | bytes 98312 | tf_op jit(solution)/shard_map/faces_out/ppermute | solution.py:27
  28.9 0.7 %collective-permute-start.7 = (f32[2,16,128]{2,1,0:T(8,128)S(1)}, f32[2,16,128]{2,1,0:T(8,128)S(1)}, u32[]{:S(2)}, u32[]{:S(2)}) collective-permute-start(f32[2,16,128]{2,1,0:T(8,128)S(1)} %get-tuple-element.26.ty0), channel_id=1, source_target_pairs={{0,2},{2,0},{4,6},{6,4},{1,3},{3,1},{5,7},{7,5},{8,10},{10,8},{12,... | collective-permute-start | bytes 49160 | tf_op jit(solution)/shard_map/faces_out/ppermute | solution.py:27
  29.6 1.3 %collective-permute-start.8 = (f32[2,16,128]{2,1,0:T(8,128)S(1)}, f32[2,16,128]{2,1,0:T(8,128)S(1)}, u32[]{:S(2)}, u32[]{:S(2)}) collective-permute-start(f32[2,16,128]{2,1,0:T(8,128)S(1)} %get-tuple-element.27.ty1), channel_id=1, source_target_pairs={{0,6},{2,4},{4,2},{6,0},{1,7},{3,5},{5,3},{7,1},{8,14},{10,12},{12... | collective-permute-start | bytes 49160 | tf_op jit(solution)/shard_map/faces_out/ppermute | solution.py:27
  30.9 1.5 %collective-permute-start.9 = (f32[8,512]{1,0:T(8,128)S(1)}, f32[8,512]{1,0:T(8,128)S(1)}, u32[]{:S(2)}, u32[]{:S(2)}) collective-permute-start(f32[8,512]{1,0:T(8,128)S(1)} %get-tuple-element.28.tz), channel_id=1, source_target_pairs={{0,1},{1,0},{2,3},{3,2},{4,5},{5,4},{6,7},{7,6},{8,9},{9,8},{10,11... | collective-permute-start | bytes 49160 | tf_op jit(solution)/shard_map/faces_out/ppermute | solution.py:27
  32.4 0.3 collective-permute-done.7.qy0
  32.7 2.5 %collective-permute-done.8.qy1 = f32[2,16,128]{2,1,0:T(8,128)S(1)} collective-permute-done((f32[2,16,128]{2,1,0:T(8,128)S(1)}, f32[2,16,128]{2,1,0:T(8,128)S(1)}, u32[]{:S(2)}, u32[]{:S(2)}) %collective-permute-start.8) | collective-permute-done | bytes 16416 | tf_op jit(solution)/shard_map/faces_out/ppermute | solution.py:27
  35.2 0.0 copy-start.6
  35.2 0.0 copy-start.12
  35.2 2.2 %image.1 = (f32[16,32,128]{2,1,0:T(8,128)S(1)}, f32[16,32,128]{2,1,0:T(8,128)S(1)}, f32[16,32,128]{2,1,0:T(8,128)S(1)}, f32[32,1,128]{2,1,0:T(1,128)}) custom-call(f32[16,32,128]{2,1,0:T(8,128)S(1)} %copy-done, f32[16,32,128]{2,1,0:T(8,128)S(1)} %copy-done.5, f32[16,32,128]{2,1,0:T(8,128)S(1)} %copy-done.4, s32[16,32,128]{2,1,0:T(8,128)S(1)} %copy-done.3, ...), custom_call_target="tpu_custom_call" | custom-call | tf_op jit(solution)/shard_map/image/pallas_call | solution.py:295
  37.4 4.3 %all-to-all-start = ((f32[32,1,128]{2,1,0:T(1,128)}), f32[32,1,128]{2,1,0:T(1,128)S(1)}, u32[]{:S(2)}, u32[]{:S(2)}) async-start(f32[32,1,128]{2,1,0:T(1,128)} %get-tuple-element.29), calls=%async_computation | async-start | bytes 32768 | tf_op jit(solution)/shard_map/sums/all_to_all | solution.py:343
  42.4 6.4 %all-to-all-done.sums = f32[32,1,128]{2,1,0:T(1,128)S(1)} async-done(((f32[32,1,128]{2,1,0:T(1,128)}), f32[32,1,128]{2,1,0:T(1,128)S(1)}, u32[]{:S(2)}, u32[]{:S(2)}) %all-to-all-start) | async-done | bytes 16416 | tf_op jit(solution)/shard_map/sums/all_to_all | solution.py:343
  48.8 1.3 %update.1 = (f32[16,32,128]{2,1,0:T(8,128)}, f32[16,32,128]{2,1,0:T(8,128)}, f32[16,32,128]{2,1,0:T(8,128)}) custom-call(f32[1]{0:T(128)S(6)} %copy.18.rz_prev, f32[32,1,128]{2,1,0:T(1,128)S(1)} %all-to-all-done.sums, f32[16,32,128]{2,1,0:T(8,128)S(1)} %copy-done.12, f32[16,32,128]{2,1,0:T(8,128)S(1)} %copy-done.1, f32[16,32,128]{2,1,0:T(8,128)S(1)} %copy-done.6, ...), custom_call_target="tpu_custom_call" | custom-call | tf_op jit(solution)/shard_map/update/pallas_call | solution.py:295
  (28 shorter events, 0.1 us)
Async XLA Ops:
  0.6 1.0 %copy-start = (f32[16,32,128]{2,1,0:T(8,128)S(1)}, f32[16,32,128]{2,1,0:T(8,128)}, u32[]{:S(2)}) copy-start(f32[16,32,128]{2,1,0:T(8,128)} %res.7) | copy-start | bytes 786436
  1.6 0.9 %copy-start.2 = (s32[16,32,128]{2,1,0:T(8,128)S(1)}, s32[16,32,128]{2,1,0:T(8,128)}, u32[]{:S(2)}) copy-start(s32[16,32,128]{2,1,0:T(8,128)} %msk.7) | copy-start | bytes 786436
  2.5 0.9 %copy-start.4 = (f32[16,32,128]{2,1,0:T(8,128)S(1)}, f32[16,32,128]{2,1,0:T(8,128)}, u32[]{:S(2)}) copy-start(f32[16,32,128]{2,1,0:T(8,128)} %mu.5) | copy-start | bytes 786436
  3.5 0.9 %copy-start.5 = (f32[16,32,128]{2,1,0:T(8,128)S(1)}, f32[16,32,128]{2,1,0:T(8,128)}, u32[]{:S(2)}) copy-start(f32[16,32,128]{2,1,0:T(8,128)} %direction.5) | copy-start | bytes 786436
  4.4 11.8 %copy-start.3 = (s32[16,32,128]{2,1,0:T(8,128)S(1)}, s32[16,32,128]{2,1,0:T(8,128)}, u32[]{:S(2)}) copy-start(s32[16,32,128]{2,1,0:T(8,128)} %msk.7) | copy-start | bytes 786436
  4.4 11.8 %copy-start.9 = (bf16[608,624]{1,0:T(8,128)(2,1)S(1)}, bf16[608,624]{1,0:T(8,128)(2,1)}, u32[]{:S(2)}) copy-start(bf16[608,624]{1,0:T(8,128)(2,1)} %constant.25.clone.back_l) | copy-start | bytes 2276356
  5.4 10.9 %copy-start.16 = (f32[8,256]{1,0:T(8,128)S(1)}, f32[8,256]{1,0:T(8,128)}, u32[]{:S(2)}) copy-start(f32[8,256]{1,0:T(8,128)} %constant.20.clone.ends) | copy-start | bytes 24580
  5.4 10.9 %collective-permute-start = (f32[4,32,128]{2,1,0:T(8,128)S(1)}, f32[4,32,128]{2,1,0:T(8,128)S(1)}, u32[]{:S(2)}, u32[]{:S(2)}) collective-permute-start(f32[4,32,128]{2,1,0:T(8,128)S(1)} %get-tuple-element.18), channel_id=1, source_target_pairs={{0,8},{8,0},{16,24},{24,16},{1,9},{9,1},{17,25},{25,17},{2,10},{10... | collective-permute-start | bytes 196616 | tf_op jit(solution)/shard_map/faces_in/ppermute | solution.py:27
  5.9 10.4 %collective-permute-start.1 = (f32[4,32,128]{2,1,0:T(8,128)S(1)}, f32[4,32,128]{2,1,0:T(8,128)S(1)}, u32[]{:S(2)}, u32[]{:S(2)}) collective-permute-start(f32[4,32,128]{2,1,0:T(8,128)S(1)} %get-tuple-element.19), channel_id=1, source_target_pairs={{0,24},{8,16},{16,8},{24,0},{1,25},{9,17},{17,9},{25,1},{2,26},{10... | collective-permute-start | bytes 196616 | tf_op jit(solution)/shard_map/faces_in/ppermute | solution.py:27
  8.5 7.8 %collective-permute-start.2 = (f32[4,16,128]{2,1,0:T(8,128)S(1)}, f32[4,16,128]{2,1,0:T(8,128)S(1)}, u32[]{:S(2)}, u32[]{:S(2)}) collective-permute-start(f32[4,16,128]{2,1,0:T(8,128)S(1)} %get-tuple-element.20), channel_id=1, source_target_pairs={{0,2},{2,0},{4,6},{6,4},{1,3},{3,1},{5,7},{7,5},{8,10},{10,8},{12,... | collective-permute-start | bytes 98312 | tf_op jit(solution)/shard_map/faces_in/ppermute | solution.py:27
  10.0 6.2 %collective-permute-start.3 = (f32[4,16,128]{2,1,0:T(8,128)S(1)}, f32[4,16,128]{2,1,0:T(8,128)S(1)}, u32[]{:S(2)}, u32[]{:S(2)}) collective-permute-start(f32[4,16,128]{2,1,0:T(8,128)S(1)} %get-tuple-element.21), channel_id=1, source_target_pairs={{0,6},{2,4},{4,2},{6,0},{1,7},{3,5},{5,3},{7,1},{8,14},{10,12},{12... | collective-permute-start | bytes 98312 | tf_op jit(solution)/shard_map/faces_in/ppermute | solution.py:27
  12.5 3.7 %collective-permute-start.4 = (f32[8,512]{1,0:T(8,128)S(1)}, f32[8,512]{1,0:T(8,128)S(1)}, u32[]{:S(2)}, u32[]{:S(2)}) collective-permute-start(f32[8,512]{1,0:T(8,128)S(1)} %get-tuple-element.22), channel_id=1, source_target_pairs={{0,1},{1,0},{2,3},{3,2},{4,5},{5,4},{6,7},{7,6},{8,9},{9,8},{10,11... | collective-permute-start | bytes 49160 | tf_op jit(solution)/shard_map/faces_in/ppermute | solution.py:27
  16.3 1.1 %copy-start.7 = (bf16[624,608]{1,0:T(8,128)(2,1)S(1)}, bf16[624,608]{1,0:T(8,128)(2,1)}, u32[]{:S(2)}) copy-start(bf16[624,608]{1,0:T(8,128)(2,1)} %constant.22.clone.cross_l) | copy-start | bytes 2276356
  17.4 1.1 %copy-start.8 = (bf16[624,608]{1,0:T(8,128)(2,1)S(1)}, bf16[624,608]{1,0:T(8,128)(2,1)}, u32[]{:S(2)}) copy-start(bf16[624,608]{1,0:T(8,128)(2,1)} %constant.21.clone.cross_h) | copy-start | bytes 2276356
  18.6 1.1 %copy-start.10 = (bf16[608,624]{1,0:T(8,128)(2,1)S(1)}, bf16[608,624]{1,0:T(8,128)(2,1)}, u32[]{:S(2)}) copy-start(bf16[608,624]{1,0:T(8,128)(2,1)} %constant.24.clone.back_h) | copy-start | bytes 2276356
  19.7 1.1 %copy-start.11 = (f32[624,256]{1,0:T(8,128)S(1)}, f32[624,256]{1,0:T(8,128)}, u32[]{:S(2)}) copy-start(f32[624,256]{1,0:T(8,128)} %constant.23.clone.inverse) | copy-start | bytes 1916932
  20.8 0.9 %copy-start.13 = (bf16[256,256]{1,0:T(8,128)(2,1)S(1)}, bf16[256,256]{1,0:T(8,128)(2,1)}, u32[]{:S(2)}) copy-start(bf16[256,256]{1,0:T(8,128)(2,1)} %constant.26.clone.out_hl) | copy-start | bytes 393220
  21.7 0.9 %copy-start.14 = (bf16[256,256]{1,0:T(8,128)(2,1)S(1)}, bf16[256,256]{1,0:T(8,128)(2,1)}, u32[]{:S(2)}) copy-start(bf16[256,256]{1,0:T(8,128)(2,1)} %constant.18.clone.fwd_hh) | copy-start | bytes 393220
  22.6 0.8 %copy-start.15 = (bf16[128,256]{1,0:T(8,128)(2,1)S(1)}, bf16[128,256]{1,0:T(8,128)(2,1)}, u32[]{:S(2)}) copy-start(bf16[128,256]{1,0:T(8,128)(2,1)} %constant.19.clone.fwd_l) | copy-start | bytes 196612
  28.3 6.9 %collective-permute-start.5 = (f32[2,32,128]{2,1,0:T(8,128)S(1)}, f32[2,32,128]{2,1,0:T(8,128)S(1)}, u32[]{:S(2)}, u32[]{:S(2)}) collective-permute-start(f32[2,32,128]{2,1,0:T(8,128)S(1)} %get-tuple-element.24.tx0), channel_id=1, source_target_pairs={{0,8},{8,0},{16,24},{24,16},{1,9},{9,1},{17,25},{25,17},{2,10},{10... | collective-permute-start | bytes 98312 | tf_op jit(solution)/shard_map/faces_out/ppermute | solution.py:27
  28.3 6.9 %collective-permute-start.6 = (f32[2,32,128]{2,1,0:T(8,128)S(1)}, f32[2,32,128]{2,1,0:T(8,128)S(1)}, u32[]{:S(2)}, u32[]{:S(2)}) collective-permute-start(f32[2,32,128]{2,1,0:T(8,128)S(1)} %get-tuple-element.25.tx1), channel_id=1, source_target_pairs={{0,24},{8,16},{16,8},{24,0},{1,25},{9,17},{17,9},{25,1},{2,26},{10... | collective-permute-start | bytes 98312 | tf_op jit(solution)/shard_map/faces_out/ppermute | solution.py:27
  28.9 3.7 %collective-permute-start.7 = (f32[2,16,128]{2,1,0:T(8,128)S(1)}, f32[2,16,128]{2,1,0:T(8,128)S(1)}, u32[]{:S(2)}, u32[]{:S(2)}) collective-permute-start(f32[2,16,128]{2,1,0:T(8,128)S(1)} %get-tuple-element.26.ty0), channel_id=1, source_target_pairs={{0,2},{2,0},{4,6},{6,4},{1,3},{3,1},{5,7},{7,5},{8,10},{10,8},{12,... | collective-permute-start | bytes 49160 | tf_op jit(solution)/shard_map/faces_out/ppermute | solution.py:27
  29.6 5.5 %collective-permute-start.8 = (f32[2,16,128]{2,1,0:T(8,128)S(1)}, f32[2,16,128]{2,1,0:T(8,128)S(1)}, u32[]{:S(2)}, u32[]{:S(2)}) collective-permute-start(f32[2,16,128]{2,1,0:T(8,128)S(1)} %get-tuple-element.27.ty1), channel_id=1, source_target_pairs={{0,6},{2,4},{4,2},{6,0},{1,7},{3,5},{5,3},{7,1},{8,14},{10,12},{12... | collective-permute-start | bytes 49160 | tf_op jit(solution)/shard_map/faces_out/ppermute | solution.py:27
  30.9 4.3 %collective-permute-start.9 = (f32[8,512]{1,0:T(8,128)S(1)}, f32[8,512]{1,0:T(8,128)S(1)}, u32[]{:S(2)}, u32[]{:S(2)}) collective-permute-start(f32[8,512]{1,0:T(8,128)S(1)} %get-tuple-element.28.tz), channel_id=1, source_target_pairs={{0,1},{1,0},{2,3},{3,2},{4,5},{5,4},{6,7},{7,6},{8,9},{9,8},{10,11... | collective-permute-start | bytes 49160 | tf_op jit(solution)/shard_map/faces_out/ppermute | solution.py:27
  35.2 13.6 %copy-start.1 = (f32[16,32,128]{2,1,0:T(8,128)S(1)}, f32[16,32,128]{2,1,0:T(8,128)}, u32[]{:S(2)}) copy-start(f32[16,32,128]{2,1,0:T(8,128)} %res.7) | copy-start | bytes 786436
  35.2 13.6 %copy-start.6 = (f32[16,32,128]{2,1,0:T(8,128)S(1)}, f32[16,32,128]{2,1,0:T(8,128)}, u32[]{:S(2)}) copy-start(f32[16,32,128]{2,1,0:T(8,128)} %direction.5) | copy-start | bytes 786436
  35.2 13.6 %copy-start.12 = (f32[16,32,128]{2,1,0:T(8,128)S(1)}, f32[16,32,128]{2,1,0:T(8,128)}, u32[]{:S(2)}) copy-start(f32[16,32,128]{2,1,0:T(8,128)} %iterate.1) | copy-start | bytes 786436
  37.4 11.3 %all-to-all-start = ((f32[32,1,128]{2,1,0:T(1,128)}), f32[32,1,128]{2,1,0:T(1,128)S(1)}, u32[]{:S(2)}, u32[]{:S(2)}) async-start(f32[32,1,128]{2,1,0:T(1,128)} %get-tuple-element.29), calls=%async_computation | async-start | bytes 32768 | tf_op jit(solution)/shard_map/sums/all_to_all | solution.py:343

commit v2 on v1

v2 whole, which is shorter than its diff:
```python
import functools

import jax
import jax.numpy as jnp
import ml_dtypes
import numpy as np
from jax import lax
from jax.experimental import pallas as pl
from jax.experimental.pallas import tpu as pltpu
from jax.sharding import PartitionSpec as P

AXES = ("gx", "gy", "gz")
F32 = jnp.float32
BF16 = jnp.bfloat16
HIGHEST = lax.Precision.HIGHEST
VMEM = pl.BlockSpec(memory_space=pltpu.VMEM)
SMEM = pl.BlockSpec(memory_space=pltpu.SMEM)
HBM = pl.BlockSpec(memory_space=pltpu.HBM)
LANES = 256
GROUP = 6


def swaps(axis, turn):
    counts = [lax.axis_size(name) for name in AXES]
    dim = AXES.index(axis)
    pairs = []
    for source in np.ndindex(*counts):
        target = list(source)
        step = 1 if (source[dim] + turn) % 2 == 0 else -1
        if axis == "gy" and not 0 <= source[dim] + step < counts[dim]:
            target[0] ^= 1
        else:
            target[dim] = (source[dim] + step) % counts[dim]
        pairs.append(tuple(int(np.ravel_multi_index(where, counts)) for where in (source, target)))
    return pairs


def swap(block, axis, turn):
    return lax.ppermute(block, AXES, swaps(axis, turn))


def place(axis):
    index = lax.axis_index(axis)
    return index % 2 == 0, index > 0, index < lax.axis_size(axis) - 1


def sides(turn0, turn1, where):
    even, below, above = where
    low = jnp.where(below, jnp.where(even, turn1, turn0), 0.0)
    high = jnp.where(above, jnp.where(even, turn0, turn1), 0.0)
    return low, high


def halves(value):
    high = value.astype(BF16)
    return high, (value - high.astype(F32)).astype(BF16)


def dot(a, b):
    return lax.dot_general(a, b, (((1,), (0,)), ((), ())), preferred_element_type=F32)


def dot_rows(a, b):
    return lax.dot_general(a, b, (((0,), (0,)), ((), ())), preferred_element_type=F32)


def dot_lanes(a, b):
    return lax.dot_general(a, b, (((1,), (1,)), ((), ())), preferred_element_type=F32)


def iota(shape, dim):
    return lax.broadcasted_iota(jnp.int32, shape, dim)


def basis(n):
    idx = np.arange(n, dtype=np.float64) + 1.0
    values = 2.0 - 2.0 * np.cos(np.pi * idx / (n + 1))
    return np.sqrt(2.0 / (n + 1)) * np.sin(np.pi * idx[:, None] * idx[None, :] / (n + 1)), values


def np_halves(table):
    high = table.astype(np.float32).astype(ml_dtypes.bfloat16)
    return high, (table - high.astype(np.float64)).astype(np.float32).astype(ml_dtypes.bfloat16)


@functools.cache
def solve_tables(size_x, size_y, size_z):
    nx, ny, nz = size_x + 2, size_y + 2, size_z + 2
    qy, ly = basis(ny)
    qz, lz = basis(nz)
    pad = -(-ny // 8) * 8
    forward = np.zeros((size_z, LANES))
    forward[:, :nz] = qz[1:-1]
    ends = np.zeros((2, LANES))
    ends[:, :nz] = qz[[0, -1]]
    fh, fl = np_halves(forward)
    eh, el = np_halves(ends)
    face = np.zeros((16, LANES), ml_dtypes.bfloat16)
    face[0:2], face[2:4], face[4:6] = eh, eh, el
    out_ends = np.zeros((32, LANES), ml_dtypes.bfloat16)
    out_ends[0:2], out_ends[16:18] = eh, el
    into = np.zeros((GROUP * pad, LANES))
    for s in range(GROUP):
        into[s * pad : s * pad + ny, s * size_y : (s + 1) * size_y] = qy[1:-1].T
    rim = np.zeros((pad, 2 * LANES))
    rim[:ny, :LANES], rim[:ny, LANES:] = qy[0][:, None], qy[-1][:, None]
    groups = nx // GROUP
    back = np.zeros((groups, GROUP * size_y + 2 * size_x, LANES))
    for g in range(groups):
        for s in range(GROUP):
            modes = slice(s * pad, s * pad + ny)
            back[g, s * size_y : (s + 1) * size_y, modes] = qy[1:-1]
            i = g * GROUP + s - 1
            if 0 <= i < size_x:
                back[g, GROUP * size_y + i, modes] = qy[0]
                back[g, GROUP * size_y + size_x + i, modes] = qy[-1]
    middle = np.full((pad, LANES), 2.0)
    middle[:ny, :nz] += ly[:, None] + lz[None, :]
    factors = np.zeros((nx, pad, LANES))
    previous = 0.0
    for i in range(nx):
        previous = 1.0 / (middle - previous)
        factors[i] = previous
    ih, il = np_halves(into)
    bh, bl = np_halves(back.reshape(-1, LANES))
    return dict(
        fwd=np.concatenate([fh, fh, fl]),
        face=face,
        into=np.concatenate([ih, il]),
        back=np.concatenate([bh, bl]),
        factors=factors.astype(np.float32).reshape(nx * pad, LANES),
        rim=rim.astype(np.float32),
        out=np.concatenate([np.ascontiguousarray(fh.T), np.ascontiguousarray(fl.T)], axis=1),
        out_ends=out_ends,
    )


def lane_rows(fields, lane):
    depth = fields[0].shape[1]
    total = None
    for f, field in enumerate(fields):
        at = iota((16, 2 * depth), 1)
        pick = jnp.where((iota((16, 2 * depth), 0) == f) & ((at == lane) | (at == lane + depth)), 1.0, 0.0).astype(BF16)
        rows = dot_lanes(pick, jnp.concatenate(halves(field), axis=1))
        total = rows if total is None else total + rows
    return total[:8]


def lane_ends(lines, even, depth):
    count = len(lines)
    pieces = []
    for line in lines:
        pieces += halves(line)
    size = lines[0].shape[1]
    stack = jnp.zeros((16, size), F32)
    for k, piece in enumerate(pieces):
        stack = jnp.where(iota((16, size), 0) == k, piece.astype(F32), stack)
    shape = (16, count * depth)
    lane = jnp.where(even, depth - 1, 0) + iota(shape, 0) // 2 * depth
    pick = jnp.where((iota(shape, 0) < 2 * count) & (iota(shape, 1) == lane), 1.0, 0.0).astype(BF16)
    wide = dot_rows(stack.astype(BF16), pick)
    return [wide[:, k * depth : (k + 1) * depth] for k in range(count)]


def pack_kernel(
    res_hbm, direction_hbm, mu_hbm, msk_hbm,
    sx0, sx1, sy0, sy1, sz, masked_out, mask_out, d_out, mu_out,
    res, direction, msk, arrived,
):
    size_x, size_y, size_z = res.shape
    even_x, even_y, even_z = (place(axis)[0] for axis in AXES)
    copies = [
        pltpu.make_async_copy(source, target, arrived.at[k])
        for k, (source, target) in enumerate(
            ((msk_hbm, msk), (res_hbm, res), (direction_hbm, direction), (mu_hbm, mu_out))
        )
    ]
    for copy in copies:
        copy.start()
    for copy in copies:
        copy.wait()
    mask = msk[...].astype(F32)
    fields = (mask * res[...], mask, mask * direction[...], mu_out[...])
    masked_out[...], mask_out[...], d_out[...] = fields[:3]
    for f, field in enumerate(fields):
        low, high = field[0], field[size_x - 1]
        sx0[f] = jnp.where(even_x, high, low)
        sx1[f] = jnp.where(even_x, low, high)
        low, high = field[:, 0], field[:, size_y - 1]
        sy0[f] = jnp.where(even_y, high, low)
        sy1[f] = jnp.where(even_y, low, high)
    flat = [field.reshape(size_x * size_y, size_z) for field in fields]
    sz[...] = lane_rows(flat, jnp.where(even_z, size_z - 1, 0))


def along_z(rows, fwd, size_z):
    high, low = halves(rows)
    return dot(jnp.concatenate([high, low], axis=1), fwd[: 2 * size_z]) + dot(high, fwd[2 * size_z :])


def own_kernel(masked, *refs):
    count = (len(refs) - 2) // 2
    tables, loaded, (work, arrived) = refs[:count], refs[count : 2 * count], refs[2 * count :]
    copies = [pltpu.make_async_copy(s, t, arrived.at[k]) for k, (s, t) in enumerate(zip(tables, loaded))]
    for copy in copies:
        copy.start()
    for copy in copies:
        copy.wait()
    size_x, size_y, size_z = masked.shape
    work[...] = along_z(masked[...].reshape(size_x * size_y, size_z), loaded[0], size_z)


def solve_kernel(
    work, mask, mu, rx0, rx1, ry0, ry1, rz, fwd, face_table, into, back, factors, rim, out, out_ends,
    own, tx0, tx1, ty0, ty1, tz,
):
    size_x, size_y, size_z = mask.shape
    rows = size_x * size_y
    pad = rim.shape[0]
    nx = size_x + 2
    where_x, where_y, where_z = (place(axis) for axis in AXES)
    even_z = where_z[0]
    x_low, x_high = sides(rx0[0:2], rx1[0:2], where_x)
    y_low, y_high = sides(ry0[0:2], ry1[0:2], where_y)
    edge = along_z(jnp.concatenate([x_low[0], x_high[0], y_low[0], y_high[0]], axis=0), fwd, size_z)
    line = rz[0:1]
    line_h, line_l = halves(line)
    at = iota((16, rows), 0)
    mine = (at < 6) & (at % 2 == jnp.where(even_z, 1, 0))
    line = jnp.where(mine, jnp.where(at // 2 == 1, line_l.astype(F32), line_h.astype(F32)), 0.0)
    face = dot_rows(line.astype(BF16), face_table[...])
    box = jnp.concatenate([edge[:size_y], work[...] + face, edge[size_y : 2 * size_y]], axis=0)
    box_h, box_l = halves(box)
    modes = []
    into_h, into_l = into[: GROUP * pad, : GROUP * size_y], into[GROUP * pad :, : GROUP * size_y]
    for g in range(nx // GROUP):
        part = slice(g * GROUP * size_y, (g + 1) * GROUP * size_y)
        modes.append(dot(into_h, box_h[part]) + dot(into_l, box_h[part]) + dot(into_h, box_l[part]))
    modes = jnp.concatenate(modes, axis=0)
    rim_low, rim_high = rim[:, :LANES], rim[:, LANES:]
    solved = []
    for i in range(nx):
        value = modes[i * pad : (i + 1) * pad]
        if 0 < i < nx - 1:
            at = 2 * size_y + i - 1
            value = value + rim_low * edge[at : at + 1] + rim_high * edge[at + size_x : at + size_x + 1]
        if i:
            value = value + solved[-1]
        solved.append(value * factors[i * pad : (i + 1) * pad])
    for i in reversed(range(nx - 1)):
        solved[i] = solved[i] + factors[i * pad : (i + 1) * pad] * solved[i + 1]
    solved = jnp.concatenate(solved, axis=0)
    high, low = halves(solved)
    group_rows = GROUP * size_y + 2 * size_x
    half = back.shape[0] // 2
    local, y_faces = [], None
    for g in range(nx // GROUP):
        part = slice(g * GROUP * pad, (g + 1) * GROUP * pad)
        table_h = back[g * group_rows : (g + 1) * group_rows, : GROUP * pad]
        table_l = back[half + g * group_rows : half + (g + 1) * group_rows, : GROUP * pad]
        value = dot(table_h, high[part]) + dot(table_l, high[part]) + dot(table_h, low[part])
        local.append(value[: GROUP * size_y])
        rest = value[GROUP * size_y :]
        y_faces = rest if y_faces is None else y_faces + rest
    local = jnp.concatenate(local + [y_faces], axis=0)
    scale = (rows * size_z) / jnp.sum(mu[...])
    local = local * scale
    high, low = halves(local)
    both = dot(high, out[...])
    local = both[:, :size_z] + both[:, size_z:] + dot(low, out[:, :size_z])
    own_h, own_l = high[size_y : size_y + rows], low[size_y : size_y + rows]
    face = dot_lanes(out_ends[0:16], own_h) + dot_lanes(out_ends[0:16], own_l) + dot_lanes(out_ends[16:32], own_h)

    def inner(shape, dim):
        at = iota(shape, dim)
        return (at >= 1) & (at <= shape[dim] - 2)

    own_flat = mask[...].reshape(rows, size_z) * local[size_y : size_y + rows]
    own_box = own_flat.reshape(size_x, size_y, size_z)
    own[...] = own_box
    shape = (size_y, size_z)
    kept = inner(shape, 0) & inner(shape, 1)
    g_low = jnp.where(kept, local[:size_y] * x_low[1], 0.0)
    g_high = jnp.where(kept, local[size_y + rows : 2 * size_y + rows] * x_high[1], 0.0)
    even = where_x[0]
    low, high = own_box[0], own_box[size_x - 1]
    tx0[0] = jnp.where(even, high, low)
    tx0[1] = jnp.where(even, g_high, g_low)
    tx1[0] = jnp.where(even, low, high)
    tx1[1] = jnp.where(even, g_low, g_high)
    shape = (size_x, size_z)
    kept = inner(shape, 0) & inner(shape, 1)
    at = 2 * size_y + rows
    g_low = jnp.where(kept, local[at : at + size_x] * y_low[1], 0.0)
    g_high = jnp.where(kept, local[at + size_x : at + 2 * size_x] * y_high[1], 0.0)
    even = where_y[0]
    low, high = own_box[:, 0], own_box[:, size_y - 1]
    ty0[0] = jnp.where(even, high, low)
    ty0[1] = jnp.where(even, g_high, g_low)
    ty1[0] = jnp.where(even, low, high)
    ty1[1] = jnp.where(even, g_low, g_high)
    mine = lane_rows([own_flat], jnp.where(even_z, size_z - 1, 0))
    ids = iota((1, rows), 1)
    x_at, y_at = ids // size_y, ids % size_y
    kept = (x_at >= 1) & (x_at <= size_x - 2) & (y_at >= 1) & (y_at <= size_y - 2)
    ghost = jnp.where(kept, jnp.where(even_z, face[1:2], face[0:1]) * rz[1:2], 0.0)
    tz[...] = jnp.where(iota((8, rows), 0) == 1, jnp.broadcast_to(ghost, (8, rows)), mine)


def beside(value, y_sides, face, box):
    size_x, size_y, size_z = box
    rows = size_x * size_y

    def wide(side):
        return jnp.broadcast_to(side[:, None, :], box).reshape(rows, size_z)

    at = iota((rows, size_z), 0) % size_y
    next_y = jnp.where(at == size_y - 1, wide(y_sides[1]), pltpu.roll(value, rows - 1, 0))
    at = iota((rows, size_z), 1)
    next_z = jnp.where(at == size_z - 1, face, pltpu.roll(value, size_z - 1, 1))
    return next_y, next_z, wide(y_sides[0])


def flux(value, x_sides, y_sides, face, wx, wy, wy0, wz, wz0, box):
    size_x, size_y, size_z = box
    rows = size_x * size_y
    ext = jnp.concatenate([x_sides[0][None], value.reshape(box), x_sides[1][None]], axis=0)
    flow = wx * (ext[1:] - ext[:-1])
    total = (flow[:-1] - flow[1:]).reshape(rows, size_z)
    next_y, next_z, before_y = beside(value, y_sides, face, box)
    flow = wy * (next_y - value)
    at = iota((rows, size_z), 0) % size_y
    first = wy0 * (value - before_y)
    total = total + jnp.where(at == 0, first, pltpu.roll(flow, 1, 0)) - flow
    flow = wz * (next_z - value)
    first = wz0 * (value - face)
    at = iota((rows, size_z), 1)
    return total + jnp.where(at == 0, first, pltpu.roll(flow, 1, 1)) - flow


def links_kernel(
    mask, d, mu, rx0, rx1, ry0, ry1, rz,
    ad_out, wx_out, wy_out, wy0_out, wz_out, wz0_out,
):
    box = mask.shape
    size_x, size_y, size_z = box
    rows = size_x * size_y
    where_x, where_y, where_z = (place(axis) for axis in AXES)
    x_near = sides(rx0[2:4], rx1[2:4], where_x)
    y_near = sides(ry0[2:4], ry1[2:4], where_y)
    d_face, mu_face = lane_ends([rz[2:3], rz[3:4]], where_z[0], size_z)
    mu_own = mu[...].reshape(rows, size_z)
    ext = jnp.concatenate([x_near[0][1][None], mu[...], x_near[1][1][None]], axis=0)
    wx = 0.5 * (ext[1:] + ext[:-1])
    next_y, next_z, before_y = beside(mu_own, [v[1] for v in y_near], mu_face, box)
    wy, wy0 = 0.5 * (mu_own + next_y), 0.5 * (mu_own + before_y)
    wz, wz0 = 0.5 * (mu_own + next_z), 0.5 * (mu_own + mu_face)
    links = (wx, wy, wy0, wz, wz0)
    wx_out[...], wy_out[...], wy0_out[...], wz_out[...], wz0_out[...] = links
    value = d[...].reshape(rows, size_z)
    ad = flux(value, [v[0] for v in x_near], [v[0] for v in y_near], d_face, *links, box)
    ad_out[...] = mask[...].reshape(rows, size_z) * ad


def image_kernel(
    masked, mask, d, own, tx0, tx1, ty0, ty1, tz, qx0, qx1, qy0, qy1, qz, ad_in, wx, wy, wy0, wz, wz0,
    z_out, az_out, sums,
):
    box = mask.shape
    size_x, size_y, size_z = box
    rows = size_x * size_y
    where_x, where_y, where_z = (place(axis) for axis in AXES)
    x_sent = sides(tx0[1:2], tx1[1:2], where_x)
    y_sent = sides(ty0[1:2], ty1[1:2], where_y)
    x_got = sides(qx0[...], qx1[...], where_x)
    y_got = sides(qy0[...], qy1[...], where_y)
    z_face, z_more = lane_ends([qz[0:1] + tz[1:2], qz[1:2]], where_z[0], size_z)
    own_box = own[...]
    z = jnp.concatenate(
        [own_box[:1] + x_got[0][1][None], own_box[1:-1], own_box[-1:] + x_got[1][1][None]], axis=0
    )
    at = iota(box, 1)
    z = z + jnp.where(at == 0, y_got[0][1][:, None, :], 0.0) + jnp.where(at == size_y - 1, y_got[1][1][:, None, :], 0.0)
    z = z.reshape(rows, size_z) + z_more
    z = z * mask[...].reshape(rows, size_z)
    x_sides = [x_got[s][0] + x_sent[s][0] for s in (0, 1)]
    y_sides = [y_got[s][0] + y_sent[s][0] for s in (0, 1)]
    az = flux(z, x_sides, y_sides, z_face, wx[...], wy[...], wy0[...], wz[...], wz0[...], box)
    az = mask[...].reshape(rows, size_z) * az
    z_out[...] = z
    az_out[...] = az
    ad, value = ad_in[...], d[...].reshape(rows, size_z)
    parts = (
        jnp.sum(masked[...].reshape(rows, size_z) * z),
        jnp.sum(z * az),
        jnp.sum(z * ad + value * az),
        jnp.sum(value * ad),
    )
    at = iota(sums.shape, 2)
    line = jnp.zeros(sums.shape, F32)
    for k, part in enumerate(parts):
        line = jnp.where(at == k, part, line)
    sums[...] = line


def update_kernel(rz_prev, sums, iterate, res, d, z, az, ad, new_iterate, new_res, new_direction):
    line = jnp.sum(sums[...], axis=0)
    rz, zaz, zad, dad = (line[:, k : k + 1] for k in range(4))
    beta = rz / rz_prev[0]
    alpha = rz / (zaz + beta * (zad + beta * dad))
    alpha3, beta3 = (v.reshape(1, 1, 1) for v in (alpha, beta))
    box = d.shape
    p = z[...].reshape(box) + beta3 * d[...]
    new_direction[...] = p
    new_iterate[...] = iterate[...] + alpha3 * p
    new_res[...] = res[...] - alpha3 * (az[...] + beta * ad[...]).reshape(box)


def call(kernel, args, outs, specs=None, scratch=(), flops=0):
    outs = [out if isinstance(out, jax.ShapeDtypeStruct) else jax.ShapeDtypeStruct(out, F32) for out in outs]
    return pl.pallas_call(
        kernel,
        out_shape=outs,
        in_specs=specs or [VMEM] * len(args),
        out_specs=[VMEM] * len(outs),
        scratch_shapes=list(scratch),
        cost_estimate=pl.CostEstimate(flops=flops, bytes_accessed=1 << 20, transcendentals=0),
        compiler_params=pltpu.CompilerParams(vmem_limit_bytes=32 * 1024 * 1024),
    )(*args)


def exchange(sx0, sx1, sy0, sy1, sz):
    return (
        swap(sx0, "gx", 0),
        swap(sx1, "gx", 1),
        swap(sy0, "gy", 0),
        swap(sy1, "gy", 1),
        swap(sz, "gz", 0),
    )


def shards(iterate, residual, direction, permeability, unfixed_node_mask, rz_prev):
    size_x, size_y, size_z = residual.shape
    box = residual.shape
    rows = size_x * size_y
    flat = (rows, size_z)
    devices = lax.axis_size(AXES)

    def faces(count):
        return [(count, size_y, size_z)] * 2 + [(count, size_x, size_z)] * 2 + [(8, rows)]

    tables = list(solve_tables(size_x, size_y, size_z).values())
    with jax.named_scope("pack"):
        *sent, masked, mask, d, mu = call(
            pack_kernel,
            (residual, direction, permeability, unfixed_node_mask),
            faces(4) + [box] * 4,
            [HBM] * 4,
            [pltpu.VMEM(box, F32), pltpu.VMEM(box, F32), pltpu.VMEM(box, jnp.int32), pltpu.SemaphoreType.DMA((4,))],
        )
    with jax.named_scope("faces_in"):
        near = exchange(*sent)
    with jax.named_scope("own_part"):
        *tables, work = call(
            own_kernel,
            (masked, *map(jnp.asarray, tables)),
            [jax.ShapeDtypeStruct(t.shape, t.dtype) for t in tables] + [(rows, LANES)],
            [VMEM] + [HBM] * len(tables),
            [pltpu.SemaphoreType.DMA((len(tables),))],
        )
    with jax.named_scope("solve"):
        own, *made = call(solve_kernel, (work, mask, mu, *near, *tables), [box] + faces(2))
    with jax.named_scope("faces_out"):
        got = exchange(*made)
    with jax.named_scope("links"):
        ad, *links = call(
            links_kernel, (mask, d, mu, *near), [flat, (size_x + 1, size_y, size_z), flat, flat, flat, flat]
        )
    with jax.named_scope("image"):
        z, az, sums = call(
            image_kernel, (masked, mask, d, own, *made, *got, ad, *links), [flat, flat, (devices, 1, 128)]
        )
    with jax.named_scope("sums"):
        sums = lax.all_to_all(sums, AXES, 0, 0, tiled=True)
    with jax.named_scope("update"):
        args = (rz_prev, sums, iterate, residual, d, z, az, ad)
        return tuple(call(update_kernel, args, [box] * 3, [SMEM] + [VMEM] * 7))


def solution(mesh):
    in_specs = (P(*AXES),) * 5 + (P(),)
    out_specs = (P(*AXES),) * 3
    return jax.shard_map(shards, mesh=mesh, in_specs=in_specs, out_specs=out_specs, check_vma=False)
```

time: 50.6 us -> 39.4 us (0.78)
  starting transfers between devices: 17 us -> 13.3 us
  local copies, waits for them, and re-layouts: 11 us -> 7.63 us
  waiting for transfers between devices: 11.4 us -> 9.08 us
  Pallas kernels: 9.33 us -> 7.54 us
    unnamed x34 -> x28, local copies, waits for them, and re-layouts: 11 us -> 7.63 us
    ppermute x10, waiting for transfers between devices: 4.98 us -> 2.68 us  [swap(): return lax.ppermute(block, AXES, swaps(axis, turn))]
    ppermute x10, starting transfers between devices: 12.8 us -> 10.6 us  [swap(): return lax.ppermute(block, AXES, swaps(axis, turn))]
    pallas_call x4 -> x6, Pallas kernels: 9.33 us -> 7.54 us  [call(): pl.pallas_call(kernel, out_shape=outs, in_specs=specs or [VMEM] * len(arg...]
    all_to_all x1, starting transfers between devices: 4.26 us -> 2.75 us  [shards(): sums = lax.all_to_all(sums, AXES, 0, 0, tiled=True)]
  transfers between devices with their start and end apart: 11 -> 11, of which waited for: 4 -> 3; matrix products, arithmetic and copies ran while one was open for 0% -> 0% of each run, Pallas kernels for 0% -> 6%
where the time goes in v2:
time: 39.4 us; the launch traced here: 39 us
  starting transfers between devices  13.3 us (34%)
  waiting for transfers between devices  9.08 us (23%)
  local copies, waits for them, and re-layouts  7.63 us (19%)
  Pallas kernels  7.54 us (19%)
  between operations  1.4 us (4%)
    ppermute x10, starting transfers between devices, swap(): return lax.ppermute(block, AXES, swaps(axis, turn))  10.6 us
    unnamed x28, local copies, waits for them, and re-layouts  7.63 us
    pallas_call x6, Pallas kernels, call(): pl.pallas_call(kernel, out_shape=outs, in_specs=specs or [VMEM] * len(arg...  7.54 us
    all_to_all x1, waiting for transfers between devices, shards(): sums = lax.all_to_all(sums, AXES, 0, 0, tiled=True)  6.39 us
    all_to_all x1, starting transfers between devices, shards(): sums = lax.all_to_all(sums, AXES, 0, 0, tiled=True)  2.75 us
    ppermute x10, waiting for transfers between devices, swap(): return lax.ppermute(block, AXES, swaps(axis, turn))  2.68 us
  transfers between devices with their start and end apart: 11, of which 3 were waited for; matrix products, arithmetic and copies ran while one was open for 0% of the time, Pallas kernels for 6%

profile of v2, /device:TPU:0, one launch (start us, length us, event | category | flops | bytes accessed | tf_op | source)
XLA Modules:
  0.0 39.0 jit_solution(2159202344297802989)
XLA Ops:
  0.6 0.0 copy-start
  0.6 0.9 %copy-done = f32[16,32,128]{2,1,0:T(8,128)S(1)} copy-done((f32[16,32,128]{2,1,0:T(8,128)S(1)}, f32[16,32,128]{2,1,0:T(8,128)}, u32[]{:S(2)}) %copy-start) | copy-done | bytes 262168
  1.6 0.9 %copy-done.4 = f32[16,32,128]{2,1,0:T(8,128)S(1)} copy-done((f32[16,32,128]{2,1,0:T(8,128)S(1)}, f32[16,32,128]{2,1,0:T(8,128)}, u32[]{:S(2)}) %copy-start.4) | copy-done | bytes 262168
  2.5 0.9 %copy-done.5 = f32[16,32,128]{2,1,0:T(8,128)S(1)} copy-done((f32[16,32,128]{2,1,0:T(8,128)S(1)}, f32[16,32,128]{2,1,0:T(8,128)}, u32[]{:S(2)}) %copy-start.5) | copy-done | bytes 262168
  3.5 0.9 %copy-done.6 = s32[16,32,128]{2,1,0:T(8,128)S(1)} copy-done((s32[16,32,128]{2,1,0:T(8,128)S(1)}, s32[16,32,128]{2,1,0:T(8,128)}, u32[]{:S(2)}) %copy-start.6) | copy-done | bytes 262168
  4.4 0.5 %pack.1 = (f32[4,32,128]{2,1,0:T(8,128)S(1)}, f32[4,32,128]{2,1,0:T(8,128)S(1)}, f32[4,16,128]{2,1,0:T(8,128)S(1)}, f32[4,16,128]{2,1,0:T(8,128)S(1)}, f32[8,512...) custom-call(f32[16,32,128]{2,1,0:T(8,128)S(1)} %copy-done, ...), custom_call_target="tpu_custom_call" | custom-call | bytes 1048576 | tf_op jit(solution)/shard_map/pack/pallas_call | solution.py:421
  5.0 0.0 copy-start.13
  5.0 0.5 %collective-permute-start = (f32[4,32,128]{2,1,0:T(8,128)S(1)}, f32[4,32,128]{2,1,0:T(8,128)S(1)}, u32[]{:S(2)}, u32[]{:S(2)}) collective-permute-start(f32[4,32,128]{2,1,0:T(8,128)S(1)} %get-tuple-element.41), channel_id=1, source_target_pairs={{0,8},{1,9},{2,10},{3,11},{4,12},{5,13},{6,14},{7,15},{8,0},{9,1},... | collective-permute-start | bytes 196616 | tf_op jit(solution)/shard_map/faces_in/ppermute | solution.py:39
  5.5 2.6 %collective-permute-start.1 = (f32[4,32,128]{2,1,0:T(8,128)S(1)}, f32[4,32,128]{2,1,0:T(8,128)S(1)}, u32[]{:S(2)}, u32[]{:S(2)}) collective-permute-start(f32[4,32,128]{2,1,0:T(8,128)S(1)} %get-tuple-element.42), channel_id=1, source_target_pairs={{0,24},{1,25},{2,26},{3,27},{4,28},{5,29},{6,30},{7,31},{8,16},{9,... | collective-permute-start | bytes 196616 | tf_op jit(solution)/shard_map/faces_in/ppermute | solution.py:39
  8.1 1.6 %collective-permute-start.2 = (f32[4,16,128]{2,1,0:T(8,128)S(1)}, f32[4,16,128]{2,1,0:T(8,128)S(1)}, u32[]{:S(2)}, u32[]{:S(2)}) collective-permute-start(f32[4,16,128]{2,1,0:T(8,128)S(1)} %get-tuple-element.43), channel_id=1, source_target_pairs={{0,2},{1,3},{2,0},{3,1},{4,6},{5,7},{6,4},{7,5},{8,10},{9,11},{10,... | collective-permute-start | bytes 98312 | tf_op jit(solution)/shard_map/faces_in/ppermute | solution.py:39
  9.7 1.5 %collective-permute-start.4 = (f32[8,512]{1,0:T(8,128)S(1)}, f32[8,512]{1,0:T(8,128)S(1)}, u32[]{:S(2)}, u32[]{:S(2)}) collective-permute-start(f32[8,512]{1,0:T(8,128)S(1)} %get-tuple-element.45), channel_id=1, source_target_pairs={{0,1},{1,0},{2,3},{3,2},{4,5},{5,4},{6,7},{7,6},{8,9},{9,8},{10,11... | collective-permute-start | bytes 49160 | tf_op jit(solution)/shard_map/faces_in/ppermute | solution.py:39
  11.2 0.0 copy-start.3
  11.2 1.1 %copy-done.3 = bf16[1344,256]{1,0:T(8,128)(2,1)S(1)} copy-done((bf16[1344,256]{1,0:T(8,128)(2,1)S(1)}, bf16[1344,256]{1,0:T(8,128)(2,1)}, u32[]{:S(2)}) %copy-start.3) | copy-done | bytes 688152
  12.3 0.9 %copy-done.9 = bf16[384,256]{1,0:T(8,128)(2,1)S(1)} copy-done((bf16[384,256]{1,0:T(8,128)(2,1)S(1)}, bf16[384,256]{1,0:T(8,128)(2,1)}, u32[]{:S(2)}) %copy-start.9) | copy-done | bytes 196632
  13.2 0.9 %copy-done.10 = bf16[256,256]{1,0:T(8,128)(2,1)S(1)} copy-done((bf16[256,256]{1,0:T(8,128)(2,1)S(1)}, bf16[256,256]{1,0:T(8,128)(2,1)}, u32[]{:S(2)}) %copy-start.10) | copy-done | bytes 131096
  14.2 0.9 %copy-done.11 = f32[40,512]{1,0:T(8,128)S(1)} copy-done((f32[40,512]{1,0:T(8,128)S(1)}, f32[40,512]{1,0:T(8,128)}, u32[]{:S(2)}) %copy-start.11) | copy-done | bytes 81944
  15.0 1.8 %own_part.1 = (bf16[384,256]{1,0:T(8,128)(2,1)S(1)}, bf16[16,256]{1,0:T(8,128)(2,1)S(1)}, bf16[480,256]{1,0:T(8,128)(2,1)S(1)}, bf16[1344,256]{1,0:T(8,128)(2,1)...) custom-call(f32[16,32,128]{2,1,0:T(8,128)S(1)} %get-tuple-element.36, ...), custom_call_target="tpu_custom_call" | custom-call | bytes 1048576 | tf_op jit(solution)/shard_map/own_part/pallas_call | solution.py:421
  16.9 0.0 collective-permute-done.2.ry0
  16.9 0.0 collective-permute-done.3.ry1
  16.9 2.0 %solve.1 = (f32[16,32,128]{2,1,0:T(8,128)S(1)}, f32[2,32,128]{2,1,0:T(8,128)S(1)}, f32[2,32,128]{2,1,0:T(8,128)S(1)}, f32[2,16,128]{2,1,0:T(8,128)S(1)}, f32[2,1...) custom-call(f32[512,256]{1,0:T(8,128)S(1)} %get-tuple-element.39.work, f32[16,32,128]{2,1,0:T(8,128)S(1)} %get-tuple-element.37.mask, ...), custom_call_target="tpu_custom_call" | custom-call | bytes 1048576 | tf_op jit(solution)/shard_map/solve/pallas_call | solution.py:421
  19.0 0.3 collective-permute-start.5
  19.2 0.4 %collective-permute-start.6 = (f32[2,32,128]{2,1,0:T(8,128)S(1)}, f32[2,32,128]{2,1,0:T(8,128)S(1)}, u32[]{:S(2)}, u32[]{:S(2)}) collective-permute-start(f32[2,32,128]{2,1,0:T(8,128)S(1)} %get-tuple-element.56.tx1), channel_id=1, source_target_pairs={{0,24},{1,25},{2,26},{3,27},{4,28},{5,29},{6,30},{7,31},{8,16},{9,... | collective-permute-start | bytes 98312 | tf_op jit(solution)/shard_map/faces_out/ppermute | solution.py:39
  19.6 3.2 %collective-permute-start.7 = (f32[2,16,128]{2,1,0:T(8,128)S(1)}, f32[2,16,128]{2,1,0:T(8,128)S(1)}, u32[]{:S(2)}, u32[]{:S(2)}) collective-permute-start(f32[2,16,128]{2,1,0:T(8,128)S(1)} %get-tuple-element.57.ty0), channel_id=1, source_target_pairs={{0,2},{1,3},{2,0},{3,1},{4,6},{5,7},{6,4},{7,5},{8,10},{9,11},{10,... | collective-permute-start | bytes 49160 | tf_op jit(solution)/shard_map/faces_out/ppermute | solution.py:39
  22.8 0.5 %collective-permute-start.9 = (f32[8,512]{1,0:T(8,128)S(1)}, f32[8,512]{1,0:T(8,128)S(1)}, u32[]{:S(2)}, u32[]{:S(2)}) collective-permute-start(f32[8,512]{1,0:T(8,128)S(1)} %get-tuple-element.59.tz), channel_id=1, source_target_pairs={{0,1},{1,0},{2,3},{3,2},{4,5},{5,4},{6,7},{7,6},{8,9},{9,8},{10,11... | collective-permute-start | bytes 49160 | tf_op jit(solution)/shard_map/faces_out/ppermute | solution.py:39
  23.3 0.6 %links.1 = (f32[512,128]{1,0:T(8,128)S(1)}, f32[17,32,128]{2,1,0:T(8,128)S(1)}, f32[512,128]{1,0:T(8,128)S(1)}, f32[512,128]{1,0:T(8,128)S(1)}, f32[512,128]{1,0:T(8,128)S(1)}, /*index=5*/f32[512,128]{1,0:T(8,128)S(1)}) custom-call(f32[16,32,128]{2,1,0:T(8,128)S(1)} %get-tuple-element.37.mask, f32[16,32,128]{2,1,0:T(8,128)S(1)} %get-tuple-element.38.d, ...), custom_call_target="tpu_custom_call" | custom-call | bytes 1048576 | tf_op jit(solution)/shard_map/links/pallas_call | solution.py:421
  23.9 0.6 %collective-permute-done.7.qy0 = f32[2,16,128]{2,1,0:T(8,128)S(1)} collective-permute-done((f32[2,16,128]{2,1,0:T(8,128)S(1)}, f32[2,16,128]{2,1,0:T(8,128)S(1)}, u32[]{:S(2)}, u32[]{:S(2)}) %collective-permute-start.7) | collective-permute-done | bytes 16416 | tf_op jit(solution)/shard_map/faces_out/ppermute | solution.py:39
  24.5 2.0 %collective-permute-done.9.qz = f32[8,512]{1,0:T(8,128)S(1)} collective-permute-done((f32[8,512]{1,0:T(8,128)S(1)}, f32[8,512]{1,0:T(8,128)S(1)}, u32[]{:S(2)}, u32[]{:S(2)}) %collective-permute-start.9) | collective-permute-done | bytes 16416 | tf_op jit(solution)/shard_map/faces_out/ppermute | solution.py:39
  26.6 0.0 copy-start.7
  26.6 1.3 %image.1 = (f32[512,128]{1,0:T(8,128)S(1)}, f32[512,128]{1,0:T(8,128)S(1)}, f32[32,1,128]{2,1,0:T(1,128)}) custom-call(f32[16,32,128]{2,1,0:T(8,128)S(1)} %get-tuple-element.36.masked, f32[16,32,128]{2,1,0:T(8,128)S(1)} %get-tuple-element.37.mask, f32[16,32,128]{2,1,0:T(8,128)S(1)} %get-tuple-element.38.d, f32[16,32,128]{2,1,0:T(8,128)S(1)} %get-tuple-element.54.own, ...), custom_call_target="tpu_custom_call" | custom-call | bytes 1048576 | tf_op jit(solution)/shard_map/image/pallas_call | solution.py:421
  27.9 2.8 %all-to-all-start = ((f32[32,1,128]{2,1,0:T(1,128)}), f32[32,1,128]{2,1,0:T(1,128)S(1)}, u32[]{:S(2)}, u32[]{:S(2)}) async-start(f32[32,1,128]{2,1,0:T(1,128)} %get-tuple-element.66), calls=%async_computation | async-start | bytes 32768 | tf_op jit(solution)/shard_map/sums/all_to_all | solution.py:484
  31.3 6.4 %all-to-all-done.sums = f32[32,1,128]{2,1,0:T(1,128)S(1)} async-done(((f32[32,1,128]{2,1,0:T(1,128)}), f32[32,1,128]{2,1,0:T(1,128)S(1)}, u32[]{:S(2)}, u32[]{:S(2)}) %all-to-all-start) | async-done | bytes 16416 | tf_op jit(solution)/shard_map/sums/all_to_all | solution.py:484
  37.7 1.3 %update.1 = (f32[16,32,128]{2,1,0:T(8,128)}, f32[16,32,128]{2,1,0:T(8,128)}, f32[16,32,128]{2,1,0:T(8,128)}) custom-call(f32[1]{0:T(128)S(6)} %copy.17.rz_prev, f32[32,1,128]{2,1,0:T(1,128)S(1)} %all-to-all-done.sums, f32[16,32,128]{2,1,0:T(8,128)S(1)} %copy-done.7, f32[16,32,128]{2,1,0:T(8,128)S(1)} %copy-done.1, f32[16,32,128]{2,1,0:T(8,128)S(1)} %get-tuple-element.38.d, ...), custom_call_target="tpu_custom_call" | custom-call | bytes 1048576 | tf_op jit(solution)/shard_map/update/pallas_call | solution.py:421
  (24 shorter events, 0.0 us)
Async XLA Ops:
  0.6 1.0 %copy-start = (f32[16,32,128]{2,1,0:T(8,128)S(1)}, f32[16,32,128]{2,1,0:T(8,128)}, u32[]{:S(2)}) copy-start(f32[16,32,128]{2,1,0:T(8,128)} %res.1) | copy-start | bytes 786436
  1.6 0.9 %copy-start.4 = (f32[16,32,128]{2,1,0:T(8,128)S(1)}, f32[16,32,128]{2,1,0:T(8,128)}, u32[]{:S(2)}) copy-start(f32[16,32,128]{2,1,0:T(8,128)} %direction_hbm.1) | copy-start | bytes 786436
  2.5 0.9 %copy-start.5 = (f32[16,32,128]{2,1,0:T(8,128)S(1)}, f32[16,32,128]{2,1,0:T(8,128)}, u32[]{:S(2)}) copy-start(f32[16,32,128]{2,1,0:T(8,128)} %mu_hbm.1) | copy-start | bytes 786436
  3.5 0.9 %copy-start.6 = (s32[16,32,128]{2,1,0:T(8,128)S(1)}, s32[16,32,128]{2,1,0:T(8,128)}, u32[]{:S(2)}) copy-start(s32[16,32,128]{2,1,0:T(8,128)} %msk_hbm.1) | copy-start | bytes 786436
  4.4 6.8 %copy-start.2 = (f32[720,256]{1,0:T(8,128)S(1)}, f32[720,256]{1,0:T(8,128)}, u32[]{:S(2)}) copy-start(f32[720,256]{1,0:T(8,128)} %constant.20.clone.refs_4_) | copy-start | bytes 2211844
  4.4 6.8 %copy-start.8 = (bf16[480,256]{1,0:T(8,128)(2,1)S(1)}, bf16[480,256]{1,0:T(8,128)(2,1)}, u32[]{:S(2)}) copy-start(bf16[480,256]{1,0:T(8,128)(2,1)} %constant.18.clone.refs_2_) | copy-start | bytes 737284
  4.4 6.8 %copy-start.12 = (bf16[32,256]{1,0:T(8,128)(2,1)S(1)}, bf16[32,256]{1,0:T(8,128)(2,1)}, u32[]{:S(2)}) copy-start(bf16[32,256]{1,0:T(8,128)(2,1)} %constant.23.clone.refs_7_) | copy-start | bytes 49156
  5.0 6.3 %copy-start.13 = (bf16[16,256]{1,0:T(8,128)(2,1)S(1)}, bf16[16,256]{1,0:T(8,128)(2,1)}, u32[]{:S(2)}) copy-start(bf16[16,256]{1,0:T(8,128)(2,1)} %constant.17.clone.refs_1_) | copy-start | bytes 24580
  5.0 12.0 %collective-permute-start = (f32[4,32,128]{2,1,0:T(8,128)S(1)}, f32[4,32,128]{2,1,0:T(8,128)S(1)}, u32[]{:S(2)}, u32[]{:S(2)}) collective-permute-start(f32[4,32,128]{2,1,0:T(8,128)S(1)} %get-tuple-element.41), channel_id=1, source_target_pairs={{0,8},{1,9},{2,10},{3,11},{4,12},{5,13},{6,14},{7,15},{8,0},{9,1},... | collective-permute-start | bytes 196616 | tf_op jit(solution)/shard_map/faces_in/ppermute | solution.py:39
  5.5 11.5 %collective-permute-start.1 = (f32[4,32,128]{2,1,0:T(8,128)S(1)}, f32[4,32,128]{2,1,0:T(8,128)S(1)}, u32[]{:S(2)}, u32[]{:S(2)}) collective-permute-start(f32[4,32,128]{2,1,0:T(8,128)S(1)} %get-tuple-element.42), channel_id=1, source_target_pairs={{0,24},{1,25},{2,26},{3,27},{4,28},{5,29},{6,30},{7,31},{8,16},{9,... | collective-permute-start | bytes 196616 | tf_op jit(solution)/shard_map/faces_in/ppermute | solution.py:39
  8.1 8.8 %collective-permute-start.2 = (f32[4,16,128]{2,1,0:T(8,128)S(1)}, f32[4,16,128]{2,1,0:T(8,128)S(1)}, u32[]{:S(2)}, u32[]{:S(2)}) collective-permute-start(f32[4,16,128]{2,1,0:T(8,128)S(1)} %get-tuple-element.43), channel_id=1, source_target_pairs={{0,2},{1,3},{2,0},{3,1},{4,6},{5,7},{6,4},{7,5},{8,10},{9,11},{10,... | collective-permute-start | bytes 98312 | tf_op jit(solution)/shard_map/faces_in/ppermute | solution.py:39
  9.7 7.2 %collective-permute-start.3 = (f32[4,16,128]{2,1,0:T(8,128)S(1)}, f32[4,16,128]{2,1,0:T(8,128)S(1)}, u32[]{:S(2)}, u32[]{:S(2)}) collective-permute-start(f32[4,16,128]{2,1,0:T(8,128)S(1)} %get-tuple-element.44), channel_id=1, source_target_pairs={{0,8},{1,9},{2,4},{3,5},{4,2},{5,3},{6,14},{7,15},{8,0},{9,1},{10,... | collective-permute-start | bytes 98312 | tf_op jit(solution)/shard_map/faces_in/ppermute | solution.py:39
  9.7 7.2 %collective-permute-start.4 = (f32[8,512]{1,0:T(8,128)S(1)}, f32[8,512]{1,0:T(8,128)S(1)}, u32[]{:S(2)}, u32[]{:S(2)}) collective-permute-start(f32[8,512]{1,0:T(8,128)S(1)} %get-tuple-element.45), channel_id=1, source_target_pairs={{0,1},{1,0},{2,3},{3,2},{4,5},{5,4},{6,7},{7,6},{8,9},{9,8},{10,11... | collective-permute-start | bytes 49160 | tf_op jit(solution)/shard_map/faces_in/ppermute | solution.py:39
  11.2 1.1 %copy-start.3 = (bf16[1344,256]{1,0:T(8,128)(2,1)S(1)}, bf16[1344,256]{1,0:T(8,128)(2,1)}, u32[]{:S(2)}) copy-start(bf16[1344,256]{1,0:T(8,128)(2,1)} %constant.19.clone.refs_3_) | copy-start | bytes 2064388
  12.3 0.9 %copy-start.9 = (bf16[384,256]{1,0:T(8,128)(2,1)S(1)}, bf16[384,256]{1,0:T(8,128)(2,1)}, u32[]{:S(2)}) copy-start(bf16[384,256]{1,0:T(8,128)(2,1)} %constant.16.clone.refs_0_) | copy-start | bytes 589828
  13.2 0.9 %copy-start.10 = (bf16[256,256]{1,0:T(8,128)(2,1)S(1)}, bf16[256,256]{1,0:T(8,128)(2,1)}, u32[]{:S(2)}) copy-start(bf16[256,256]{1,0:T(8,128)(2,1)} %constant.22.clone.refs_6_) | copy-start | bytes 393220
  14.2 0.9 %copy-start.11 = (f32[40,512]{1,0:T(8,128)S(1)}, f32[40,512]{1,0:T(8,128)}, u32[]{:S(2)}) copy-start(f32[40,512]{1,0:T(8,128)} %constant.21.clone.refs_5_) | copy-start | bytes 245764
  19.0 7.6 %collective-permute-start.5 = (f32[2,32,128]{2,1,0:T(8,128)S(1)}, f32[2,32,128]{2,1,0:T(8,128)S(1)}, u32[]{:S(2)}, u32[]{:S(2)}) collective-permute-start(f32[2,32,128]{2,1,0:T(8,128)S(1)} %get-tuple-element.55.tx0), channel_id=1, source_target_pairs={{0,8},{1,9},{2,10},{3,11},{4,12},{5,13},{6,14},{7,15},{8,0},{9,1},... | collective-permute-start | bytes 98312 | tf_op jit(solution)/shard_map/faces_out/ppermute | solution.py:39
  19.2 7.3 %collective-permute-start.6 = (f32[2,32,128]{2,1,0:T(8,128)S(1)}, f32[2,32,128]{2,1,0:T(8,128)S(1)}, u32[]{:S(2)}, u32[]{:S(2)}) collective-permute-start(f32[2,32,128]{2,1,0:T(8,128)S(1)} %get-tuple-element.56.tx1), channel_id=1, source_target_pairs={{0,24},{1,25},{2,26},{3,27},{4,28},{5,29},{6,30},{7,31},{8,16},{9,... | collective-permute-start | bytes 98312 | tf_op jit(solution)/shard_map/faces_out/ppermute | solution.py:39
  19.6 4.9 %collective-permute-start.7 = (f32[2,16,128]{2,1,0:T(8,128)S(1)}, f32[2,16,128]{2,1,0:T(8,128)S(1)}, u32[]{:S(2)}, u32[]{:S(2)}) collective-permute-start(f32[2,16,128]{2,1,0:T(8,128)S(1)} %get-tuple-element.57.ty0), channel_id=1, source_target_pairs={{0,2},{1,3},{2,0},{3,1},{4,6},{5,7},{6,4},{7,5},{8,10},{9,11},{10,... | collective-permute-start | bytes 49160 | tf_op jit(solution)/shard_map/faces_out/ppermute | solution.py:39
  22.8 1.7 %collective-permute-start.8 = (f32[2,16,128]{2,1,0:T(8,128)S(1)}, f32[2,16,128]{2,1,0:T(8,128)S(1)}, u32[]{:S(2)}, u32[]{:S(2)}) collective-permute-start(f32[2,16,128]{2,1,0:T(8,128)S(1)} %get-tuple-element.58.ty1), channel_id=1, source_target_pairs={{0,8},{1,9},{2,4},{3,5},{4,2},{5,3},{6,14},{7,15},{8,0},{9,1},{10,... | collective-permute-start | bytes 49160 | tf_op jit(solution)/shard_map/faces_out/ppermute | solution.py:39
  22.8 3.7 %collective-permute-start.9 = (f32[8,512]{1,0:T(8,128)S(1)}, f32[8,512]{1,0:T(8,128)S(1)}, u32[]{:S(2)}, u32[]{:S(2)}) collective-permute-start(f32[8,512]{1,0:T(8,128)S(1)} %get-tuple-element.59.tz), channel_id=1, source_target_pairs={{0,1},{1,0},{2,3},{3,2},{4,5},{5,4},{6,7},{7,6},{8,9},{9,8},{10,11... | collective-permute-start | bytes 49160 | tf_op jit(solution)/shard_map/faces_out/ppermute | solution.py:39
  26.6 11.1 %copy-start.1 = (f32[16,32,128]{2,1,0:T(8,128)S(1)}, f32[16,32,128]{2,1,0:T(8,128)}, u32[]{:S(2)}) copy-start(f32[16,32,128]{2,1,0:T(8,128)} %res.1) | copy-start | bytes 786436
  26.6 11.1 %copy-start.7 = (f32[16,32,128]{2,1,0:T(8,128)S(1)}, f32[16,32,128]{2,1,0:T(8,128)}, u32[]{:S(2)}) copy-start(f32[16,32,128]{2,1,0:T(8,128)} %iterate.1) | copy-start | bytes 786436
  27.9 9.8 %all-to-all-start = ((f32[32,1,128]{2,1,0:T(1,128)}), f32[32,1,128]{2,1,0:T(1,128)S(1)}, u32[]{:S(2)}, u32[]{:S(2)}) async-start(f32[32,1,128]{2,1,0:T(1,128)} %get-tuple-element.66), calls=%async_computation | async-start | bytes 32768 | tf_op jit(solution)/shard_map/sums/all_to_all | solution.py:484

commit v3 on v2

--- a/solution.py
+++ b/solution.py
@@ -15,7 +15,6 @@
 HIGHEST = lax.Precision.HIGHEST
 VMEM = pl.BlockSpec(memory_space=pltpu.VMEM)
 SMEM = pl.BlockSpec(memory_space=pltpu.SMEM)
-HBM = pl.BlockSpec(memory_space=pltpu.HBM)
 LANES = 256
 GROUP = 6
 
@@ -102,33 +101,32 @@
     into = np.zeros((GROUP * pad, LANES))
     for s in range(GROUP):
         into[s * pad : s * pad + ny, s * size_y : (s + 1) * size_y] = qy[1:-1].T
-    rim = np.zeros((pad, 2 * LANES))
-    rim[:ny, :LANES], rim[:ny, LANES:] = qy[0][:, None], qy[-1][:, None]
+    rim = np.zeros((pad, LANES // 2))
+    rim[:ny, 0], rim[:ny, 1] = qy[0], qy[-1]
     groups = nx // GROUP
-    back = np.zeros((groups, GROUP * size_y + 2 * size_x, LANES))
-    for g in range(groups):
-        for s in range(GROUP):
-            modes = slice(s * pad, s * pad + ny)
-            back[g, s * size_y : (s + 1) * size_y, modes] = qy[1:-1]
+    back = np.zeros((GROUP * size_y, LANES))
+    faces = np.zeros((groups, 2, size_x, LANES))
+    for s in range(GROUP):
+        modes = slice(s * pad, s * pad + ny)
+        back[s * size_y : (s + 1) * size_y, modes] = qy[1:-1]
+        for g in range(groups):
             i = g * GROUP + s - 1
             if 0 <= i < size_x:
-                back[g, GROUP * size_y + i, modes] = qy[0]
-                back[g, GROUP * size_y + size_x + i, modes] = qy[-1]
+                faces[g, 0, i, modes] = qy[0]
+                faces[g, 1, i, modes] = qy[-1]
     middle = np.full((pad, LANES), 2.0)
     middle[:ny, :nz] += ly[:, None] + lz[None, :]
-    factors = np.zeros((nx, pad, LANES))
-    previous = 0.0
-    for i in range(nx):
-        previous = 1.0 / (middle - previous)
-        factors[i] = previous
+    middle[ny:], middle[:, nz:] = 4.0, 4.0
     ih, il = np_halves(into)
-    bh, bl = np_halves(back.reshape(-1, LANES))
+    bh, bl = np_halves(back)
+    gh, gl = np_halves(faces.reshape(-1, LANES))
     return dict(
-        fwd=np.concatenate([fh, fh, fl]),
+        fwd=np.concatenate([fh, fl]),
+        middle=middle.astype(np.float32),
         face=face,
         into=np.concatenate([ih, il]),
         back=np.concatenate([bh, bl]),
-        factors=factors.astype(np.float32).reshape(nx * pad, LANES),
+        back_faces=np.concatenate([gh, gl]),
         rim=rim.astype(np.float32),
         out=np.concatenate([np.ascontiguousarray(fh.T), np.ascontiguousarray(fl.T)], axis=1),
         out_ends=out_ends,
@@ -162,26 +160,12 @@
     return [wide[:, k * depth : (k + 1) * depth] for k in range(count)]
 
 
-def pack_kernel(
-    res_hbm, direction_hbm, mu_hbm, msk_hbm,
-    sx0, sx1, sy0, sy1, sz, masked_out, mask_out, d_out, mu_out,
-    res, direction, msk, arrived,
-):
-    size_x, size_y, size_z = res.shape
+def pack_kernel(masked, msk, direction, mu, sx0, sx1, sy0, sy1, sz, mask_out, d):
+    size_x, size_y, size_z = masked.shape
     even_x, even_y, even_z = (place(axis)[0] for axis in AXES)
-    copies = [
-        pltpu.make_async_copy(source, target, arrived.at[k])
-        for k, (source, target) in enumerate(
-            ((msk_hbm, msk), (res_hbm, res), (direction_hbm, direction), (mu_hbm, mu_out))
-        )
-    ]
-    for copy in copies:
-        copy.start()
-    for copy in copies:
-        copy.wait()
     mask = msk[...].astype(F32)
-    fields = (mask * res[...], mask, mask * direction[...], mu_out[...])
-    masked_out[...], mask_out[...], d_out[...] = fields[:3]
+    fields = (masked[...], mask, mask * direction[...], mu[...])
+    mask_out[...], d[...] = fields[1], fields[2]
     for f, field in enumerate(fields):
         low, high = field[0], field[size_x - 1]
         sx0[f] = jnp.where(even_x, high, low)
@@ -195,23 +179,25 @@
 
 def along_z(rows, fwd, size_z):
     high, low = halves(rows)
-    return dot(jnp.concatenate([high, low], axis=1), fwd[: 2 * size_z]) + dot(high, fwd[2 * size_z :])
-
-
-def own_kernel(masked, *refs):
-    count = (len(refs) - 2) // 2
-    tables, loaded, (work, arrived) = refs[:count], refs[count : 2 * count], refs[2 * count :]
-    copies = [pltpu.make_async_copy(s, t, arrived.at[k]) for k, (s, t) in enumerate(zip(tables, loaded))]
-    for copy in copies:
-        copy.start()
-    for copy in copies:
-        copy.wait()
+    table = fwd[:size_z]
+    return dot(jnp.concatenate([high, low], axis=1), jnp.concatenate([table, table], axis=0)) + dot(high, fwd[size_z:])
+
+
+def own_kernel(masked, mu, fwd, middle, work, factors, scale):
     size_x, size_y, size_z = masked.shape
-    work[...] = along_z(masked[...].reshape(size_x * size_y, size_z), loaded[0], size_z)
+    work[...] = along_z(masked[...].reshape(size_x * size_y, size_z), fwd, size_z)
+    pad = middle.shape[0]
+    along = middle[...]
+    previous = 1.0 / along
+    factors[0:pad] = previous
+    for i in range(1, size_x + 2):
+        previous = 1.0 / (along - previous)
+        factors[i * pad : (i + 1) * pad] = previous
+    scale[...] = jnp.full((8, size_z), (size_x * size_y * size_z) / jnp.sum(mu[...]))
 
 
 def solve_kernel(
-    work, mask, mu, rx0, rx1, ry0, ry1, rz, fwd, face_table, into, back, factors, rim, out, out_ends,
+    work, factors, scale, mask, rx0, rx1, ry0, ry1, rz, fwd, face_table, into, back, back_faces, rim, out, out_ends,
     own, tx0, tx1, ty0, ty1, tz,
 ):
     size_x, size_y, size_z = mask.shape
@@ -237,7 +223,7 @@
         part = slice(g * GROUP * size_y, (g + 1) * GROUP * size_y)
         modes.append(dot(into_h, box_h[part]) + dot(into_l, box_h[part]) + dot(into_h, box_l[part]))
     modes = jnp.concatenate(modes, axis=0)
-    rim_low, rim_high = rim[:, :LANES], rim[:, LANES:]
+    rim_low, rim_high = (jnp.broadcast_to(rim[:, k : k + 1], (pad, LANES)) for k in (0, 1))
     solved = []
     for i in range(nx):
         value = modes[i * pad : (i + 1) * pad]
@@ -251,20 +237,21 @@
         solved[i] = solved[i] + factors[i * pad : (i + 1) * pad] * solved[i + 1]
     solved = jnp.concatenate(solved, axis=0)
     high, low = halves(solved)
-    group_rows = GROUP * size_y + 2 * size_x
-    half = back.shape[0] // 2
+    own_rows, face_rows = GROUP * size_y, 2 * size_x
+    half = back_faces.shape[0] // 2
     local, y_faces = [], None
     for g in range(nx // GROUP):
         part = slice(g * GROUP * pad, (g + 1) * GROUP * pad)
-        table_h = back[g * group_rows : (g + 1) * group_rows, : GROUP * pad]
-        table_l = back[half + g * group_rows : half + (g + 1) * group_rows, : GROUP * pad]
+        line = slice(g * face_rows, (g + 1) * face_rows)
+        table_h = jnp.concatenate([back[:own_rows], back_faces[line]], axis=0)[:, : GROUP * pad]
+        line = slice(half + g * face_rows, half + (g + 1) * face_rows)
+        table_l = jnp.concatenate([back[own_rows:], back_faces[line]], axis=0)[:, : GROUP * pad]
         value = dot(table_h, high[part]) + dot(table_l, high[part]) + dot(table_h, low[part])
-        local.append(value[: GROUP * size_y])
-        rest = value[GROUP * size_y :]
+        local.append(value[:own_rows])
+        rest = value[own_rows:]
         y_faces = rest if y_faces is None else y_faces + rest
     local = jnp.concatenate(local + [y_faces], axis=0)
-    scale = (rows * size_z) / jnp.sum(mu[...])
-    local = local * scale
+    local = local * scale[0:1, 0:1]
     high, low = halves(local)
     both = dot(high, out[...])
     local = both[:, :size_z] + both[:, size_z:] + dot(low, out[:, :size_z])
@@ -416,15 +403,14 @@
     new_res[...] = res[...] - alpha3 * (az[...] + beta * ad[...]).reshape(box)
 
 
-def call(kernel, args, outs, specs=None, scratch=(), flops=0):
-    outs = [out if isinstance(out, jax.ShapeDtypeStruct) else jax.ShapeDtypeStruct(out, F32) for out in outs]
+def call(kernel, args, outs, specs=None):
+    outs = [jax.ShapeDtypeStruct(out, F32) for out in outs]
     return pl.pallas_call(
         kernel,
         out_shape=outs,
         in_specs=specs or [VMEM] * len(args),
         out_specs=[VMEM] * len(outs),
-        scratch_shapes=list(scratch),
-        cost_estimate=pl.CostEstimate(flops=flops, bytes_accessed=1 << 20, transcendentals=0),
+        cost_estimate=pl.CostEstimate(flops=0, bytes_accessed=1 << 20, transcendentals=0),
         compiler_params=pltpu.CompilerParams(vmem_limit_bytes=32 * 1024 * 1024),
     )(*args)
 
@@ -449,27 +435,19 @@
     def faces(count):
         return [(count, size_y, size_z)] * 2 + [(count, size_x, size_z)] * 2 + [(8, rows)]
 
-    tables = list(solve_tables(size_x, size_y, size_z).values())
+    fwd, middle, *tables = map(jnp.asarray, solve_tables(size_x, size_y, size_z).values())
+    with jax.named_scope("masks"):
+        masked = unfixed_node_mask.astype(F32) * residual
+        mu = permeability
     with jax.named_scope("pack"):
-        *sent, masked, mask, d, mu = call(
-            pack_kernel,
-            (residual, direction, permeability, unfixed_node_mask),
-            faces(4) + [box] * 4,
-            [HBM] * 4,
-            [pltpu.VMEM(box, F32), pltpu.VMEM(box, F32), pltpu.VMEM(box, jnp.int32), pltpu.SemaphoreType.DMA((4,))],
-        )
+        *sent, mask, d = call(pack_kernel, (masked, unfixed_node_mask, direction, mu), faces(4) + [box] * 2)
     with jax.named_scope("faces_in"):
         near = exchange(*sent)
     with jax.named_scope("own_part"):
-        *tables, work = call(
-            own_kernel,
-            (masked, *map(jnp.asarray, tables)),
-            [jax.ShapeDtypeStruct(t.shape, t.dtype) for t in tables] + [(rows, LANES)],
-            [VMEM] + [HBM] * len(tables),
-            [pltpu.SemaphoreType.DMA((len(tables),))],
-        )
+        modes = ((size_x + 2) * middle.shape[0], LANES)
+        part = call(own_kernel, (masked, mu, fwd, middle), [(rows, LANES), modes, (8, size_z)])
     with jax.named_scope("solve"):
-        own, *made = call(solve_kernel, (work, mask, mu, *near, *tables), [box] + faces(2))
+        own, *made = call(solve_kernel, (*part, mask, *near, fwd, *tables), [box] + faces(2))
     with jax.named_scope("faces_out"):
         got = exchange(*made)
     with jax.named_scope("links"):

time: 39.4 us -> 34 us (0.86)
  local copies, waits for them, and re-layouts: 7.63 us -> 0.15 us
  starting transfers between devices: 13.3 us -> 15.3 us
  Pallas kernels: 7.54 us -> 5.88 us
  other arithmetic: 0 us -> 1.14 us
  waiting for transfers between devices: 9.08 us -> 9.93 us
    unnamed x28, local copies, waits for them, and re-layouts: 7.63 us -> 0.15 us
    pallas_call x6, Pallas kernels: 7.54 us -> 5.88 us  [call(): pl.pallas_call(kernel, out_shape=outs, in_specs=specs or [VMEM] * len(arg...]
    mul x0 -> x1, other arithmetic: none -> 1.14 us  [shards(): masked = unfixed_node_mask.astype(F32) * residual]
    ppermute x10, starting transfers between devices: 10.6 us -> 11.6 us  [swap(): return lax.ppermute(block, AXES, swaps(axis, turn))]
    all_to_all x1, starting transfers between devices: 2.75 us -> 3.71 us  [shards(): sums = lax.all_to_all(sums, AXES, 0, 0, tiled=True)]
    ppermute x10, waiting for transfers between devices: 2.68 us -> 3.54 us  [swap(): return lax.ppermute(block, AXES, swaps(axis, turn))]
  transfers between devices with their start and end apart: 11 -> 11, of which waited for: 3 -> 3; matrix products, arithmetic and copies ran while one was open for 0% -> 0% of each run, Pallas kernels for 6% -> 3%
where the time goes in v3:
time: 34 us; the launch traced here: 33.9 us
  starting transfers between devices  15.3 us (45%)
  waiting for transfers between devices  9.93 us (29%)
  Pallas kernels  5.88 us (17%)
  between operations  1.47 us (4%)
  other arithmetic  1.14 us (3%)
    ppermute x10, starting transfers between devices, swap(): return lax.ppermute(block, AXES, swaps(axis, turn))  11.6 us
    all_to_all x1, waiting for transfers between devices, shards(): sums = lax.all_to_all(sums, AXES, 0, 0, tiled=True)  6.39 us
    pallas_call x6, Pallas kernels, call(): pl.pallas_call(kernel, out_shape=outs, in_specs=specs or [VMEM] * len(arg...  5.88 us
    all_to_all x1, starting transfers between devices, shards(): sums = lax.all_to_all(sums, AXES, 0, 0, tiled=True)  3.71 us
    ppermute x10, waiting for transfers between devices, swap(): return lax.ppermute(block, AXES, swaps(axis, turn))  3.54 us
    mul x1, other arithmetic, shards(): masked = unfixed_node_mask.astype(F32) * residual  1.14 us
  transfers between devices with their start and end apart: 11, of which 3 were waited for; matrix products, arithmetic and copies ran while one was open for 0% of the time, Pallas kernels for 3%

profile of v3, /device:TPU:0, one launch (start us, length us, event | category | flops | bytes accessed | tf_op | source)
XLA Modules:
  0.0 33.9 jit_solution(5281701826175895703)
XLA Ops:
  0.7 1.1 %convert_multiply_fusion.masked = f32[16,32,128]{2,1,0:T(8,128)S(1)} fusion(f32[16,32,128]{2,1,0:T(8,128)} %res.1, s32[16,32,128]{2,1,0:T(8,128)} %msk.1), kind=kLoop, calls=%fused_computation | loop fusion | flops 131072 | bytes 786432 | tf_op jit(solution)/shard_map/masks/mul | solution.py:440
  1.8 0.0 copy-done
  1.8 0.1 copy-done.4
  1.9 0.4 %pack.1 = (f32[4,32,128]{2,1,0:T(8,128)S(1)}, f32[4,32,128]{2,1,0:T(8,128)S(1)}, f32[4,16,128]{2,1,0:T(8,128)S(1)}, f32[4,16,128]{2,1,0:T(8,128)S(1)}, f32[8,512...) custom-call(f32[16,32,128]{2,1,0:T(8,128)S(1)} %convert_multiply_fusion.masked, ...), custom_call_target="tpu_custom_call" | custom-call | bytes 1048576 | tf_op jit(solution)/shard_map/pack/pallas_call | solution.py:408
  2.3 0.5 %collective-permute-start = (f32[4,32,128]{2,1,0:T(8,128)S(1)}, f32[4,32,128]{2,1,0:T(8,128)S(1)}, u32[]{:S(2)}, u32[]{:S(2)}) collective-permute-start(f32[4,32,128]{2,1,0:T(8,128)S(1)} %get-tuple-element.33), channel_id=1, source_target_pairs={{0,8},{1,9},{2,10},{3,11},{4,12},{5,13},{6,14},{7,15},{8,0},{9,1},... | collective-permute-start | bytes 196616 | tf_op jit(solution)/shard_map/faces_in/ppermute | solution.py:38
  2.8 2.6 %collective-permute-start.1 = (f32[4,32,128]{2,1,0:T(8,128)S(1)}, f32[4,32,128]{2,1,0:T(8,128)S(1)}, u32[]{:S(2)}, u32[]{:S(2)}) collective-permute-start(f32[4,32,128]{2,1,0:T(8,128)S(1)} %get-tuple-element.34), channel_id=1, source_target_pairs={{0,24},{1,25},{2,26},{3,27},{4,28},{5,29},{6,30},{7,31},{8,16},{9,... | collective-permute-start | bytes 196616 | tf_op jit(solution)/shard_map/faces_in/ppermute | solution.py:38
  5.4 1.6 %collective-permute-start.2 = (f32[4,16,128]{2,1,0:T(8,128)S(1)}, f32[4,16,128]{2,1,0:T(8,128)S(1)}, u32[]{:S(2)}, u32[]{:S(2)}) collective-permute-start(f32[4,16,128]{2,1,0:T(8,128)S(1)} %get-tuple-element.35), channel_id=1, source_target_pairs={{0,2},{1,3},{2,0},{3,1},{4,6},{5,7},{6,4},{7,5},{8,10},{9,11},{10,... | collective-permute-start | bytes 98312 | tf_op jit(solution)/shard_map/faces_in/ppermute | solution.py:38
  6.9 0.0 collective-permute-start.3
  6.9 0.0 copy-start.9
  7.0 1.6 %collective-permute-start.4 = (f32[8,512]{1,0:T(8,128)S(1)}, f32[8,512]{1,0:T(8,128)S(1)}, u32[]{:S(2)}, u32[]{:S(2)}) collective-permute-start(f32[8,512]{1,0:T(8,128)S(1)} %get-tuple-element.37), channel_id=1, source_target_pairs={{0,1},{1,0},{2,3},{3,2},{4,5},{5,4},{6,7},{7,6},{8,9},{9,8},{10,11... | collective-permute-start | bytes 49160 | tf_op jit(solution)/shard_map/faces_in/ppermute | solution.py:38
  8.6 0.3 own_part.1
  8.9 1.9 %collective-permute-done.4.rz = f32[8,512]{1,0:T(8,128)S(1)} collective-permute-done((f32[8,512]{1,0:T(8,128)S(1)}, f32[8,512]{1,0:T(8,128)S(1)}, u32[]{:S(2)}, u32[]{:S(2)}) %collective-permute-start.4) | collective-permute-done | bytes 16416 | tf_op jit(solution)/shard_map/faces_in/ppermute | solution.py:38
  10.8 0.0 collective-permute-done.2.ry0
  10.8 0.0 collective-permute-done.3.ry1
  10.8 0.0 collective-permute-done.rx0
  10.8 0.0 collective-permute-done.1.rx1
  10.9 2.0 %solve.1 = (f32[16,32,128]{2,1,0:T(8,128)S(1)}, f32[2,32,128]{2,1,0:T(8,128)S(1)}, f32[2,32,128]{2,1,0:T(8,128)S(1)}, f32[2,16,128]{2,1,0:T(8,128)S(1)}, f32[2,1...) custom-call(f32[512,256]{1,0:T(8,128)S(1)} %get-tuple-element.30.work, f32[720,256]{1,0:T(8,128)S(1)} %get-tuple-element.31.factors, ...), custom_call_target="tpu_custom_call" | custom-call | bytes 1048576 | tf_op jit(solution)/shard_map/solve/pallas_call | solution.py:408
  12.9 0.0 collective-permute-start.5
  12.9 0.7 %collective-permute-start.6 = (f32[2,32,128]{2,1,0:T(8,128)S(1)}, f32[2,32,128]{2,1,0:T(8,128)S(1)}, u32[]{:S(2)}, u32[]{:S(2)}) collective-permute-start(f32[2,32,128]{2,1,0:T(8,128)S(1)} %get-tuple-element.40.tx1), channel_id=1, source_target_pairs={{0,24},{1,25},{2,26},{3,27},{4,28},{5,29},{6,30},{7,31},{8,16},{9,... | collective-permute-start | bytes 98312 | tf_op jit(solution)/shard_map/faces_out/ppermute | solution.py:38
  13.6 3.1 %collective-permute-start.7 = (f32[2,16,128]{2,1,0:T(8,128)S(1)}, f32[2,16,128]{2,1,0:T(8,128)S(1)}, u32[]{:S(2)}, u32[]{:S(2)}) collective-permute-start(f32[2,16,128]{2,1,0:T(8,128)S(1)} %get-tuple-element.41.ty0), channel_id=1, source_target_pairs={{0,2},{1,3},{2,0},{3,1},{4,6},{5,7},{6,4},{7,5},{8,10},{9,11},{10,... | collective-permute-start | bytes 49160 | tf_op jit(solution)/shard_map/faces_out/ppermute | solution.py:38
  16.7 0.0 collective-permute-start.8
  16.7 1.5 %collective-permute-start.9 = (f32[8,512]{1,0:T(8,128)S(1)}, f32[8,512]{1,0:T(8,128)S(1)}, u32[]{:S(2)}, u32[]{:S(2)}) collective-permute-start(f32[8,512]{1,0:T(8,128)S(1)} %get-tuple-element.43.tz), channel_id=1, source_target_pairs={{0,1},{1,0},{2,3},{3,2},{4,5},{5,4},{6,7},{7,6},{8,9},{9,8},{10,11... | collective-permute-start | bytes 49160 | tf_op jit(solution)/shard_map/faces_out/ppermute | solution.py:38
  18.2 0.6 %links.1 = (f32[512,128]{1,0:T(8,128)S(1)}, f32[17,32,128]{2,1,0:T(8,128)S(1)}, f32[512,128]{1,0:T(8,128)S(1)}, f32[512,128]{1,0:T(8,128)S(1)}, f32[512,128]{1,0:T(8,128)S(1)}, /*index=5*/f32[512,128]{1,0:T(8,128)S(1)}) custom-call(f32[16,32,128]{2,1,0:T(8,128)S(1)} %get-tuple-element.28.mask, f32[16,32,128]{2,1,0:T(8,128)S(1)} %get-tuple-element.29.d, ...), custom_call_target="tpu_custom_call" | custom-call | bytes 1048576 | tf_op jit(solution)/shard_map/links/pallas_call | solution.py:408
  18.8 0.0 collective-permute-done.8.qy1
  18.8 1.6 %collective-permute-done.9.qz = f32[8,512]{1,0:T(8,128)S(1)} collective-permute-done((f32[8,512]{1,0:T(8,128)S(1)}, f32[8,512]{1,0:T(8,128)S(1)}, u32[]{:S(2)}, u32[]{:S(2)}) %collective-permute-start.9) | collective-permute-done | bytes 16416 | tf_op jit(solution)/shard_map/faces_out/ppermute | solution.py:38
  20.5 0.0 collective-permute-done.5.qx0
  20.5 0.0 collective-permute-done.6.qx1
  20.5 0.0 copy-start.5
  20.5 1.3 %image.1 = (f32[512,128]{1,0:T(8,128)S(1)}, f32[512,128]{1,0:T(8,128)S(1)}, f32[32,1,128]{2,1,0:T(1,128)}) custom-call(f32[16,32,128]{2,1,0:T(8,128)S(1)} %convert_multiply_fusion.masked, f32[16,32,128]{2,1,0:T(8,128)S(1)} %get-tuple-element.28.mask, f32[16,32,128]{2,1,0:T(8,128)S(1)} %get-tuple-element.29.d, f32[16,32,128]{2,1,0:T(8,128)S(1)} %get-tuple-element.38.own, ...), custom_call_target="tpu_custom_call" | custom-call | bytes 1048576 | tf_op jit(solution)/shard_map/image/pallas_call | solution.py:408
  21.8 3.7 %all-to-all-start = ((f32[32,1,128]{2,1,0:T(1,128)}), f32[32,1,128]{2,1,0:T(1,128)S(1)}, u32[]{:S(2)}, u32[]{:S(2)}) async-start(f32[32,1,128]{2,1,0:T(1,128)} %get-tuple-element.50), calls=%async_computation | async-start | bytes 32768 | tf_op jit(solution)/shard_map/sums/all_to_all | solution.py:462
  26.1 6.4 %all-to-all-done.sums = f32[32,1,128]{2,1,0:T(1,128)S(1)} async-done(((f32[32,1,128]{2,1,0:T(1,128)}), f32[32,1,128]{2,1,0:T(1,128)S(1)}, u32[]{:S(2)}, u32[]{:S(2)}) %all-to-all-start) | async-done | bytes 16416 | tf_op jit(solution)/shard_map/sums/all_to_all | solution.py:462
  32.5 1.3 %update.1 = (f32[16,32,128]{2,1,0:T(8,128)}, f32[16,32,128]{2,1,0:T(8,128)}, f32[16,32,128]{2,1,0:T(8,128)}) custom-call(f32[1]{0:T(128)S(6)} %copy.18.rz_prev, f32[32,1,128]{2,1,0:T(1,128)S(1)} %all-to-all-done.sums, f32[16,32,128]{2,1,0:T(8,128)S(1)} %copy-done.5, f32[16,32,128]{2,1,0:T(8,128)S(1)} %copy-done.2, f32[16,32,128]{2,1,0:T(8,128)S(1)} %get-tuple-element.29.d, ...), custom_call_target="tpu_custom_call" | custom-call | bytes 1048576 | tf_op jit(solution)/shard_map/update/pallas_call | solution.py:408
  (25 shorter events, 0.0 us)
Async XLA Ops:
  0.6 1.2 %copy-start.1 = (s32[16,32,128]{2,1,0:T(8,128)S(1)}, s32[16,32,128]{2,1,0:T(8,128)}, u32[]{:S(2)}) copy-start(s32[16,32,128]{2,1,0:T(8,128)} %msk.1) | copy-start | bytes 786436
  0.6 1.2 %copy-start = (f32[16,32,128]{2,1,0:T(8,128)S(1)}, f32[16,32,128]{2,1,0:T(8,128)}, u32[]{:S(2)}) copy-start(f32[16,32,128]{2,1,0:T(8,128)} %mu.5) | copy-start | bytes 786436
  0.7 1.2 %copy-start.4 = (f32[16,32,128]{2,1,0:T(8,128)S(1)}, f32[16,32,128]{2,1,0:T(8,128)}, u32[]{:S(2)}) copy-start(f32[16,32,128]{2,1,0:T(8,128)} %direction.1) | copy-start | bytes 786436
  1.9 6.6 %copy-start.3 = (bf16[256,256]{1,0:T(8,128)(2,1)S(1)}, bf16[256,256]{1,0:T(8,128)(2,1)}, u32[]{:S(2)}) copy-start(bf16[256,256]{1,0:T(8,128)(2,1)} %constant.18.clone.fwd) | copy-start | bytes 393220
  1.9 6.6 %copy-start.10 = (f32[40,256]{1,0:T(8,128)S(1)}, f32[40,256]{1,0:T(8,128)}, u32[]{:S(2)}) copy-start(f32[40,256]{1,0:T(8,128)} %constant.19.clone.middle) | copy-start | bytes 122884
  1.9 8.9 %copy-start.12 = (bf16[32,256]{1,0:T(8,128)(2,1)S(1)}, bf16[32,256]{1,0:T(8,128)(2,1)}, u32[]{:S(2)}) copy-start(bf16[32,256]{1,0:T(8,128)(2,1)} %constant.26.clone.out_ends) | copy-start | bytes 49156
  2.3 8.5 %collective-permute-start = (f32[4,32,128]{2,1,0:T(8,128)S(1)}, f32[4,32,128]{2,1,0:T(8,128)S(1)}, u32[]{:S(2)}, u32[]{:S(2)}) collective-permute-start(f32[4,32,128]{2,1,0:T(8,128)S(1)} %get-tuple-element.33), channel_id=1, source_target_pairs={{0,8},{1,9},{2,10},{3,11},{4,12},{5,13},{6,14},{7,15},{8,0},{9,1},... | collective-permute-start | bytes 196616 | tf_op jit(solution)/shard_map/faces_in/ppermute | solution.py:38
  2.8 8.0 %collective-permute-start.1 = (f32[4,32,128]{2,1,0:T(8,128)S(1)}, f32[4,32,128]{2,1,0:T(8,128)S(1)}, u32[]{:S(2)}, u32[]{:S(2)}) collective-permute-start(f32[4,32,128]{2,1,0:T(8,128)S(1)} %get-tuple-element.34), channel_id=1, source_target_pairs={{0,24},{1,25},{2,26},{3,27},{4,28},{5,29},{6,30},{7,31},{8,16},{9,... | collective-permute-start | bytes 196616 | tf_op jit(solution)/shard_map/faces_in/ppermute | solution.py:38
  5.4 5.4 %collective-permute-start.2 = (f32[4,16,128]{2,1,0:T(8,128)S(1)}, f32[4,16,128]{2,1,0:T(8,128)S(1)}, u32[]{:S(2)}, u32[]{:S(2)}) collective-permute-start(f32[4,16,128]{2,1,0:T(8,128)S(1)} %get-tuple-element.35), channel_id=1, source_target_pairs={{0,2},{1,3},{2,0},{3,1},{4,6},{5,7},{6,4},{7,5},{8,10},{9,11},{10,... | collective-permute-start | bytes 98312 | tf_op jit(solution)/shard_map/faces_in/ppermute | solution.py:38
  6.9 3.8 %collective-permute-start.3 = (f32[4,16,128]{2,1,0:T(8,128)S(1)}, f32[4,16,128]{2,1,0:T(8,128)S(1)}, u32[]{:S(2)}, u32[]{:S(2)}) collective-permute-start(f32[4,16,128]{2,1,0:T(8,128)S(1)} %get-tuple-element.36), channel_id=1, source_target_pairs={{0,8},{1,9},{2,4},{3,5},{4,2},{5,3},{6,14},{7,15},{8,0},{9,1},{10,... | collective-permute-start | bytes 98312 | tf_op jit(solution)/shard_map/faces_in/ppermute | solution.py:38
  6.9 3.9 %copy-start.6 = (bf16[480,256]{1,0:T(8,128)(2,1)S(1)}, bf16[480,256]{1,0:T(8,128)(2,1)}, u32[]{:S(2)}) copy-start(bf16[480,256]{1,0:T(8,128)(2,1)} %constant.21.clone.into) | copy-start | bytes 737284
  6.9 3.9 %copy-start.7 = (bf16[384,256]{1,0:T(8,128)(2,1)S(1)}, bf16[384,256]{1,0:T(8,128)(2,1)}, u32[]{:S(2)}) copy-start(bf16[384,256]{1,0:T(8,128)(2,1)} %constant.22.clone.back) | copy-start | bytes 589828
  6.9 3.9 %copy-start.8 = (bf16[256,256]{1,0:T(8,128)(2,1)S(1)}, bf16[256,256]{1,0:T(8,128)(2,1)}, u32[]{:S(2)}) copy-start(bf16[256,256]{1,0:T(8,128)(2,1)} %constant.25.clone.out) | copy-start | bytes 393220
  6.9 3.9 %copy-start.9 = (bf16[192,256]{1,0:T(8,128)(2,1)S(1)}, bf16[192,256]{1,0:T(8,128)(2,1)}, u32[]{:S(2)}) copy-start(bf16[192,256]{1,0:T(8,128)(2,1)} %constant.23.clone.back_faces) | copy-start | bytes 294916
  7.0 3.8 %collective-permute-start.4 = (f32[8,512]{1,0:T(8,128)S(1)}, f32[8,512]{1,0:T(8,128)S(1)}, u32[]{:S(2)}, u32[]{:S(2)}) collective-permute-start(f32[8,512]{1,0:T(8,128)S(1)} %get-tuple-element.37), channel_id=1, source_target_pairs={{0,1},{1,0},{2,3},{3,2},{4,5},{5,4},{6,7},{7,6},{8,9},{9,8},{10,11... | collective-permute-start | bytes 49160 | tf_op jit(solution)/shard_map/faces_in/ppermute | solution.py:38
  8.6 2.3 %copy-start.11 = (f32[40,128]{1,0:T(8,128)S(1)}, f32[40,128]{1,0:T(8,128)}, u32[]{:S(2)}) copy-start(f32[40,128]{1,0:T(8,128)} %constant.24.clone.rim) | copy-start | bytes 61444
  8.6 2.3 %copy-start.13 = (bf16[16,256]{1,0:T(8,128)(2,1)S(1)}, bf16[16,256]{1,0:T(8,128)(2,1)}, u32[]{:S(2)}) copy-start(bf16[16,256]{1,0:T(8,128)(2,1)} %constant.20.clone.face_table) | copy-start | bytes 24580
  12.9 7.6 %collective-permute-start.5 = (f32[2,32,128]{2,1,0:T(8,128)S(1)}, f32[2,32,128]{2,1,0:T(8,128)S(1)}, u32[]{:S(2)}, u32[]{:S(2)}) collective-permute-start(f32[2,32,128]{2,1,0:T(8,128)S(1)} %get-tuple-element.39.tx0), channel_id=1, source_target_pairs={{0,8},{1,9},{2,10},{3,11},{4,12},{5,13},{6,14},{7,15},{8,0},{9,1},... | collective-permute-start | bytes 98312 | tf_op jit(solution)/shard_map/faces_out/ppermute | solution.py:38
  12.9 7.5 %collective-permute-start.6 = (f32[2,32,128]{2,1,0:T(8,128)S(1)}, f32[2,32,128]{2,1,0:T(8,128)S(1)}, u32[]{:S(2)}, u32[]{:S(2)}) collective-permute-start(f32[2,32,128]{2,1,0:T(8,128)S(1)} %get-tuple-element.40.tx1), channel_id=1, source_target_pairs={{0,24},{1,25},{2,26},{3,27},{4,28},{5,29},{6,30},{7,31},{8,16},{9,... | collective-permute-start | bytes 98312 | tf_op jit(solution)/shard_map/faces_out/ppermute | solution.py:38
  13.6 5.2 %collective-permute-start.7 = (f32[2,16,128]{2,1,0:T(8,128)S(1)}, f32[2,16,128]{2,1,0:T(8,128)S(1)}, u32[]{:S(2)}, u32[]{:S(2)}) collective-permute-start(f32[2,16,128]{2,1,0:T(8,128)S(1)} %get-tuple-element.41.ty0), channel_id=1, source_target_pairs={{0,2},{1,3},{2,0},{3,1},{4,6},{5,7},{6,4},{7,5},{8,10},{9,11},{10,... | collective-permute-start | bytes 49160 | tf_op jit(solution)/shard_map/faces_out/ppermute | solution.py:38
  16.7 2.1 %collective-permute-start.8 = (f32[2,16,128]{2,1,0:T(8,128)S(1)}, f32[2,16,128]{2,1,0:T(8,128)S(1)}, u32[]{:S(2)}, u32[]{:S(2)}) collective-permute-start(f32[2,16,128]{2,1,0:T(8,128)S(1)} %get-tuple-element.42.ty1), channel_id=1, source_target_pairs={{0,8},{1,9},{2,4},{3,5},{4,2},{5,3},{6,14},{7,15},{8,0},{9,1},{10,... | collective-permute-start | bytes 49160 | tf_op jit(solution)/shard_map/faces_out/ppermute | solution.py:38
  16.7 3.7 %collective-permute-start.9 = (f32[8,512]{1,0:T(8,128)S(1)}, f32[8,512]{1,0:T(8,128)S(1)}, u32[]{:S(2)}, u32[]{:S(2)}) collective-permute-start(f32[8,512]{1,0:T(8,128)S(1)} %get-tuple-element.43.tz), channel_id=1, source_target_pairs={{0,1},{1,0},{2,3},{3,2},{4,5},{5,4},{6,7},{7,6},{8,9},{9,8},{10,11... | collective-permute-start | bytes 49160 | tf_op jit(solution)/shard_map/faces_out/ppermute | solution.py:38
  20.5 12.1 %copy-start.2 = (f32[16,32,128]{2,1,0:T(8,128)S(1)}, f32[16,32,128]{2,1,0:T(8,128)}, u32[]{:S(2)}) copy-start(f32[16,32,128]{2,1,0:T(8,128)} %res.1) | copy-start | bytes 786436
  20.5 12.1 %copy-start.5 = (f32[16,32,128]{2,1,0:T(8,128)S(1)}, f32[16,32,128]{2,1,0:T(8,128)}, u32[]{:S(2)}) copy-start(f32[16,32,128]{2,1,0:T(8,128)} %iterate.1) | copy-start | bytes 786436
  21.8 10.8 %all-to-all-start = ((f32[32,1,128]{2,1,0:T(1,128)}), f32[32,1,128]{2,1,0:T(1,128)S(1)}, u32[]{:S(2)}, u32[]{:S(2)}) async-start(f32[32,1,128]{2,1,0:T(1,128)} %get-tuple-element.50), calls=%async_computation | async-start | bytes 32768 | tf_op jit(solution)/shard_map/sums/all_to_all | solution.py:462

commit v4 on v3

--- a/solution.py
+++ b/solution.py
@@ -294,122 +294,130 @@
     tz[...] = jnp.where(iota((8, rows), 0) == 1, jnp.broadcast_to(ghost, (8, rows)), mine)
 
 
-def beside(value, y_sides, face, box):
+def stencil(slabs, y_low, y_high, faces, links, box):
     size_x, size_y, size_z = box
-    rows = size_x * size_y
-
-    def wide(side):
-        return jnp.broadcast_to(side[:, None, :], box).reshape(rows, size_z)
-
-    at = iota((rows, size_z), 0) % size_y
-    next_y = jnp.where(at == size_y - 1, wide(y_sides[1]), pltpu.roll(value, rows - 1, 0))
-    at = iota((rows, size_z), 1)
-    next_z = jnp.where(at == size_z - 1, face, pltpu.roll(value, size_z - 1, 1))
-    return next_y, next_z, wide(y_sides[0])
-
-
-def flux(value, x_sides, y_sides, face, wx, wy, wy0, wz, wz0, box):
-    size_x, size_y, size_z = box
-    rows = size_x * size_y
-    ext = jnp.concatenate([x_sides[0][None], value.reshape(box), x_sides[1][None]], axis=0)
-    flow = wx * (ext[1:] - ext[:-1])
-    total = (flow[:-1] - flow[1:]).reshape(rows, size_z)
-    next_y, next_z, before_y = beside(value, y_sides, face, box)
-    flow = wy * (next_y - value)
-    at = iota((rows, size_z), 0) % size_y
-    first = wy0 * (value - before_y)
-    total = total + jnp.where(at == 0, first, pltpu.roll(flow, 1, 0)) - flow
-    flow = wz * (next_z - value)
-    first = wz0 * (value - face)
-    at = iota((rows, size_z), 1)
-    return total + jnp.where(at == 0, first, pltpu.roll(flow, 1, 1)) - flow
+    wx, wy, wy0, wz, wz0 = links
+    row, lane = iota((size_y, size_z), 0), iota((size_y, size_z), 1)
+    below = wx[0] * (slabs[1] - slabs[0])
+    for i in range(size_x):
+        value, face = slabs[i + 1], faces(i)
+        above = wx[i + 1] * (slabs[i + 2] - value)
+        total = below - above
+        below = above
+        flow = wy[i] * (jnp.where(row == size_y - 1, y_high[i : i + 1], pltpu.roll(value, size_y - 1, 0)) - value)
+        first = wy0[i : i + 1] * (value - y_low[i : i + 1])
+        total = total + (jnp.where(row == 0, first, pltpu.roll(flow, 1, 0)) - flow)
+        flow = wz[i] * (jnp.where(lane == size_z - 1, face, pltpu.roll(value, size_z - 1, 1)) - value)
+        first = wz0[i] * (value - face)
+        yield i, total + (jnp.where(lane == 0, first, pltpu.roll(flow, 1, 1)) - flow)
 
 
 def links_kernel(
-    mask, d, mu, rx0, rx1, ry0, ry1, rz,
-    ad_out, wx_out, wy_out, wy0_out, wz_out, wz0_out,
+    rz_prev, mask, d, mu, rx0, rx1, ry0, ry1, rz,
+    ad_out, wx, wy, wy0, wz, wz0, dad, rz_line,
 ):
     box = mask.shape
     size_x, size_y, size_z = box
-    rows = size_x * size_y
     where_x, where_y, where_z = (place(axis) for axis in AXES)
     x_near = sides(rx0[2:4], rx1[2:4], where_x)
     y_near = sides(ry0[2:4], ry1[2:4], where_y)
-    d_face, mu_face = lane_ends([rz[2:3], rz[3:4]], where_z[0], size_z)
-    mu_own = mu[...].reshape(rows, size_z)
-    ext = jnp.concatenate([x_near[0][1][None], mu[...], x_near[1][1][None]], axis=0)
-    wx = 0.5 * (ext[1:] + ext[:-1])
-    next_y, next_z, before_y = beside(mu_own, [v[1] for v in y_near], mu_face, box)
-    wy, wy0 = 0.5 * (mu_own + next_y), 0.5 * (mu_own + before_y)
-    wz, wz0 = 0.5 * (mu_own + next_z), 0.5 * (mu_own + mu_face)
-    links = (wx, wy, wy0, wz, wz0)
-    wx_out[...], wy_out[...], wy0_out[...], wz_out[...], wz0_out[...] = links
-    value = d[...].reshape(rows, size_z)
-    ad = flux(value, [v[0] for v in x_near], [v[0] for v in y_near], d_face, *links, box)
-    ad_out[...] = mask[...].reshape(rows, size_z) * ad
+    d_face, mu_face = (
+        wide.reshape(box) for wide in lane_ends([rz[2:3], rz[3:4]], where_z[0], size_z)
+    )
+    row, lane = iota((size_y, size_z), 0), iota((size_y, size_z), 1)
+    slabs = [x_near[0][1]] + [mu[i] for i in range(size_x)] + [x_near[1][1]]
+    wx[0] = 0.5 * (slabs[0] + slabs[1])
+    mu_low, mu_high = y_near[0][1], y_near[1][1]
+    for i in range(size_x):
+        value, face = slabs[i + 1], mu_face[i]
+        wx[i + 1] = 0.5 * (value + slabs[i + 2])
+        wy[i] = 0.5 * (value + jnp.where(row == size_y - 1, mu_high[i : i + 1], pltpu.roll(value, size_y - 1, 0)))
+        wy0[i : i + 1] = 0.5 * (value[0:1] + mu_low[i : i + 1])
+        wz[i] = 0.5 * (value + jnp.where(lane == size_z - 1, face, pltpu.roll(value, size_z - 1, 1)))
+        wz0[i] = 0.5 * (value + face)
+    slabs = [x_near[0][0]] + [d[i] for i in range(size_x)] + [x_near[1][0]]
+    total = jnp.zeros((size_y, size_z), F32)
+    for i, image in stencil(slabs, y_near[0][0], y_near[1][0], lambda i: d_face[i], (wx, wy, wy0, wz, wz0), box):
+        image = mask[i] * image
+        ad_out[i] = image
+        total = total + slabs[i + 1] * image
+    dad[...] = jnp.sum(total, axis=0, keepdims=True)
+    rz_line[...] = jnp.full(rz_line.shape, rz_prev[0])
 
 
 def image_kernel(
-    masked, mask, d, own, tx0, tx1, ty0, ty1, tz, qx0, qx1, qy0, qy1, qz, ad_in, wx, wy, wy0, wz, wz0,
+    masked, mask, d, own, tx0, tx1, ty0, ty1, tz, qx0, qx1, qy0, qy1, qz, ad, wx, wy, wy0, wz, wz0, dad,
     z_out, az_out, sums,
 ):
     box = mask.shape
     size_x, size_y, size_z = box
-    rows = size_x * size_y
     where_x, where_y, where_z = (place(axis) for axis in AXES)
-    x_sent = sides(tx0[1:2], tx1[1:2], where_x)
-    y_sent = sides(ty0[1:2], ty1[1:2], where_y)
+    x_sent = sides(tx0[1], tx1[1], where_x)
+    y_sent = sides(ty0[1], ty1[1], where_y)
     x_got = sides(qx0[...], qx1[...], where_x)
     y_got = sides(qy0[...], qy1[...], where_y)
-    z_face, z_more = lane_ends([qz[0:1] + tz[1:2], qz[1:2]], where_z[0], size_z)
-    own_box = own[...]
-    z = jnp.concatenate(
-        [own_box[:1] + x_got[0][1][None], own_box[1:-1], own_box[-1:] + x_got[1][1][None]], axis=0
+    face, more = (
+        wide.reshape(box) for wide in lane_ends([qz[0:1] + tz[1:2], qz[1:2]], where_z[0], size_z)
     )
-    at = iota(box, 1)
-    z = z + jnp.where(at == 0, y_got[0][1][:, None, :], 0.0) + jnp.where(at == size_y - 1, y_got[1][1][:, None, :], 0.0)
-    z = z.reshape(rows, size_z) + z_more
-    z = z * mask[...].reshape(rows, size_z)
-    x_sides = [x_got[s][0] + x_sent[s][0] for s in (0, 1)]
-    y_sides = [y_got[s][0] + y_sent[s][0] for s in (0, 1)]
-    az = flux(z, x_sides, y_sides, z_face, wx[...], wy[...], wy0[...], wz[...], wz0[...], box)
-    az = mask[...].reshape(rows, size_z) * az
-    z_out[...] = z
-    az_out[...] = az
-    ad, value = ad_in[...], d[...].reshape(rows, size_z)
-    parts = (
-        jnp.sum(masked[...].reshape(rows, size_z) * z),
-        jnp.sum(z * az),
-        jnp.sum(z * ad + value * az),
-        jnp.sum(value * ad),
-    )
+    row = iota((size_y, size_z), 0)
+    slabs = [x_got[0][0] + x_sent[0]]
+    for i in range(size_x):
+        value = own[i] + more[i]
+        value = value + jnp.where(row == 0, y_got[0][1][i : i + 1], 0.0)
+        value = value + jnp.where(row == size_y - 1, y_got[1][1][i : i + 1], 0.0)
+        if i == 0:
+            value = value + x_got[0][1]
+        if i == size_x - 1:
+            value = value + x_got[1][1]
+        z_out[i] = value
+        slabs.append(value)
+    slabs.append(x_got[1][0] + x_sent[1])
+    y_sides = [y_got[s][0] + y_sent[s] for s in (0, 1)]
+    rz = zaz = zad = jnp.zeros((size_y, size_z), F32)
+    for i, image in stencil(slabs, *y_sides, lambda i: face[i], (wx, wy, wy0, wz, wz0), box):
+        value = slabs[i + 1]
+        image = mask[i] * image
+        az_out[i] = image
+        rz = rz + masked[i] * value
+        zaz = zaz + value * image
+        zad = zad + (value * ad[i] + d[i] * image)
     at = iota(sums.shape, 2)
     line = jnp.zeros(sums.shape, F32)
-    for k, part in enumerate(parts):
-        line = jnp.where(at == k, part, line)
+    for k, part in enumerate((rz, zaz, zad, dad[...])):
+        line = jnp.where(at == k, jnp.sum(part), line)
     sums[...] = line
 
 
-def update_kernel(rz_prev, sums, iterate, res, d, z, az, ad, new_iterate, new_res, new_direction):
+def update_kernel(
+    rz_line, sums, iterate, res, d, z, az, ad, new_iterate, new_res, new_direction, out_iterate, out_res, out_p, gone,
+):
     line = jnp.sum(sums[...], axis=0)
     rz, zaz, zad, dad = (line[:, k : k + 1] for k in range(4))
-    beta = rz / rz_prev[0]
+    beta = rz / rz_line[:, 0:1]
     alpha = rz / (zaz + beta * (zad + beta * dad))
-    alpha3, beta3 = (v.reshape(1, 1, 1) for v in (alpha, beta))
-    box = d.shape
-    p = z[...].reshape(box) + beta3 * d[...]
-    new_direction[...] = p
-    new_iterate[...] = iterate[...] + alpha3 * p
-    new_res[...] = res[...] - alpha3 * (az[...] + beta * ad[...]).reshape(box)
-
-
-def call(kernel, args, outs, specs=None):
+    alpha, beta = (v.reshape(1, 1, 1) for v in (alpha, beta))
+    p = z[...] + beta * d[...]
+    out_p[...] = p
+    copies = [pltpu.make_async_copy(out_p, new_direction, gone.at[0])]
+    copies[0].start()
+    out_iterate[...] = iterate[...] + alpha * p
+    copies.append(pltpu.make_async_copy(out_iterate, new_iterate, gone.at[1]))
+    copies[1].start()
+    out_res[...] = res[...] - alpha * (az[...] + beta * ad[...])
+    copies.append(pltpu.make_async_copy(out_res, new_res, gone.at[2]))
+    copies[2].start()
+    for copy in copies:
+        copy.wait()
+
+
+def call(kernel, args, outs, specs=None, out_spec=VMEM, scratch=()):
     outs = [jax.ShapeDtypeStruct(out, F32) for out in outs]
     return pl.pallas_call(
         kernel,
         out_shape=outs,
         in_specs=specs or [VMEM] * len(args),
-        out_specs=[VMEM] * len(outs),
+        out_specs=[out_spec] * len(outs),
+        scratch_shapes=list(scratch),
         cost_estimate=pl.CostEstimate(flops=0, bytes_accessed=1 << 20, transcendentals=0),
         compiler_params=pltpu.CompilerParams(vmem_limit_bytes=32 * 1024 * 1024),
     )(*args)
@@ -451,18 +459,16 @@
     with jax.named_scope("faces_out"):
         got = exchange(*made)
     with jax.named_scope("links"):
-        ad, *links = call(
-            links_kernel, (mask, d, mu, *near), [flat, (size_x + 1, size_y, size_z), flat, flat, flat, flat]
-        )
+        outs = [box, (size_x + 1, size_y, size_z), box, (size_x, size_z), box, box, (1, size_z), (1, size_z)]
+        ad, *links, rz_line = call(links_kernel, (rz_prev, mask, d, mu, *near), outs, [SMEM] + [VMEM] * 8)
     with jax.named_scope("image"):
-        z, az, sums = call(
-            image_kernel, (masked, mask, d, own, *made, *got, ad, *links), [flat, flat, (devices, 1, 128)]
-        )
+        z, az, sums = call(image_kernel, (masked, mask, d, own, *made, *got, ad, *links), [box, box, (devices, 1, 128)])
     with jax.named_scope("sums"):
         sums = lax.all_to_all(sums, AXES, 0, 0, tiled=True)
     with jax.named_scope("update"):
-        args = (rz_prev, sums, iterate, residual, d, z, az, ad)
-        return tuple(call(update_kernel, args, [box] * 3, [SMEM] + [VMEM] * 7))
+        args = (rz_line, sums, iterate, residual, d, z, az, ad)
+        scratch = [pltpu.VMEM(box, F32)] * 3 + [pltpu.SemaphoreType.DMA((3,))]
+        return tuple(call(update_kernel, args, [box] * 3, None, pl.BlockSpec(memory_space=pl.ANY), scratch))
 
 
 def solution(mesh):

time: 34 us -> 33.3 us (0.979)
  blocking collectives: 0 us -> 10.6 us
  waiting for transfers between devices: 9.93 us -> 2.89 us
  starting transfers between devices: 15.3 us -> 11.6 us
  Pallas kernels: 5.88 us -> 5.27 us
    all_to_all x0 -> x1, blocking collectives: none -> 10.6 us  [shards(): sums = lax.all_to_all(sums, AXES, 0, 0, tiled=True)]
    all_to_all x1 -> x0, waiting for transfers between devices: 6.39 us -> none  [shards(): sums = lax.all_to_all(sums, AXES, 0, 0, tiled=True)]
    all_to_all x1 -> x0, starting transfers between devices: 3.71 us -> none  [shards(): sums = lax.all_to_all(sums, AXES, 0, 0, tiled=True)]
    ppermute x10, waiting for transfers between devices: 3.54 us -> 2.89 us  [swap(): return lax.ppermute(block, AXES, swaps(axis, turn))]
    pallas_call x6, Pallas kernels: 5.88 us -> 5.27 us  [call(): pl.pallas_call(kernel, out_shape=outs, in_specs=specs or [VMEM] * len(arg...]
  transfers between devices with their start and end apart: 11 -> 10, of which waited for: 3 -> 2; matrix products, arithmetic and copies ran while one was open for 0% -> 0% of each run, Pallas kernels for 3% -> 3%
where the time goes in v4:
time: 33.3 us; the launch traced here: 33.1 us
  starting transfers between devices  11.6 us (35%)
  blocking collectives  10.6 us (32%)
  Pallas kernels  5.27 us (16%)
  waiting for transfers between devices  2.89 us (9%)
  between operations  1.47 us (4%)
  other arithmetic  1.14 us (3%)
    ppermute x10, starting transfers between devices, swap(): return lax.ppermute(block, AXES, swaps(axis, turn))  11.6 us
    all_to_all x1, blocking collectives, shards(): sums = lax.all_to_all(sums, AXES, 0, 0, tiled=True)  10.6 us
    pallas_call x6, Pallas kernels, call(): pl.pallas_call(kernel, out_shape=outs, in_specs=specs or [VMEM] * len(arg...  5.27 us
    ppermute x10, waiting for transfers between devices, swap(): return lax.ppermute(block, AXES, swaps(axis, turn))  2.89 us
    mul x1, other arithmetic, shards(): masked = unfixed_node_mask.astype(F32) * residual  1.14 us
  transfers between devices with their start and end apart: 10, of which 2 were waited for; matrix products, arithmetic and copies ran while one was open for 0% of the time, Pallas kernels for 3%

profile of v4, /device:TPU:0, one launch (start us, length us, event | category | flops | bytes accessed | tf_op | source)
XLA Modules:
  0.0 33.1 jit_solution(14938886413977092071)
XLA Ops:
  0.7 1.1 %convert_multiply_fusion.masked = f32[16,32,128]{2,1,0:T(8,128)S(1)} fusion(f32[16,32,128]{2,1,0:T(8,128)} %res.1, s32[16,32,128]{2,1,0:T(8,128)} %msk.1), kind=kLoop, calls=%fused_computation | loop fusion | flops 131072 | bytes 786432 | tf_op jit(solution)/shard_map/masks/mul | solution.py:448
  1.8 0.0 copy-done
  1.8 0.1 copy-done.4
  1.9 0.4 %pack.1 = (f32[4,32,128]{2,1,0:T(8,128)S(1)}, f32[4,32,128]{2,1,0:T(8,128)S(1)}, f32[4,16,128]{2,1,0:T(8,128)S(1)}, f32[4,16,128]{2,1,0:T(8,128)S(1)}, f32[8,512...) custom-call(f32[16,32,128]{2,1,0:T(8,128)S(1)} %convert_multiply_fusion.masked, ...), custom_call_target="tpu_custom_call" | custom-call | bytes 1048576 | tf_op jit(solution)/shard_map/pack/pallas_call | solution.py:415
  2.3 0.5 %collective-permute-start = (f32[4,32,128]{2,1,0:T(8,128)S(1)}, f32[4,32,128]{2,1,0:T(8,128)S(1)}, u32[]{:S(2)}, u32[]{:S(2)}) collective-permute-start(f32[4,32,128]{2,1,0:T(8,128)S(1)} %get-tuple-element.32), channel_id=1, source_target_pairs={{0,8},{1,9},{2,10},{3,11},{4,12},{5,13},{6,14},{7,15},{8,0},{9,1},... | collective-permute-start | bytes 196616 | tf_op jit(solution)/shard_map/faces_in/ppermute | solution.py:38
  2.8 2.6 %collective-permute-start.1 = (f32[4,32,128]{2,1,0:T(8,128)S(1)}, f32[4,32,128]{2,1,0:T(8,128)S(1)}, u32[]{:S(2)}, u32[]{:S(2)}) collective-permute-start(f32[4,32,128]{2,1,0:T(8,128)S(1)} %get-tuple-element.33), channel_id=1, source_target_pairs={{0,24},{1,25},{2,26},{3,27},{4,28},{5,29},{6,30},{7,31},{8,16},{9,... | collective-permute-start | bytes 196616 | tf_op jit(solution)/shard_map/faces_in/ppermute | solution.py:38
  5.4 1.6 %collective-permute-start.2 = (f32[4,16,128]{2,1,0:T(8,128)S(1)}, f32[4,16,128]{2,1,0:T(8,128)S(1)}, u32[]{:S(2)}, u32[]{:S(2)}) collective-permute-start(f32[4,16,128]{2,1,0:T(8,128)S(1)} %get-tuple-element.34), channel_id=1, source_target_pairs={{0,2},{1,3},{2,0},{3,1},{4,6},{5,7},{6,4},{7,5},{8,10},{9,11},{10,... | collective-permute-start | bytes 98312 | tf_op jit(solution)/shard_map/faces_in/ppermute | solution.py:38
  6.9 0.0 collective-permute-start.3
  6.9 0.0 copy-start.9
  7.0 1.6 %collective-permute-start.4 = (f32[8,512]{1,0:T(8,128)S(1)}, f32[8,512]{1,0:T(8,128)S(1)}, u32[]{:S(2)}, u32[]{:S(2)}) collective-permute-start(f32[8,512]{1,0:T(8,128)S(1)} %get-tuple-element.36), channel_id=1, source_target_pairs={{0,1},{1,0},{2,3},{3,2},{4,5},{5,4},{6,7},{7,6},{8,9},{9,8},{10,11... | collective-permute-start | bytes 49160 | tf_op jit(solution)/shard_map/faces_in/ppermute | solution.py:38
  8.6 0.3 own_part.1
  8.9 1.9 %collective-permute-done.4.rz = f32[8,512]{1,0:T(8,128)S(1)} collective-permute-done((f32[8,512]{1,0:T(8,128)S(1)}, f32[8,512]{1,0:T(8,128)S(1)}, u32[]{:S(2)}, u32[]{:S(2)}) %collective-permute-start.4) | collective-permute-done | bytes 16416 | tf_op jit(solution)/shard_map/faces_in/ppermute | solution.py:38
  10.8 0.0 collective-permute-done.2.ry0
  10.8 0.0 collective-permute-done.3.ry1
  10.8 0.0 collective-permute-done.rx0
  10.8 0.0 collective-permute-done.1.rx1
  10.9 2.0 %solve.1 = (f32[16,32,128]{2,1,0:T(8,128)S(1)}, f32[2,32,128]{2,1,0:T(8,128)S(1)}, f32[2,32,128]{2,1,0:T(8,128)S(1)}, f32[2,16,128]{2,1,0:T(8,128)S(1)}, f32[2,1...) custom-call(f32[512,256]{1,0:T(8,128)S(1)} %get-tuple-element.38.work, f32[720,256]{1,0:T(8,128)S(1)} %get-tuple-element.39.factors, ...), custom_call_target="tpu_custom_call" | custom-call | bytes 1048576 | tf_op jit(solution)/shard_map/solve/pallas_call | solution.py:415
  12.9 0.0 collective-permute-start.5
  13.0 0.6 %collective-permute-start.6 = (f32[2,32,128]{2,1,0:T(8,128)S(1)}, f32[2,32,128]{2,1,0:T(8,128)S(1)}, u32[]{:S(2)}, u32[]{:S(2)}) collective-permute-start(f32[2,32,128]{2,1,0:T(8,128)S(1)} %get-tuple-element.43.tx1), channel_id=1, source_target_pairs={{0,24},{1,25},{2,26},{3,27},{4,28},{5,29},{6,30},{7,31},{8,16},{9,... | collective-permute-start | bytes 98312 | tf_op jit(solution)/shard_map/faces_out/ppermute | solution.py:38
  13.6 3.1 %collective-permute-start.7 = (f32[2,16,128]{2,1,0:T(8,128)S(1)}, f32[2,16,128]{2,1,0:T(8,128)S(1)}, u32[]{:S(2)}, u32[]{:S(2)}) collective-permute-start(f32[2,16,128]{2,1,0:T(8,128)S(1)} %get-tuple-element.44.ty0), channel_id=1, source_target_pairs={{0,2},{1,3},{2,0},{3,1},{4,6},{5,7},{6,4},{7,5},{8,10},{9,11},{10,... | collective-permute-start | bytes 49160 | tf_op jit(solution)/shard_map/faces_out/ppermute | solution.py:38
  16.7 0.0 collective-permute-start.8
  16.7 1.5 %collective-permute-start.9 = (f32[8,512]{1,0:T(8,128)S(1)}, f32[8,512]{1,0:T(8,128)S(1)}, u32[]{:S(2)}, u32[]{:S(2)}) collective-permute-start(f32[8,512]{1,0:T(8,128)S(1)} %get-tuple-element.46.tz), channel_id=1, source_target_pairs={{0,1},{1,0},{2,3},{3,2},{4,5},{5,4},{6,7},{7,6},{8,9},{9,8},{10,11... | collective-permute-start | bytes 49160 | tf_op jit(solution)/shard_map/faces_out/ppermute | solution.py:38
  18.9 0.6 %links.1 = (f32[16,32,128]{2,1,0:T(8,128)S(1)}, f32[17,32,128]{2,1,0:T(8,128)S(1)}, f32[16,32,128]{2,1,0:T(8,128)S(1)}, f32[16,128]{1,0:T(8,128)S(1)}, f32[16,32...) custom-call(f32[1]{0:T(128)S(6)} %copy.18.rz_prev, ...), custom_call_target="tpu_custom_call" | custom-call | bytes 1048576 | tf_op jit(solution)/shard_map/links/pallas_call | solution.py:415
  19.5 0.0 collective-permute-done.7.qy0
  19.5 0.0 collective-permute-done.8.qy1
  19.5 1.0 %collective-permute-done.9.qz = f32[8,512]{1,0:T(8,128)S(1)} collective-permute-done((f32[8,512]{1,0:T(8,128)S(1)}, f32[8,512]{1,0:T(8,128)S(1)}, u32[]{:S(2)}, u32[]{:S(2)}) %collective-permute-start.9) | collective-permute-done | bytes 16416 | tf_op jit(solution)/shard_map/faces_out/ppermute | solution.py:38
  20.5 0.0 collective-permute-done.5.qx0
  20.5 0.0 collective-permute-done.6.qx1
  20.5 0.0 copy-start.5
  20.5 0.7 %image.1 = (f32[16,32,128]{2,1,0:T(8,128)S(1)}, f32[16,32,128]{2,1,0:T(8,128)S(1)}, f32[32,1,128]{2,1,0:T(1,128)S(1)}) custom-call(f32[16,32,128]{2,1,0:T(8,128)S(1)} %convert_multiply_fusion.masked, f32[16,32,128]{2,1,0:T(8,128)S(1)} %get-tuple-element.30.mask, f32[16,32,128]{2,1,0:T(8,128)S(1)} %get-tuple-element.31.d, ...), custom_call_target="tpu_custom_call" | custom-call | bytes 1048576 | tf_op jit(solution)/shard_map/image/pallas_call | solution.py:415
  21.2 10.6 %all_to_all.5.sums = f32[32,1,128]{2,1,0:T(1,128)S(1)} all-to-all(f32[32,1,128]{2,1,0:T(1,128)S(1)} %get-tuple-element.54), channel_id=1, replica_groups=mesh['gx'=4,'gy'=4,'gz'=2] {'gx','gy','gz'}, dimensions={0} | all-to-all | bytes 32768 | tf_op jit(solution)/shard_map/sums/all_to_all | solution.py:467
  31.9 1.3 %update.1 = (f32[16,32,128]{2,1,0:T(8,128)}, f32[16,32,128]{2,1,0:T(8,128)}, f32[16,32,128]{2,1,0:T(8,128)}) custom-call(f32[1,128]{1,0:T(1,128)S(1)} %get-tuple-element.37.rz_line, f32[32,1,128]{2,1,0:T(1,128)S(1)} %all_to_all.5.sums, f32[16,32,128]{2,1,0:T(8,128)S(1)} %copy-done.5, f32[16,32,128]{2,1,0:T(8,128)S(1)} %copy-done.2, ...), custom_call_target="tpu_custom_call" | custom-call | bytes 1048576 | tf_op jit(solution)/shard_map/update/pallas_call | solution.py:415
  (24 shorter events, 0.0 us)
Async XLA Ops:
  0.6 1.2 %copy-start.1 = (s32[16,32,128]{2,1,0:T(8,128)S(1)}, s32[16,32,128]{2,1,0:T(8,128)}, u32[]{:S(2)}) copy-start(s32[16,32,128]{2,1,0:T(8,128)} %msk.1) | copy-start | bytes 786436
  0.6 1.2 %copy-start = (f32[16,32,128]{2,1,0:T(8,128)S(1)}, f32[16,32,128]{2,1,0:T(8,128)}, u32[]{:S(2)}) copy-start(f32[16,32,128]{2,1,0:T(8,128)} %mu.5) | copy-start | bytes 786436
  0.7 1.2 %copy-start.4 = (f32[16,32,128]{2,1,0:T(8,128)S(1)}, f32[16,32,128]{2,1,0:T(8,128)}, u32[]{:S(2)}) copy-start(f32[16,32,128]{2,1,0:T(8,128)} %direction.1) | copy-start | bytes 786436
  1.9 6.6 %copy-start.3 = (bf16[256,256]{1,0:T(8,128)(2,1)S(1)}, bf16[256,256]{1,0:T(8,128)(2,1)}, u32[]{:S(2)}) copy-start(bf16[256,256]{1,0:T(8,128)(2,1)} %constant.18.clone.fwd) | copy-start | bytes 393220
  1.9 6.6 %copy-start.10 = (f32[40,256]{1,0:T(8,128)S(1)}, f32[40,256]{1,0:T(8,128)}, u32[]{:S(2)}) copy-start(f32[40,256]{1,0:T(8,128)} %constant.19.clone.middle) | copy-start | bytes 122884
  1.9 8.9 %copy-start.12 = (bf16[32,256]{1,0:T(8,128)(2,1)S(1)}, bf16[32,256]{1,0:T(8,128)(2,1)}, u32[]{:S(2)}) copy-start(bf16[32,256]{1,0:T(8,128)(2,1)} %constant.26.clone.out_ends) | copy-start | bytes 49156
  2.3 8.5 %collective-permute-start = (f32[4,32,128]{2,1,0:T(8,128)S(1)}, f32[4,32,128]{2,1,0:T(8,128)S(1)}, u32[]{:S(2)}, u32[]{:S(2)}) collective-permute-start(f32[4,32,128]{2,1,0:T(8,128)S(1)} %get-tuple-element.32), channel_id=1, source_target_pairs={{0,8},{1,9},{2,10},{3,11},{4,12},{5,13},{6,14},{7,15},{8,0},{9,1},... | collective-permute-start | bytes 196616 | tf_op jit(solution)/shard_map/faces_in/ppermute | solution.py:38
  2.8 8.0 %collective-permute-start.1 = (f32[4,32,128]{2,1,0:T(8,128)S(1)}, f32[4,32,128]{2,1,0:T(8,128)S(1)}, u32[]{:S(2)}, u32[]{:S(2)}) collective-permute-start(f32[4,32,128]{2,1,0:T(8,128)S(1)} %get-tuple-element.33), channel_id=1, source_target_pairs={{0,24},{1,25},{2,26},{3,27},{4,28},{5,29},{6,30},{7,31},{8,16},{9,... | collective-permute-start | bytes 196616 | tf_op jit(solution)/shard_map/faces_in/ppermute | solution.py:38
  5.4 5.4 %collective-permute-start.2 = (f32[4,16,128]{2,1,0:T(8,128)S(1)}, f32[4,16,128]{2,1,0:T(8,128)S(1)}, u32[]{:S(2)}, u32[]{:S(2)}) collective-permute-start(f32[4,16,128]{2,1,0:T(8,128)S(1)} %get-tuple-element.34), channel_id=1, source_target_pairs={{0,2},{1,3},{2,0},{3,1},{4,6},{5,7},{6,4},{7,5},{8,10},{9,11},{10,... | collective-permute-start | bytes 98312 | tf_op jit(solution)/shard_map/faces_in/ppermute | solution.py:38
  6.9 3.8 %collective-permute-start.3 = (f32[4,16,128]{2,1,0:T(8,128)S(1)}, f32[4,16,128]{2,1,0:T(8,128)S(1)}, u32[]{:S(2)}, u32[]{:S(2)}) collective-permute-start(f32[4,16,128]{2,1,0:T(8,128)S(1)} %get-tuple-element.35), channel_id=1, source_target_pairs={{0,8},{1,9},{2,4},{3,5},{4,2},{5,3},{6,14},{7,15},{8,0},{9,1},{10,... | collective-permute-start | bytes 98312 | tf_op jit(solution)/shard_map/faces_in/ppermute | solution.py:38
  6.9 3.9 %copy-start.6 = (bf16[480,256]{1,0:T(8,128)(2,1)S(1)}, bf16[480,256]{1,0:T(8,128)(2,1)}, u32[]{:S(2)}) copy-start(bf16[480,256]{1,0:T(8,128)(2,1)} %constant.21.clone.into) | copy-start | bytes 737284
  6.9 3.9 %copy-start.7 = (bf16[384,256]{1,0:T(8,128)(2,1)S(1)}, bf16[384,256]{1,0:T(8,128)(2,1)}, u32[]{:S(2)}) copy-start(bf16[384,256]{1,0:T(8,128)(2,1)} %constant.22.clone.back) | copy-start | bytes 589828
  6.9 3.9 %copy-start.8 = (bf16[256,256]{1,0:T(8,128)(2,1)S(1)}, bf16[256,256]{1,0:T(8,128)(2,1)}, u32[]{:S(2)}) copy-start(bf16[256,256]{1,0:T(8,128)(2,1)} %constant.25.clone.out) | copy-start | bytes 393220
  6.9 3.9 %copy-start.9 = (bf16[192,256]{1,0:T(8,128)(2,1)S(1)}, bf16[192,256]{1,0:T(8,128)(2,1)}, u32[]{:S(2)}) copy-start(bf16[192,256]{1,0:T(8,128)(2,1)} %constant.23.clone.back_faces) | copy-start | bytes 294916
  7.0 3.8 %collective-permute-start.4 = (f32[8,512]{1,0:T(8,128)S(1)}, f32[8,512]{1,0:T(8,128)S(1)}, u32[]{:S(2)}, u32[]{:S(2)}) collective-permute-start(f32[8,512]{1,0:T(8,128)S(1)} %get-tuple-element.36), channel_id=1, source_target_pairs={{0,1},{1,0},{2,3},{3,2},{4,5},{5,4},{6,7},{7,6},{8,9},{9,8},{10,11... | collective-permute-start | bytes 49160 | tf_op jit(solution)/shard_map/faces_in/ppermute | solution.py:38
  8.6 2.3 %copy-start.11 = (f32[40,128]{1,0:T(8,128)S(1)}, f32[40,128]{1,0:T(8,128)}, u32[]{:S(2)}) copy-start(f32[40,128]{1,0:T(8,128)} %constant.24.clone.rim) | copy-start | bytes 61444
  8.6 2.3 %copy-start.13 = (bf16[16,256]{1,0:T(8,128)(2,1)S(1)}, bf16[16,256]{1,0:T(8,128)(2,1)}, u32[]{:S(2)}) copy-start(bf16[16,256]{1,0:T(8,128)(2,1)} %constant.20.clone.face_table) | copy-start | bytes 24580
  12.9 7.6 %collective-permute-start.5 = (f32[2,32,128]{2,1,0:T(8,128)S(1)}, f32[2,32,128]{2,1,0:T(8,128)S(1)}, u32[]{:S(2)}, u32[]{:S(2)}) collective-permute-start(f32[2,32,128]{2,1,0:T(8,128)S(1)} %get-tuple-element.42.tx0), channel_id=1, source_target_pairs={{0,8},{1,9},{2,10},{3,11},{4,12},{5,13},{6,14},{7,15},{8,0},{9,1},... | collective-permute-start | bytes 98312 | tf_op jit(solution)/shard_map/faces_out/ppermute | solution.py:38
  13.0 7.5 %collective-permute-start.6 = (f32[2,32,128]{2,1,0:T(8,128)S(1)}, f32[2,32,128]{2,1,0:T(8,128)S(1)}, u32[]{:S(2)}, u32[]{:S(2)}) collective-permute-start(f32[2,32,128]{2,1,0:T(8,128)S(1)} %get-tuple-element.43.tx1), channel_id=1, source_target_pairs={{0,24},{1,25},{2,26},{3,27},{4,28},{5,29},{6,30},{7,31},{8,16},{9,... | collective-permute-start | bytes 98312 | tf_op jit(solution)/shard_map/faces_out/ppermute | solution.py:38
  13.6 5.9 %collective-permute-start.7 = (f32[2,16,128]{2,1,0:T(8,128)S(1)}, f32[2,16,128]{2,1,0:T(8,128)S(1)}, u32[]{:S(2)}, u32[]{:S(2)}) collective-permute-start(f32[2,16,128]{2,1,0:T(8,128)S(1)} %get-tuple-element.44.ty0), channel_id=1, source_target_pairs={{0,2},{1,3},{2,0},{3,1},{4,6},{5,7},{6,4},{7,5},{8,10},{9,11},{10,... | collective-permute-start | bytes 49160 | tf_op jit(solution)/shard_map/faces_out/ppermute | solution.py:38
  16.7 2.8 %collective-permute-start.8 = (f32[2,16,128]{2,1,0:T(8,128)S(1)}, f32[2,16,128]{2,1,0:T(8,128)S(1)}, u32[]{:S(2)}, u32[]{:S(2)}) collective-permute-start(f32[2,16,128]{2,1,0:T(8,128)S(1)} %get-tuple-element.45.ty1), channel_id=1, source_target_pairs={{0,8},{1,9},{2,4},{3,5},{4,2},{5,3},{6,14},{7,15},{8,0},{9,1},{10,... | collective-permute-start | bytes 49160 | tf_op jit(solution)/shard_map/faces_out/ppermute | solution.py:38
  16.7 3.7 %collective-permute-start.9 = (f32[8,512]{1,0:T(8,128)S(1)}, f32[8,512]{1,0:T(8,128)S(1)}, u32[]{:S(2)}, u32[]{:S(2)}) collective-permute-start(f32[8,512]{1,0:T(8,128)S(1)} %get-tuple-element.46.tz), channel_id=1, source_target_pairs={{0,1},{1,0},{2,3},{3,2},{4,5},{5,4},{6,7},{7,6},{8,9},{9,8},{10,11... | collective-permute-start | bytes 49160 | tf_op jit(solution)/shard_map/faces_out/ppermute | solution.py:38
  20.5 11.4 %copy-start.2 = (f32[16,32,128]{2,1,0:T(8,128)S(1)}, f32[16,32,128]{2,1,0:T(8,128)}, u32[]{:S(2)}) copy-start(f32[16,32,128]{2,1,0:T(8,128)} %res.1) | copy-start | bytes 786436
  20.5 11.4 %copy-start.5 = (f32[16,32,128]{2,1,0:T(8,128)S(1)}, f32[16,32,128]{2,1,0:T(8,128)}, u32[]{:S(2)}) copy-start(f32[16,32,128]{2,1,0:T(8,128)} %iterate.1) | copy-start | bytes 786436

commit v5 on v4

--- a/solution.py
+++ b/solution.py
@@ -103,30 +103,20 @@
         into[s * pad : s * pad + ny, s * size_y : (s + 1) * size_y] = qy[1:-1].T
     rim = np.zeros((pad, LANES // 2))
     rim[:ny, 0], rim[:ny, 1] = qy[0], qy[-1]
-    groups = nx // GROUP
     back = np.zeros((GROUP * size_y, LANES))
-    faces = np.zeros((groups, 2, size_x, LANES))
     for s in range(GROUP):
-        modes = slice(s * pad, s * pad + ny)
-        back[s * size_y : (s + 1) * size_y, modes] = qy[1:-1]
-        for g in range(groups):
-            i = g * GROUP + s - 1
-            if 0 <= i < size_x:
-                faces[g, 0, i, modes] = qy[0]
-                faces[g, 1, i, modes] = qy[-1]
+        back[s * size_y : (s + 1) * size_y, s * pad : s * pad + ny] = qy[1:-1]
     middle = np.full((pad, LANES), 2.0)
     middle[:ny, :nz] += ly[:, None] + lz[None, :]
     middle[ny:], middle[:, nz:] = 4.0, 4.0
     ih, il = np_halves(into)
     bh, bl = np_halves(back)
-    gh, gl = np_halves(faces.reshape(-1, LANES))
     return dict(
         fwd=np.concatenate([fh, fl]),
         middle=middle.astype(np.float32),
         face=face,
         into=np.concatenate([ih, il]),
         back=np.concatenate([bh, bl]),
-        back_faces=np.concatenate([gh, gl]),
         rim=rim.astype(np.float32),
         out=np.concatenate([np.ascontiguousarray(fh.T), np.ascontiguousarray(fl.T)], axis=1),
         out_ends=out_ends,
@@ -160,20 +150,22 @@
     return [wide[:, k * depth : (k + 1) * depth] for k in range(count)]
 
 
-def pack_kernel(masked, msk, direction, mu, sx0, sx1, sy0, sy1, sz, mask_out, d):
+def pack_kernel(masked, msk, direction, mu, sx0, sx1, sy0, sy1, sz):
     size_x, size_y, size_z = masked.shape
     even_x, even_y, even_z = (place(axis)[0] for axis in AXES)
-    mask = msk[...].astype(F32)
-    fields = (masked[...], mask, mask * direction[...], mu[...])
-    mask_out[...], d[...] = fields[1], fields[2]
-    for f, field in enumerate(fields):
-        low, high = field[0], field[size_x - 1]
+
+    def fields(where):
+        mask = msk[where].astype(F32)
+        return masked[where], mask, mask * direction[where], mu[where]
+
+    for f, (low, high) in enumerate(zip(fields(0), fields(size_x - 1))):
         sx0[f] = jnp.where(even_x, high, low)
         sx1[f] = jnp.where(even_x, low, high)
-        low, high = field[:, 0], field[:, size_y - 1]
+    every = slice(None)
+    for f, (low, high) in enumerate(zip(fields((every, 0)), fields((every, size_y - 1)))):
         sy0[f] = jnp.where(even_y, high, low)
         sy1[f] = jnp.where(even_y, low, high)
-    flat = [field.reshape(size_x * size_y, size_z) for field in fields]
+    flat = [field.reshape(size_x * size_y, size_z) for field in fields(every)]
     sz[...] = lane_rows(flat, jnp.where(even_z, size_z - 1, 0))
 
 
@@ -183,8 +175,10 @@
     return dot(jnp.concatenate([high, low], axis=1), jnp.concatenate([table, table], axis=0)) + dot(high, fwd[size_z:])
 
 
-def own_kernel(masked, mu, fwd, middle, work, factors, scale):
+def own_kernel(masked, msk, direction, mu, fwd, middle, work, mask, d, factors, scale):
     size_x, size_y, size_z = masked.shape
+    mask[...] = msk[...].astype(F32)
+    d[...] = mask[...] * direction[...]
     work[...] = along_z(masked[...].reshape(size_x * size_y, size_z), fwd, size_z)
     pad = middle.shape[0]
     along = middle[...]
@@ -197,7 +191,7 @@
 
 
 def solve_kernel(
-    work, factors, scale, mask, rx0, rx1, ry0, ry1, rz, fwd, face_table, into, back, back_faces, rim, out, out_ends,
+    work, factors, scale, mask, rx0, rx1, ry0, ry1, rz, fwd, face_table, into, back, rim, out, out_ends,
     own, tx0, tx1, ty0, ty1, tz,
 ):
     size_x, size_y, size_z = mask.shape
@@ -237,20 +231,17 @@
         solved[i] = solved[i] + factors[i * pad : (i + 1) * pad] * solved[i + 1]
     solved = jnp.concatenate(solved, axis=0)
     high, low = halves(solved)
-    own_rows, face_rows = GROUP * size_y, 2 * size_x
-    half = back_faces.shape[0] // 2
-    local, y_faces = [], None
+    rest = jnp.zeros((LANES - GROUP * pad, LANES), BF16)
+    high, low = (jnp.concatenate([half, rest], axis=0) for half in (high, low))
+    own_rows = GROUP * size_y
+    back_all = jnp.concatenate([back[:own_rows], back[own_rows:], back[:own_rows]], axis=1)
+    local = []
     for g in range(nx // GROUP):
-        part = slice(g * GROUP * pad, (g + 1) * GROUP * pad)
-        line = slice(g * face_rows, (g + 1) * face_rows)
-        table_h = jnp.concatenate([back[:own_rows], back_faces[line]], axis=0)[:, : GROUP * pad]
-        line = slice(half + g * face_rows, half + (g + 1) * face_rows)
-        table_l = jnp.concatenate([back[own_rows:], back_faces[line]], axis=0)[:, : GROUP * pad]
-        value = dot(table_h, high[part]) + dot(table_l, high[part]) + dot(table_h, low[part])
-        local.append(value[:own_rows])
-        rest = value[own_rows:]
-        y_faces = rest if y_faces is None else y_faces + rest
-    local = jnp.concatenate(local + [y_faces], axis=0)
+        part = slice(g * GROUP * pad, g * GROUP * pad + LANES)
+        local.append(dot(back_all, jnp.concatenate([high[part], high[part], low[part]], axis=0)))
+    own_modes = solved[pad : (nx - 1) * pad].reshape(size_x, pad, LANES)
+    local += [jnp.sum(own_modes * rim_low[None], axis=1), jnp.sum(own_modes * rim_high[None], axis=1)]
+    local = jnp.concatenate(local, axis=0)
     local = local * scale[0:1, 0:1]
     high, low = halves(local)
     both = dot(high, out[...])
@@ -448,14 +439,15 @@
         masked = unfixed_node_mask.astype(F32) * residual
         mu = permeability
     with jax.named_scope("pack"):
-        *sent, mask, d = call(pack_kernel, (masked, unfixed_node_mask, direction, mu), faces(4) + [box] * 2)
+        sent = call(pack_kernel, (masked, unfixed_node_mask, direction, mu), faces(4))
     with jax.named_scope("faces_in"):
         near = exchange(*sent)
     with jax.named_scope("own_part"):
         modes = ((size_x + 2) * middle.shape[0], LANES)
-        part = call(own_kernel, (masked, mu, fwd, middle), [(rows, LANES), modes, (8, size_z)])
+        args = (masked, unfixed_node_mask, direction, mu, fwd, middle)
+        work, mask, d, *part = call(own_kernel, args, [(rows, LANES), box, box, modes, (8, size_z)])
     with jax.named_scope("solve"):
-        own, *made = call(solve_kernel, (*part, mask, *near, fwd, *tables), [box] + faces(2))
+        own, *made = call(solve_kernel, (work, *part, mask, *near, fwd, *tables), [box] + faces(2))
     with jax.named_scope("faces_out"):
         got = exchange(*made)
     with jax.named_scope("links"):

time: 33.3 us -> 33 us (level)
  no operation moved by 1% of the time
where the time goes in v5:
time: 33 us; the launch traced here: 32.8 us
  starting transfers between devices  11.5 us (35%)
  blocking collectives  10.6 us (32%)
  Pallas kernels  5.05 us (15%)
  waiting for transfers between devices  2.84 us (9%)
  between operations  1.46 us (4%)
  other arithmetic  1.14 us (3%)
    ppermute x10, starting transfers between devices, swap(): return lax.ppermute(block, AXES, swaps(axis, turn))  11.5 us
    all_to_all x1, blocking collectives, shards(): sums = lax.all_to_all(sums, AXES, 0, 0, tiled=True)  10.6 us
    pallas_call x6, Pallas kernels, call(): pl.pallas_call(kernel, out_shape=outs, in_specs=specs or [VMEM] * len(arg...  5.05 us
    ppermute x10, waiting for transfers between devices, swap(): return lax.ppermute(block, AXES, swaps(axis, turn))  2.84 us
    mul x1, other arithmetic, shards(): masked = unfixed_node_mask.astype(F32) * residual  1.14 us
  transfers between devices with their start and end apart: 10, of which 2 were waited for; matrix products, arithmetic and copies ran while one was open for 0% of the time, Pallas kernels for 3%

profile of v5, /device:TPU:0, one launch (start us, length us, event | category | flops | bytes accessed | tf_op | source)
XLA Modules:
  0.0 32.8 jit_solution(9811537273487314641)
XLA Ops:
  0.7 1.1 %convert_multiply_fusion.masked = f32[16,32,128]{2,1,0:T(8,128)S(1)} fusion(f32[16,32,128]{2,1,0:T(8,128)} %res.1, s32[16,32,128]{2,1,0:T(8,128)} %msk.3), kind=kLoop, calls=%fused_computation | loop fusion | flops 131072 | bytes 786432 | tf_op jit(solution)/shard_map/masks/mul | solution.py:439
  1.8 0.0 copy-done.1
  1.8 0.1 copy-done.2
  1.9 0.4 %pack.1 = (f32[4,32,128]{2,1,0:T(8,128)S(1)}, f32[4,32,128]{2,1,0:T(8,128)S(1)}, f32[4,16,128]{2,1,0:T(8,128)S(1)}, f32[4,16,128]{2,1,0:T(8,128)S(1)}, f32[8,512]{1,0:T(8,128)S(1)}) custom-call(f32[16,32,128]{2,1,0:T(8,128)S(1)} %convert_multiply_fusion.masked, s32[16,32,128]{2,1,0:T(8,128)S(1)} %copy-done, f32[16,32,128]{2,1,0:T(8,128)S(1)} %copy-done.2, ...), custom_call_target="tpu_custom_call" | custom-call | bytes 1048576 | tf_op jit(solution)/shard_map/pack/pallas_call | solution.py:406
  2.3 0.5 %collective-permute-start = (f32[4,32,128]{2,1,0:T(8,128)S(1)}, f32[4,32,128]{2,1,0:T(8,128)S(1)}, u32[]{:S(2)}, u32[]{:S(2)}) collective-permute-start(f32[4,32,128]{2,1,0:T(8,128)S(1)} %get-tuple-element.32), channel_id=1, source_target_pairs={{0,8},{1,9},{2,10},{3,11},{4,12},{5,13},{6,14},{7,15},{8,0},{9,1},... | collective-permute-start | bytes 196616 | tf_op jit(solution)/shard_map/faces_in/ppermute | solution.py:38
  2.8 2.6 %collective-permute-start.1 = (f32[4,32,128]{2,1,0:T(8,128)S(1)}, f32[4,32,128]{2,1,0:T(8,128)S(1)}, u32[]{:S(2)}, u32[]{:S(2)}) collective-permute-start(f32[4,32,128]{2,1,0:T(8,128)S(1)} %get-tuple-element.33), channel_id=1, source_target_pairs={{0,24},{1,25},{2,26},{3,27},{4,28},{5,29},{6,30},{7,31},{8,16},{9,... | collective-permute-start | bytes 196616 | tf_op jit(solution)/shard_map/faces_in/ppermute | solution.py:38
  5.4 1.6 %collective-permute-start.2 = (f32[4,16,128]{2,1,0:T(8,128)S(1)}, f32[4,16,128]{2,1,0:T(8,128)S(1)}, u32[]{:S(2)}, u32[]{:S(2)}) collective-permute-start(f32[4,16,128]{2,1,0:T(8,128)S(1)} %get-tuple-element.34), channel_id=1, source_target_pairs={{0,2},{1,3},{2,0},{3,1},{4,6},{5,7},{6,4},{7,5},{8,10},{9,11},{10,... | collective-permute-start | bytes 98312 | tf_op jit(solution)/shard_map/faces_in/ppermute | solution.py:38
  7.0 0.0 collective-permute-start.3
  7.0 1.6 %collective-permute-start.4 = (f32[8,512]{1,0:T(8,128)S(1)}, f32[8,512]{1,0:T(8,128)S(1)}, u32[]{:S(2)}, u32[]{:S(2)}) collective-permute-start(f32[8,512]{1,0:T(8,128)S(1)} %get-tuple-element.36), channel_id=1, source_target_pairs={{0,1},{1,0},{2,3},{3,2},{4,5},{5,4},{6,7},{7,6},{8,9},{9,8},{10,11... | collective-permute-start | bytes 49160 | tf_op jit(solution)/shard_map/faces_in/ppermute | solution.py:38
  8.6 0.0 copy-start.12
  8.6 0.3 %own_part.1 = (f32[512,256]{1,0:T(8,128)S(1)}, f32[16,32,128]{2,1,0:T(8,128)S(1)}, f32[16,32,128]{2,1,0:T(8,128)S(1)}, f32[720,256]{1,0:T(8,128)S(1)}, f32[8,128]{1,0:T(8,128)S(1)}) custom-call(f32[16,32,128]{2,1,0:T(8,128)S(1)} %convert_multiply_fusion.masked, s32[16,32,128]{2,1,0:T(8,128)S(1)} %copy-done, f32[16,32,128]{2,1,0:T(8,128)S(1)} %copy-done.2, ...), custom_call_target="tpu_custom_call" | custom-call | bytes 1048576 | tf_op jit(solution)/shard_map/own_part/pallas_call | solution.py:406
  9.0 1.8 %collective-permute-done.4.rz = f32[8,512]{1,0:T(8,128)S(1)} collective-permute-done((f32[8,512]{1,0:T(8,128)S(1)}, f32[8,512]{1,0:T(8,128)S(1)}, u32[]{:S(2)}, u32[]{:S(2)}) %collective-permute-start.4) | collective-permute-done | bytes 16416 | tf_op jit(solution)/shard_map/faces_in/ppermute | solution.py:38
  10.8 0.0 collective-permute-done.2.ry0
  10.8 0.0 collective-permute-done.3.ry1
  10.8 0.0 collective-permute-done.rx0
  10.8 0.0 collective-permute-done.1.rx1
  10.9 1.7 %solve.1 = (f32[16,32,128]{2,1,0:T(8,128)S(1)}, f32[2,32,128]{2,1,0:T(8,128)S(1)}, f32[2,32,128]{2,1,0:T(8,128)S(1)}, f32[2,16,128]{2,1,0:T(8,128)S(1)}, f32[2,1...) custom-call(f32[512,256]{1,0:T(8,128)S(1)} %get-tuple-element.38.work, f32[720,256]{1,0:T(8,128)S(1)} %get-tuple-element.39.factors, ...), custom_call_target="tpu_custom_call" | custom-call | bytes 1048576 | tf_op jit(solution)/shard_map/solve/pallas_call | solution.py:406
  12.6 0.0 collective-permute-start.5
  12.7 0.7 %collective-permute-start.6 = (f32[2,32,128]{2,1,0:T(8,128)S(1)}, f32[2,32,128]{2,1,0:T(8,128)S(1)}, u32[]{:S(2)}, u32[]{:S(2)}) collective-permute-start(f32[2,32,128]{2,1,0:T(8,128)S(1)} %get-tuple-element.43.tx1), channel_id=1, source_target_pairs={{0,24},{1,25},{2,26},{3,27},{4,28},{5,29},{6,30},{7,31},{8,16},{9,... | collective-permute-start | bytes 98312 | tf_op jit(solution)/shard_map/faces_out/ppermute | solution.py:38
  13.3 3.1 %collective-permute-start.7 = (f32[2,16,128]{2,1,0:T(8,128)S(1)}, f32[2,16,128]{2,1,0:T(8,128)S(1)}, u32[]{:S(2)}, u32[]{:S(2)}) collective-permute-start(f32[2,16,128]{2,1,0:T(8,128)S(1)} %get-tuple-element.44.ty0), channel_id=1, source_target_pairs={{0,2},{1,3},{2,0},{3,1},{4,6},{5,7},{6,4},{7,5},{8,10},{9,11},{10,... | collective-permute-start | bytes 49160 | tf_op jit(solution)/shard_map/faces_out/ppermute | solution.py:38
  16.4 0.0 collective-permute-start.8
  16.4 1.5 %collective-permute-start.9 = (f32[8,512]{1,0:T(8,128)S(1)}, f32[8,512]{1,0:T(8,128)S(1)}, u32[]{:S(2)}, u32[]{:S(2)}) collective-permute-start(f32[8,512]{1,0:T(8,128)S(1)} %get-tuple-element.46.tz), channel_id=1, source_target_pairs={{0,1},{1,0},{2,3},{3,2},{4,5},{5,4},{6,7},{7,6},{8,9},{9,8},{10,11... | collective-permute-start | bytes 49160 | tf_op jit(solution)/shard_map/faces_out/ppermute | solution.py:38
  18.6 0.6 %links.1 = (f32[16,32,128]{2,1,0:T(8,128)S(1)}, f32[17,32,128]{2,1,0:T(8,128)S(1)}, f32[16,32,128]{2,1,0:T(8,128)S(1)}, f32[16,128]{1,0:T(8,128)S(1)}, f32[16,32...) custom-call(f32[1]{0:T(128)S(6)} %copy.17.rz_prev, ...), custom_call_target="tpu_custom_call" | custom-call | bytes 1048576 | tf_op jit(solution)/shard_map/links/pallas_call | solution.py:406
  19.1 0.0 collective-permute-done.7.qy0
  19.1 0.0 collective-permute-done.8.qy1
  19.1 1.0 %collective-permute-done.9.qz = f32[8,512]{1,0:T(8,128)S(1)} collective-permute-done((f32[8,512]{1,0:T(8,128)S(1)}, f32[8,512]{1,0:T(8,128)S(1)}, u32[]{:S(2)}, u32[]{:S(2)}) %collective-permute-start.9) | collective-permute-done | bytes 16416 | tf_op jit(solution)/shard_map/faces_out/ppermute | solution.py:38
  20.1 0.0 collective-permute-done.5.qx0
  20.1 0.0 collective-permute-done.6.qx1
  20.1 0.0 copy-start.5
  20.1 0.7 %image.1 = (f32[16,32,128]{2,1,0:T(8,128)S(1)}, f32[16,32,128]{2,1,0:T(8,128)S(1)}, f32[32,1,128]{2,1,0:T(1,128)S(1)}) custom-call(f32[16,32,128]{2,1,0:T(8,128)S(1)} %convert_multiply_fusion.masked, f32[16,32,128]{2,1,0:T(8,128)S(1)} %get-tuple-element.30.mask, f32[16,32,128]{2,1,0:T(8,128)S(1)} %get-tuple-element.31.d, ...), custom_call_target="tpu_custom_call" | custom-call | bytes 1048576 | tf_op jit(solution)/shard_map/image/pallas_call | solution.py:406
  20.9 10.6 %all_to_all.5.sums = f32[32,1,128]{2,1,0:T(1,128)S(1)} all-to-all(f32[32,1,128]{2,1,0:T(1,128)S(1)} %get-tuple-element.54), channel_id=1, replica_groups=mesh['gx'=4,'gy'=4,'gz'=2] {'gx','gy','gz'}, dimensions={0} | all-to-all | bytes 32768 | tf_op jit(solution)/shard_map/sums/all_to_all | solution.py:459
  31.5 1.3 %update.1 = (f32[16,32,128]{2,1,0:T(8,128)}, f32[16,32,128]{2,1,0:T(8,128)}, f32[16,32,128]{2,1,0:T(8,128)}) custom-call(f32[1,128]{1,0:T(1,128)S(1)} %get-tuple-element.37.rz_line, f32[32,1,128]{2,1,0:T(1,128)S(1)} %all_to_all.5.sums, f32[16,32,128]{2,1,0:T(8,128)S(1)} %copy-done.5, f32[16,32,128]{2,1,0:T(8,128)S(1)} %copy-done.3, ...), custom_call_target="tpu_custom_call" | custom-call | bytes 1048576 | tf_op jit(solution)/shard_map/update/pallas_call | solution.py:406
  (22 shorter events, 0.0 us)
Async XLA Ops:
  0.6 1.2 %copy-start = (s32[16,32,128]{2,1,0:T(8,128)S(1)}, s32[16,32,128]{2,1,0:T(8,128)}, u32[]{:S(2)}) copy-start(s32[16,32,128]{2,1,0:T(8,128)} %msk.3) | copy-start | bytes 786436
  0.6 1.2 %copy-start.1 = (f32[16,32,128]{2,1,0:T(8,128)S(1)}, f32[16,32,128]{2,1,0:T(8,128)}, u32[]{:S(2)}) copy-start(f32[16,32,128]{2,1,0:T(8,128)} %mu.5) | copy-start | bytes 786436
  0.7 1.2 %copy-start.2 = (f32[16,32,128]{2,1,0:T(8,128)S(1)}, f32[16,32,128]{2,1,0:T(8,128)}, u32[]{:S(2)}) copy-start(f32[16,32,128]{2,1,0:T(8,128)} %direction.3) | copy-start | bytes 786436
  1.9 6.7 %copy-start.4 = (bf16[256,256]{1,0:T(8,128)(2,1)S(1)}, bf16[256,256]{1,0:T(8,128)(2,1)}, u32[]{:S(2)}) copy-start(bf16[256,256]{1,0:T(8,128)(2,1)} %constant.16.clone.fwd) | copy-start | bytes 393220
  1.9 6.7 %copy-start.9 = (f32[40,256]{1,0:T(8,128)S(1)}, f32[40,256]{1,0:T(8,128)}, u32[]{:S(2)}) copy-start(f32[40,256]{1,0:T(8,128)} %constant.17.clone.middle) | copy-start | bytes 122884
  2.3 8.5 %collective-permute-start = (f32[4,32,128]{2,1,0:T(8,128)S(1)}, f32[4,32,128]{2,1,0:T(8,128)S(1)}, u32[]{:S(2)}, u32[]{:S(2)}) collective-permute-start(f32[4,32,128]{2,1,0:T(8,128)S(1)} %get-tuple-element.32), channel_id=1, source_target_pairs={{0,8},{1,9},{2,10},{3,11},{4,12},{5,13},{6,14},{7,15},{8,0},{9,1},... | collective-permute-start | bytes 196616 | tf_op jit(solution)/shard_map/faces_in/ppermute | solution.py:38
  2.8 8.0 %collective-permute-start.1 = (f32[4,32,128]{2,1,0:T(8,128)S(1)}, f32[4,32,128]{2,1,0:T(8,128)S(1)}, u32[]{:S(2)}, u32[]{:S(2)}) collective-permute-start(f32[4,32,128]{2,1,0:T(8,128)S(1)} %get-tuple-element.33), channel_id=1, source_target_pairs={{0,24},{1,25},{2,26},{3,27},{4,28},{5,29},{6,30},{7,31},{8,16},{9,... | collective-permute-start | bytes 196616 | tf_op jit(solution)/shard_map/faces_in/ppermute | solution.py:38
  5.4 5.4 %collective-permute-start.2 = (f32[4,16,128]{2,1,0:T(8,128)S(1)}, f32[4,16,128]{2,1,0:T(8,128)S(1)}, u32[]{:S(2)}, u32[]{:S(2)}) collective-permute-start(f32[4,16,128]{2,1,0:T(8,128)S(1)} %get-tuple-element.34), channel_id=1, source_target_pairs={{0,2},{1,3},{2,0},{3,1},{4,6},{5,7},{6,4},{7,5},{8,10},{9,11},{10,... | collective-permute-start | bytes 98312 | tf_op jit(solution)/shard_map/faces_in/ppermute | solution.py:38
  7.0 3.8 %collective-permute-start.3 = (f32[4,16,128]{2,1,0:T(8,128)S(1)}, f32[4,16,128]{2,1,0:T(8,128)S(1)}, u32[]{:S(2)}, u32[]{:S(2)}) collective-permute-start(f32[4,16,128]{2,1,0:T(8,128)S(1)} %get-tuple-element.35), channel_id=1, source_target_pairs={{0,8},{1,9},{2,4},{3,5},{4,2},{5,3},{6,14},{7,15},{8,0},{9,1},{10,... | collective-permute-start | bytes 98312 | tf_op jit(solution)/shard_map/faces_in/ppermute | solution.py:38
  7.0 3.8 %copy-start.6 = (bf16[480,256]{1,0:T(8,128)(2,1)S(1)}, bf16[480,256]{1,0:T(8,128)(2,1)}, u32[]{:S(2)}) copy-start(bf16[480,256]{1,0:T(8,128)(2,1)} %constant.19.clone.into) | copy-start | bytes 737284
  7.0 3.9 %copy-start.7 = (bf16[384,256]{1,0:T(8,128)(2,1)S(1)}, bf16[384,256]{1,0:T(8,128)(2,1)}, u32[]{:S(2)}) copy-start(bf16[384,256]{1,0:T(8,128)(2,1)} %constant.20.clone.back) | copy-start | bytes 589828
  7.0 3.9 %copy-start.8 = (bf16[256,256]{1,0:T(8,128)(2,1)S(1)}, bf16[256,256]{1,0:T(8,128)(2,1)}, u32[]{:S(2)}) copy-start(bf16[256,256]{1,0:T(8,128)(2,1)} %constant.22.clone.out) | copy-start | bytes 393220
  7.0 3.8 %collective-permute-start.4 = (f32[8,512]{1,0:T(8,128)S(1)}, f32[8,512]{1,0:T(8,128)S(1)}, u32[]{:S(2)}, u32[]{:S(2)}) collective-permute-start(f32[8,512]{1,0:T(8,128)S(1)} %get-tuple-element.36), channel_id=1, source_target_pairs={{0,1},{1,0},{2,3},{3,2},{4,5},{5,4},{6,7},{7,6},{8,9},{9,8},{10,11... | collective-permute-start | bytes 49160 | tf_op jit(solution)/shard_map/faces_in/ppermute | solution.py:38
  8.6 2.3 %copy-start.10 = (f32[40,128]{1,0:T(8,128)S(1)}, f32[40,128]{1,0:T(8,128)}, u32[]{:S(2)}) copy-start(f32[40,128]{1,0:T(8,128)} %constant.21.clone.rim) | copy-start | bytes 61444
  8.6 2.3 %copy-start.11 = (bf16[32,256]{1,0:T(8,128)(2,1)S(1)}, bf16[32,256]{1,0:T(8,128)(2,1)}, u32[]{:S(2)}) copy-start(bf16[32,256]{1,0:T(8,128)(2,1)} %constant.23.clone.out_ends) | copy-start | bytes 49156
  8.6 2.3 %copy-start.12 = (bf16[16,256]{1,0:T(8,128)(2,1)S(1)}, bf16[16,256]{1,0:T(8,128)(2,1)}, u32[]{:S(2)}) copy-start(bf16[16,256]{1,0:T(8,128)(2,1)} %constant.18.clone.face_table) | copy-start | bytes 24580
  12.6 7.5 %collective-permute-start.5 = (f32[2,32,128]{2,1,0:T(8,128)S(1)}, f32[2,32,128]{2,1,0:T(8,128)S(1)}, u32[]{:S(2)}, u32[]{:S(2)}) collective-permute-start(f32[2,32,128]{2,1,0:T(8,128)S(1)} %get-tuple-element.42.tx0), channel_id=1, source_target_pairs={{0,8},{1,9},{2,10},{3,11},{4,12},{5,13},{6,14},{7,15},{8,0},{9,1},... | collective-permute-start | bytes 98312 | tf_op jit(solution)/shard_map/faces_out/ppermute | solution.py:38
  12.7 7.5 %collective-permute-start.6 = (f32[2,32,128]{2,1,0:T(8,128)S(1)}, f32[2,32,128]{2,1,0:T(8,128)S(1)}, u32[]{:S(2)}, u32[]{:S(2)}) collective-permute-start(f32[2,32,128]{2,1,0:T(8,128)S(1)} %get-tuple-element.43.tx1), channel_id=1, source_target_pairs={{0,24},{1,25},{2,26},{3,27},{4,28},{5,29},{6,30},{7,31},{8,16},{9,... | collective-permute-start | bytes 98312 | tf_op jit(solution)/shard_map/faces_out/ppermute | solution.py:38
  13.3 5.8 %collective-permute-start.7 = (f32[2,16,128]{2,1,0:T(8,128)S(1)}, f32[2,16,128]{2,1,0:T(8,128)S(1)}, u32[]{:S(2)}, u32[]{:S(2)}) collective-permute-start(f32[2,16,128]{2,1,0:T(8,128)S(1)} %get-tuple-element.44.ty0), channel_id=1, source_target_pairs={{0,2},{1,3},{2,0},{3,1},{4,6},{5,7},{6,4},{7,5},{8,10},{9,11},{10,... | collective-permute-start | bytes 49160 | tf_op jit(solution)/shard_map/faces_out/ppermute | solution.py:38
  16.4 2.7 %collective-permute-start.8 = (f32[2,16,128]{2,1,0:T(8,128)S(1)}, f32[2,16,128]{2,1,0:T(8,128)S(1)}, u32[]{:S(2)}, u32[]{:S(2)}) collective-permute-start(f32[2,16,128]{2,1,0:T(8,128)S(1)} %get-tuple-element.45.ty1), channel_id=1, source_target_pairs={{0,8},{1,9},{2,4},{3,5},{4,2},{5,3},{6,14},{7,15},{8,0},{9,1},{10,... | collective-permute-start | bytes 49160 | tf_op jit(solution)/shard_map/faces_out/ppermute | solution.py:38
  16.4 3.7 %collective-permute-start.9 = (f32[8,512]{1,0:T(8,128)S(1)}, f32[8,512]{1,0:T(8,128)S(1)}, u32[]{:S(2)}, u32[]{:S(2)}) collective-permute-start(f32[8,512]{1,0:T(8,128)S(1)} %get-tuple-element.46.tz), channel_id=1, source_target_pairs={{0,1},{1,0},{2,3},{3,2},{4,5},{5,4},{6,7},{7,6},{8,9},{9,8},{10,11... | collective-permute-start | bytes 49160 | tf_op jit(solution)/shard_map/faces_out/ppermute | solution.py:38
  20.1 11.4 %copy-start.3 = (f32[16,32,128]{2,1,0:T(8,128)S(1)}, f32[16,32,128]{2,1,0:T(8,128)}, u32[]{:S(2)}) copy-start(f32[16,32,128]{2,1,0:T(8,128)} %res.1) | copy-start | bytes 786436
  20.1 11.4 %copy-start.5 = (f32[16,32,128]{2,1,0:T(8,128)S(1)}, f32[16,32,128]{2,1,0:T(8,128)}, u32[]{:S(2)}) copy-start(f32[16,32,128]{2,1,0:T(8,128)} %iterate.1) | copy-start | bytes 786436

commit v6 on v5

--- a/solution.py
+++ b/solution.py
@@ -17,6 +17,7 @@
 SMEM = pl.BlockSpec(memory_space=pltpu.SMEM)
 LANES = 256
 GROUP = 6
+FOUR = 4
 
 
 def swaps(axis, turn):
@@ -94,13 +95,17 @@
     ends[:, :nz] = qz[[0, -1]]
     fh, fl = np_halves(forward)
     eh, el = np_halves(ends)
-    face = np.zeros((16, LANES), ml_dtypes.bfloat16)
-    face[0:2], face[2:4], face[4:6] = eh, eh, el
     out_ends = np.zeros((32, LANES), ml_dtypes.bfloat16)
     out_ends[0:2], out_ends[16:18] = eh, el
-    into = np.zeros((GROUP * pad, LANES))
-    for s in range(GROUP):
+    into = np.zeros((FOUR * pad, FOUR * size_y))
+    for s in range(FOUR):
         into[s * pad : s * pad + ny, s * size_y : (s + 1) * size_y] = qy[1:-1].T
+    ih, il = np_halves(into)
+    one = np.zeros((-(-pad // 16) * 16, FOUR * size_y), ml_dtypes.bfloat16)
+    for k, half in enumerate((ih, il, ih)):
+        one[:pad, k * size_y : (k + 1) * size_y] = half[:pad, :size_y]
+    row_ends = np.zeros((8, LANES))
+    row_ends[:2] = ends
     rim = np.zeros((pad, LANES // 2))
     rim[:ny, 0], rim[:ny, 1] = qy[0], qy[-1]
     back = np.zeros((GROUP * size_y, LANES))
@@ -109,13 +114,13 @@
     middle = np.full((pad, LANES), 2.0)
     middle[:ny, :nz] += ly[:, None] + lz[None, :]
     middle[ny:], middle[:, nz:] = 4.0, 4.0
-    ih, il = np_halves(into)
     bh, bl = np_halves(back)
     return dict(
         fwd=np.concatenate([fh, fl]),
         middle=middle.astype(np.float32),
-        face=face,
-        into=np.concatenate([ih, il]),
+        into=np.concatenate([ih, il], axis=1),
+        one=one,
+        row_ends=row_ends.astype(np.float32),
         back=np.concatenate([bh, bl]),
         rim=rim.astype(np.float32),
         out=np.concatenate([np.ascontiguousarray(fh.T), np.ascontiguousarray(fl.T)], axis=1),
@@ -171,16 +176,27 @@
 
 def along_z(rows, fwd, size_z):
     high, low = halves(rows)
-    table = fwd[:size_z]
-    return dot(jnp.concatenate([high, low], axis=1), jnp.concatenate([table, table], axis=0)) + dot(high, fwd[size_z:])
-
-
-def own_kernel(masked, msk, direction, mu, fwd, middle, work, mask, d, factors, scale):
+    both = jnp.concatenate([high, low], axis=1)
+    table = jnp.concatenate([fwd[:size_z], fwd[:size_z]], axis=0)
+    half = rows.shape[0] // 32 * 16
+    parts = [dot(both[part], table) + dot(high[part], fwd[size_z:]) for part in (slice(0, half), slice(half, None))]
+    return jnp.concatenate(parts, axis=0)
+
+
+def own_kernel(masked, msk, direction, mu, middle, into, modes, mask, d, factors, scale):
     size_x, size_y, size_z = masked.shape
     mask[...] = msk[...].astype(F32)
     d[...] = mask[...] * direction[...]
-    work[...] = along_z(masked[...].reshape(size_x * size_y, size_z), fwd, size_z)
-    pad = middle.shape[0]
+    pad, depth = middle.shape[0], FOUR * size_y
+    high, low = halves(masked[...].reshape(size_x * size_y, size_z))
+    table = jnp.concatenate([into[...], into[:, :depth]], axis=1)
+    for g in range(0, size_x // FOUR, 2):
+        pair = []
+        for part in (slice(g * depth, (g + 1) * depth), slice((g + 1) * depth, (g + 2) * depth)):
+            pair.append(jnp.concatenate([high[part], high[part], low[part]], axis=0))
+        value = dot(table, jnp.concatenate(pair, axis=1))
+        modes[g * FOUR * pad : (g + 1) * FOUR * pad] = value[:, :size_z]
+        modes[(g + 1) * FOUR * pad : (g + 2) * FOUR * pad] = value[:, size_z:]
     along = middle[...]
     previous = 1.0 / along
     factors[0:pad] = previous
@@ -191,7 +207,7 @@
 
 
 def solve_kernel(
-    work, factors, scale, mask, rx0, rx1, ry0, ry1, rz, fwd, face_table, into, back, rim, out, out_ends,
+    modes, factors, scale, mask, rx0, rx1, ry0, ry1, rz, fwd, into, one, row_ends, back, rim, out, out_ends,
     own, tx0, tx1, ty0, ty1, tz,
 ):
     size_x, size_y, size_z = mask.shape
@@ -202,33 +218,40 @@
     even_z = where_z[0]
     x_low, x_high = sides(rx0[0:2], rx1[0:2], where_x)
     y_low, y_high = sides(ry0[0:2], ry1[0:2], where_y)
-    edge = along_z(jnp.concatenate([x_low[0], x_high[0], y_low[0], y_high[0]], axis=0), fwd, size_z)
-    line = rz[0:1]
-    line_h, line_l = halves(line)
-    at = iota((16, rows), 0)
-    mine = (at < 6) & (at % 2 == jnp.where(even_z, 1, 0))
-    line = jnp.where(mine, jnp.where(at // 2 == 1, line_l.astype(F32), line_h.astype(F32)), 0.0)
-    face = dot_rows(line.astype(BF16), face_table[...])
-    box = jnp.concatenate([edge[:size_y], work[...] + face, edge[size_y : 2 * size_y]], axis=0)
-    box_h, box_l = halves(box)
-    modes = []
-    into_h, into_l = into[: GROUP * pad, : GROUP * size_y], into[GROUP * pad :, : GROUP * size_y]
-    for g in range(nx // GROUP):
-        part = slice(g * GROUP * size_y, (g + 1) * GROUP * size_y)
-        modes.append(dot(into_h, box_h[part]) + dot(into_l, box_h[part]) + dot(into_h, box_l[part]))
-    modes = jnp.concatenate(modes, axis=0)
-    rim_low, rim_high = (jnp.broadcast_to(rim[:, k : k + 1], (pad, LANES)) for k in (0, 1))
+    depth, count = FOUR * size_y, size_x // FOUR
+    line_h, line_l = halves(rz[0:1])
+    at = iota((16, depth), 0)
+    lines = jnp.zeros((16, depth), F32)
+    for g in range(count):
+        part = slice(g * depth, (g + 1) * depth)
+        lines = jnp.where(at == g, line_h[:, part].astype(F32), lines)
+        lines = jnp.where(at == count + g, line_l[:, part].astype(F32), lines)
+    lines = lines.astype(BF16)
+    face_h, face_l = dot_lanes(into[:, :depth], lines), dot_lanes(into[:, depth:], lines)
+    face = face_h[:, :count] + face_h[:, count : 2 * count] + face_l[:, :count]
+    end = jnp.where(even_z, row_ends[1:2], row_ends[0:1])
+    side_h, side_l = halves(jnp.concatenate([x_low[0], x_high[0]], axis=1))
+    rest = jnp.zeros((one.shape[1] - 3 * size_y, 2 * size_z), BF16)
+    ghosts = dot(one[...], jnp.concatenate([side_h, side_h, side_l, rest], axis=0))
+    rim_low, rim_high = (jnp.broadcast_to(rim[:, k : k + 1], (pad, size_z)) for k in (0, 1))
+    slabs = [ghosts[:pad, :size_z]]
+    for i in range(size_x):
+        value = modes[i * pad : (i + 1) * pad]
+        slabs.append(value + rim_low * y_low[0][i : i + 1] + rim_high * y_high[0][i : i + 1])
+    slabs.append(ghosts[:pad, size_z:])
+    values = along_z(jnp.concatenate(slabs, axis=0), fwd, size_z)
     solved = []
     for i in range(nx):
-        value = modes[i * pad : (i + 1) * pad]
+        value = values[i * pad : (i + 1) * pad]
         if 0 < i < nx - 1:
-            at = 2 * size_y + i - 1
-            value = value + rim_low * edge[at : at + 1] + rim_high * edge[at + size_x : at + size_x + 1]
+            g, k = divmod(i - 1, FOUR)
+            value = value + face[k * pad : (k + 1) * pad, g : g + 1] * end
         if i:
             value = value + solved[-1]
         solved.append(value * factors[i * pad : (i + 1) * pad])
     for i in reversed(range(nx - 1)):
         solved[i] = solved[i] + factors[i * pad : (i + 1) * pad] * solved[i + 1]
+    rim_low, rim_high = (jnp.broadcast_to(rim[:, k : k + 1], (pad, LANES)) for k in (0, 1))
     solved = jnp.concatenate(solved, axis=0)
     high, low = halves(solved)
     rest = jnp.zeros((LANES - GROUP * pad, LANES), BF16)
@@ -244,8 +267,12 @@
     local = jnp.concatenate(local, axis=0)
     local = local * scale[0:1, 0:1]
     high, low = halves(local)
-    both = dot(high, out[...])
-    local = both[:, :size_z] + both[:, size_z:] + dot(low, out[:, :size_z])
+    half = high.shape[0] // 32 * 16
+    parts = []
+    for part in (slice(0, half), slice(half, None)):
+        both = dot(high[part], out[...])
+        parts.append(both[:, :size_z] + both[:, size_z:] + dot(low[part], out[:, :size_z]))
+    local = jnp.concatenate(parts, axis=0)
     own_h, own_l = high[size_y : size_y + rows], low[size_y : size_y + rows]
     face = dot_lanes(out_ends[0:16], own_h) + dot_lanes(out_ends[0:16], own_l) + dot_lanes(out_ends[16:32], own_h)
 
@@ -282,7 +309,10 @@
     x_at, y_at = ids // size_y, ids % size_y
     kept = (x_at >= 1) & (x_at <= size_x - 2) & (y_at >= 1) & (y_at <= size_y - 2)
     ghost = jnp.where(kept, jnp.where(even_z, face[1:2], face[0:1]) * rz[1:2], 0.0)
-    tz[...] = jnp.where(iota((8, rows), 0) == 1, jnp.broadcast_to(ghost, (8, rows)), mine)
+    for unused in (tx1, ty0, ty1):
+        unused[2:] = jnp.zeros((unused.shape[0] - 2, *unused.shape[1:]), F32)
+    tz[8:] = jnp.zeros((tz.shape[0] - 8, rows), F32)
+    tz[0:8] = jnp.where(iota((8, rows), 0) == 1, jnp.broadcast_to(ghost, (8, rows)), mine)
 
 
 def stencil(slabs, y_low, y_high, faces, links, box):
@@ -345,8 +375,8 @@
     where_x, where_y, where_z = (place(axis) for axis in AXES)
     x_sent = sides(tx0[1], tx1[1], where_x)
     y_sent = sides(ty0[1], ty1[1], where_y)
-    x_got = sides(qx0[...], qx1[...], where_x)
-    y_got = sides(qy0[...], qy1[...], where_y)
+    x_got = sides(qx0[0:2], qx1[0:2], where_x)
+    y_got = sides(qy0[0:2], qy1[0:2], where_y)
     face, more = (
         wide.reshape(box) for wide in lane_ends([qz[0:1] + tz[1:2], qz[1:2]], where_z[0], size_z)
     )
@@ -434,7 +464,11 @@
     def faces(count):
         return [(count, size_y, size_z)] * 2 + [(count, size_x, size_z)] * 2 + [(8, rows)]
 
-    fwd, middle, *tables = map(jnp.asarray, solve_tables(size_x, size_y, size_z).values())
+    layer = size_y * size_z
+    made_faces = [(2, size_y, size_z), (3, size_y, size_z)]
+    made_faces += [(3 * size_y // size_x, size_x, size_z)] * 2 + [(3 * layer // rows, rows)]
+
+    fwd, middle, into, *tables = map(jnp.asarray, solve_tables(size_x, size_y, size_z).values())
     with jax.named_scope("masks"):
         masked = unfixed_node_mask.astype(F32) * residual
         mu = permeability
@@ -443,11 +477,12 @@
     with jax.named_scope("faces_in"):
         near = exchange(*sent)
     with jax.named_scope("own_part"):
-        modes = ((size_x + 2) * middle.shape[0], LANES)
-        args = (masked, unfixed_node_mask, direction, mu, fwd, middle)
-        work, mask, d, *part = call(own_kernel, args, [(rows, LANES), box, box, modes, (8, size_z)])
+        pad = middle.shape[0]
+        args = (masked, unfixed_node_mask, direction, mu, middle, into)
+        outs = [(size_x * pad, size_z), box, box, ((size_x + 2) * pad, LANES), (8, size_z)]
+        modes, mask, d, *part = call(own_kernel, args, outs)
     with jax.named_scope("solve"):
-        own, *made = call(solve_kernel, (work, *part, mask, *near, fwd, *tables), [box] + faces(2))
+        own, *made = call(solve_kernel, (modes, *part, mask, *near, fwd, into, *tables), [box] + made_faces)
     with jax.named_scope("faces_out"):
         got = exchange(*made)
     with jax.named_scope("links"):

time: 33 us -> 32.3 us (0.979)
  blocking collectives: 10.6 us -> 10.2 us
  waiting for transfers between devices: 2.84 us -> 3.17 us
    all_to_all x1, blocking collectives: 10.6 us -> 10.2 us  [shards(): sums = lax.all_to_all(sums, AXES, 0, 0, tiled=True)]
where the time goes in v6:
time: 32.3 us; the launch traced here: 32.1 us
  starting transfers between devices  11.2 us (35%)
  blocking collectives  10.2 us (32%)
  Pallas kernels  4.75 us (15%)
  waiting for transfers between devices  3.17 us (10%)
  between operations  1.49 us (5%)
  other arithmetic  1.14 us (4%)
    ppermute x10, starting transfers between devices, swap(): return lax.ppermute(block, AXES, swaps(axis, turn))  11.2 us
    all_to_all x1, blocking collectives, shards(): sums = lax.all_to_all(sums, AXES, 0, 0, tiled=True)  10.2 us
    pallas_call x6, Pallas kernels, call(): pl.pallas_call(kernel, out_shape=outs, in_specs=specs or [VMEM] * len(arg...  4.75 us
    ppermute x10, waiting for transfers between devices, swap(): return lax.ppermute(block, AXES, swaps(axis, turn))  3.17 us
    mul x1, other arithmetic, shards(): masked = unfixed_node_mask.astype(F32) * residual  1.14 us
  transfers between devices with their start and end apart: 10, of which 2 were waited for; matrix products, arithmetic and copies ran while one was open for 0% of the time, Pallas kernels for 3%

profile of v6, /device:TPU:0, one launch (start us, length us, event | category | flops | bytes accessed | tf_op | source)
XLA Modules:
  0.0 32.1 jit_solution(15727836185961250086)
XLA Ops:
  0.7 1.1 %convert_multiply_fusion.masked = f32[16,32,128]{2,1,0:T(8,128)S(1)} fusion(f32[16,32,128]{2,1,0:T(8,128)} %res.1, s32[16,32,128]{2,1,0:T(8,128)} %msk.3), kind=kLoop, calls=%fused_computation | loop fusion | flops 131072 | bytes 786432 | tf_op jit(solution)/shard_map/masks/mul | solution.py:473
  1.8 0.0 copy-done.1
  1.8 0.1 copy-done.3
  1.9 0.4 %pack.1 = (f32[4,32,128]{2,1,0:T(8,128)S(1)}, f32[4,32,128]{2,1,0:T(8,128)S(1)}, f32[4,16,128]{2,1,0:T(8,128)S(1)}, f32[4,16,128]{2,1,0:T(8,128)S(1)}, f32[8,512]{1,0:T(8,128)S(1)}) custom-call(f32[16,32,128]{2,1,0:T(8,128)S(1)} %convert_multiply_fusion.masked, s32[16,32,128]{2,1,0:T(8,128)S(1)} %copy-done, f32[16,32,128]{2,1,0:T(8,128)S(1)} %copy-done.3, ...), custom_call_target="tpu_custom_call" | custom-call | bytes 1048576 | tf_op jit(solution)/shard_map/pack/pallas_call | solution.py:436
  2.3 0.5 %collective-permute-start = (f32[4,32,128]{2,1,0:T(8,128)S(1)}, f32[4,32,128]{2,1,0:T(8,128)S(1)}, u32[]{:S(2)}, u32[]{:S(2)}) collective-permute-start(f32[4,32,128]{2,1,0:T(8,128)S(1)} %get-tuple-element.32), channel_id=1, source_target_pairs={{0,8},{1,9},{2,10},{3,11},{4,12},{5,13},{6,14},{7,15},{8,0},{9,1},... | collective-permute-start | bytes 196616 | tf_op jit(solution)/shard_map/faces_in/ppermute | solution.py:39
  2.8 2.6 %collective-permute-start.1 = (f32[4,32,128]{2,1,0:T(8,128)S(1)}, f32[4,32,128]{2,1,0:T(8,128)S(1)}, u32[]{:S(2)}, u32[]{:S(2)}) collective-permute-start(f32[4,32,128]{2,1,0:T(8,128)S(1)} %get-tuple-element.33), channel_id=1, source_target_pairs={{0,24},{1,25},{2,26},{3,27},{4,28},{5,29},{6,30},{7,31},{8,16},{9,... | collective-permute-start | bytes 196616 | tf_op jit(solution)/shard_map/faces_in/ppermute | solution.py:39
  5.4 1.6 %collective-permute-start.2 = (f32[4,16,128]{2,1,0:T(8,128)S(1)}, f32[4,16,128]{2,1,0:T(8,128)S(1)}, u32[]{:S(2)}, u32[]{:S(2)}) collective-permute-start(f32[4,16,128]{2,1,0:T(8,128)S(1)} %get-tuple-element.34), channel_id=1, source_target_pairs={{0,2},{1,3},{2,0},{3,1},{4,6},{5,7},{6,4},{7,5},{8,10},{9,11},{10,... | collective-permute-start | bytes 98312 | tf_op jit(solution)/shard_map/faces_in/ppermute | solution.py:39
  7.0 0.0 collective-permute-start.3
  7.0 1.6 %collective-permute-start.4 = (f32[8,512]{1,0:T(8,128)S(1)}, f32[8,512]{1,0:T(8,128)S(1)}, u32[]{:S(2)}, u32[]{:S(2)}) collective-permute-start(f32[8,512]{1,0:T(8,128)S(1)} %get-tuple-element.36), channel_id=1, source_target_pairs={{0,1},{1,0},{2,3},{3,2},{4,5},{5,4},{6,7},{7,6},{8,9},{9,8},{10,11... | collective-permute-start | bytes 49160 | tf_op jit(solution)/shard_map/faces_in/ppermute | solution.py:39
  8.6 0.0 copy-start.12
  8.6 0.0 copy-start.13
  8.6 0.3 %own_part.1 = (f32[640,128]{1,0:T(8,128)S(1)}, f32[16,32,128]{2,1,0:T(8,128)S(1)}, f32[16,32,128]{2,1,0:T(8,128)S(1)}, f32[720,256]{1,0:T(8,128)S(1)}, f32[8,128]{1,0:T(8,128)S(1)}) custom-call(f32[16,32,128]{2,1,0:T(8,128)S(1)} %convert_multiply_fusion.masked, s32[16,32,128]{2,1,0:T(8,128)S(1)} %copy-done, f32[16,32,128]{2,1,0:T(8,128)S(1)} %copy-done.3, ...), custom_call_target="tpu_custom_call" | custom-call | bytes 1048576 | tf_op jit(solution)/shard_map/own_part/pallas_call | solution.py:436
  8.9 1.8 %collective-permute-done.4.rz = f32[8,512]{1,0:T(8,128)S(1)} collective-permute-done((f32[8,512]{1,0:T(8,128)S(1)}, f32[8,512]{1,0:T(8,128)S(1)}, u32[]{:S(2)}, u32[]{:S(2)}) %collective-permute-start.4) | collective-permute-done | bytes 16416 | tf_op jit(solution)/shard_map/faces_in/ppermute | solution.py:39
  10.8 0.0 collective-permute-done.2.ry0
  10.8 0.0 collective-permute-done.3.ry1
  10.8 0.0 collective-permute-done.rx0
  10.8 0.0 collective-permute-done.1.rx1
  10.9 1.5 %solve.1 = (f32[16,32,128]{2,1,0:T(8,128)S(1)}, f32[2,32,128]{2,1,0:T(8,128)S(1)}, f32[3,32,128]{2,1,0:T(8,128)S(1)}, f32[6,16,128]{2,1,0:T(8,128)S(1)}, f32[6,1...) custom-call(f32[640,128]{1,0:T(8,128)S(1)} %get-tuple-element.38.modes, f32[720,256]{1,0:T(8,128)S(1)} %get-tuple-element.39.factors, ...), custom_call_target="tpu_custom_call" | custom-call | bytes 1048576 | tf_op jit(solution)/shard_map/solve/pallas_call | solution.py:436
  12.4 0.0 collective-permute-start.6
  12.4 3.1 %collective-permute-start.7 = (f32[6,16,128]{2,1,0:T(8,128)S(1)}, f32[6,16,128]{2,1,0:T(8,128)S(1)}, u32[]{:S(2)}, u32[]{:S(2)}) collective-permute-start(f32[6,16,128]{2,1,0:T(8,128)S(1)} %get-tuple-element.44.ty0), channel_id=1, source_target_pairs={{0,2},{1,3},{2,0},{3,1},{4,6},{5,7},{6,4},{7,5},{8,10},{9,11},{10,... | collective-permute-start | bytes 147464 | tf_op jit(solution)/shard_map/faces_out/ppermute | solution.py:39
  15.5 0.3 collective-permute-start.8
  15.8 1.5 %collective-permute-start.9 = (f32[24,512]{1,0:T(8,128)S(1)}, f32[24,512]{1,0:T(8,128)S(1)}, u32[]{:S(2)}, u32[]{:S(2)}) collective-permute-start(f32[24,512]{1,0:T(8,128)S(1)} %get-tuple-element.46.tz), channel_id=1, source_target_pairs={{0,1},{1,0},{2,3},{3,2},{4,5},{5,4},{6,7},{7,6},{8,9},{9,8},{10,11... | collective-permute-start | bytes 147464 | tf_op jit(solution)/shard_map/faces_out/ppermute | solution.py:39
  17.4 0.0 collective-permute-start.5
  18.0 0.6 %links.1 = (f32[16,32,128]{2,1,0:T(8,128)S(1)}, f32[17,32,128]{2,1,0:T(8,128)S(1)}, f32[16,32,128]{2,1,0:T(8,128)S(1)}, f32[16,128]{1,0:T(8,128)S(1)}, f32[16,32...) custom-call(f32[1]{0:T(128)S(6)} %copy.18.rz_prev, ...), custom_call_target="tpu_custom_call" | custom-call | bytes 1048576 | tf_op jit(solution)/shard_map/links/pallas_call | solution.py:436
  18.6 0.0 collective-permute-done.5.qx0
  18.6 0.0 collective-permute-done.6.qx1
  18.6 0.0 collective-permute-done.7.qy0
  18.6 0.0 collective-permute-done.8.qy1
  18.6 1.3 %collective-permute-done.9.qz = f32[24,512]{1,0:T(8,128)S(1)} collective-permute-done((f32[24,512]{1,0:T(8,128)S(1)}, f32[24,512]{1,0:T(8,128)S(1)}, u32[]{:S(2)}, u32[]{:S(2)}) %collective-permute-start.9) | collective-permute-done | bytes 49184 | tf_op jit(solution)/shard_map/faces_out/ppermute | solution.py:39
  19.9 0.7 %image.1 = (f32[16,32,128]{2,1,0:T(8,128)S(1)}, f32[16,32,128]{2,1,0:T(8,128)S(1)}, f32[32,1,128]{2,1,0:T(1,128)S(1)}) custom-call(f32[16,32,128]{2,1,0:T(8,128)S(1)} %convert_multiply_fusion.masked, f32[16,32,128]{2,1,0:T(8,128)S(1)} %get-tuple-element.30.mask, f32[16,32,128]{2,1,0:T(8,128)S(1)} %get-tuple-element.31.d, ...), custom_call_target="tpu_custom_call" | custom-call | bytes 1048576 | tf_op jit(solution)/shard_map/image/pallas_call | solution.py:436
  20.6 10.2 %all_to_all.5.sums = f32[32,1,128]{2,1,0:T(1,128)S(1)} all-to-all(f32[32,1,128]{2,1,0:T(1,128)S(1)} %get-tuple-element.54), channel_id=1, replica_groups=mesh['gx'=4,'gy'=4,'gz'=2] {'gx','gy','gz'}, dimensions={0} | all-to-all | bytes 32768 | tf_op jit(solution)/shard_map/sums/all_to_all | solution.py:494
  30.9 1.3 %update.1 = (f32[16,32,128]{2,1,0:T(8,128)}, f32[16,32,128]{2,1,0:T(8,128)}, f32[16,32,128]{2,1,0:T(8,128)}) custom-call(f32[1,128]{1,0:T(1,128)S(1)} %get-tuple-element.37.rz_line, f32[32,1,128]{2,1,0:T(1,128)S(1)} %all_to_all.5.sums, f32[16,32,128]{2,1,0:T(8,128)S(1)} %copy-done.5, f32[16,32,128]{2,1,0:T(8,128)S(1)} %copy-done.2, ...), custom_call_target="tpu_custom_call" | custom-call | bytes 1048576 | tf_op jit(solution)/shard_map/update/pallas_call | solution.py:436
  (24 shorter events, 0.0 us)
Async XLA Ops:
  0.6 1.2 %copy-start = (s32[16,32,128]{2,1,0:T(8,128)S(1)}, s32[16,32,128]{2,1,0:T(8,128)}, u32[]{:S(2)}) copy-start(s32[16,32,128]{2,1,0:T(8,128)} %msk.3) | copy-start | bytes 786436
  0.6 1.2 %copy-start.1 = (f32[16,32,128]{2,1,0:T(8,128)S(1)}, f32[16,32,128]{2,1,0:T(8,128)}, u32[]{:S(2)}) copy-start(f32[16,32,128]{2,1,0:T(8,128)} %mu.5) | copy-start | bytes 786436
  0.7 1.2 %copy-start.3 = (f32[16,32,128]{2,1,0:T(8,128)S(1)}, f32[16,32,128]{2,1,0:T(8,128)}, u32[]{:S(2)}) copy-start(f32[16,32,128]{2,1,0:T(8,128)} %direction.3) | copy-start | bytes 786436
  1.9 6.7 %copy-start.4 = (bf16[160,256]{1,0:T(8,128)(2,1)S(1)}, bf16[160,256]{1,0:T(8,128)(2,1)}, u32[]{:S(2)}) copy-start(bf16[160,256]{1,0:T(8,128)(2,1)} %constant.20.clone.into) | copy-start | bytes 245764
  1.9 6.7 %copy-start.9 = (f32[40,256]{1,0:T(8,128)S(1)}, f32[40,256]{1,0:T(8,128)}, u32[]{:S(2)}) copy-start(f32[40,256]{1,0:T(8,128)} %constant.19.clone.middle) | copy-start | bytes 122884
  2.3 8.5 %collective-permute-start = (f32[4,32,128]{2,1,0:T(8,128)S(1)}, f32[4,32,128]{2,1,0:T(8,128)S(1)}, u32[]{:S(2)}, u32[]{:S(2)}) collective-permute-start(f32[4,32,128]{2,1,0:T(8,128)S(1)} %get-tuple-element.32), channel_id=1, source_target_pairs={{0,8},{1,9},{2,10},{3,11},{4,12},{5,13},{6,14},{7,15},{8,0},{9,1},... | collective-permute-start | bytes 196616 | tf_op jit(solution)/shard_map/faces_in/ppermute | solution.py:39
  2.8 8.0 %collective-permute-start.1 = (f32[4,32,128]{2,1,0:T(8,128)S(1)}, f32[4,32,128]{2,1,0:T(8,128)S(1)}, u32[]{:S(2)}, u32[]{:S(2)}) collective-permute-start(f32[4,32,128]{2,1,0:T(8,128)S(1)} %get-tuple-element.33), channel_id=1, source_target_pairs={{0,24},{1,25},{2,26},{3,27},{4,28},{5,29},{6,30},{7,31},{8,16},{9,... | collective-permute-start | bytes 196616 | tf_op jit(solution)/shard_map/faces_in/ppermute | solution.py:39
  5.4 5.4 %collective-permute-start.2 = (f32[4,16,128]{2,1,0:T(8,128)S(1)}, f32[4,16,128]{2,1,0:T(8,128)S(1)}, u32[]{:S(2)}, u32[]{:S(2)}) collective-permute-start(f32[4,16,128]{2,1,0:T(8,128)S(1)} %get-tuple-element.34), channel_id=1, source_target_pairs={{0,2},{1,3},{2,0},{3,1},{4,6},{5,7},{6,4},{7,5},{8,10},{9,11},{10,... | collective-permute-start | bytes 98312 | tf_op jit(solution)/shard_map/faces_in/ppermute | solution.py:39
  7.0 3.8 %collective-permute-start.3 = (f32[4,16,128]{2,1,0:T(8,128)S(1)}, f32[4,16,128]{2,1,0:T(8,128)S(1)}, u32[]{:S(2)}, u32[]{:S(2)}) collective-permute-start(f32[4,16,128]{2,1,0:T(8,128)S(1)} %get-tuple-element.35), channel_id=1, source_target_pairs={{0,8},{1,9},{2,4},{3,5},{4,2},{5,3},{6,14},{7,15},{8,0},{9,1},{10,... | collective-permute-start | bytes 98312 | tf_op jit(solution)/shard_map/faces_in/ppermute | solution.py:39
  7.0 3.8 %copy-start.6 = (bf16[384,256]{1,0:T(8,128)(2,1)S(1)}, bf16[384,256]{1,0:T(8,128)(2,1)}, u32[]{:S(2)}) copy-start(bf16[384,256]{1,0:T(8,128)(2,1)} %constant.23.clone.back) | copy-start | bytes 589828
  7.0 3.9 %copy-start.7 = (bf16[256,256]{1,0:T(8,128)(2,1)S(1)}, bf16[256,256]{1,0:T(8,128)(2,1)}, u32[]{:S(2)}) copy-start(bf16[256,256]{1,0:T(8,128)(2,1)} %constant.25.clone.out) | copy-start | bytes 393220
  7.0 3.9 %copy-start.8 = (bf16[256,256]{1,0:T(8,128)(2,1)S(1)}, bf16[256,256]{1,0:T(8,128)(2,1)}, u32[]{:S(2)}) copy-start(bf16[256,256]{1,0:T(8,128)(2,1)} %constant.18.clone.fwd) | copy-start | bytes 393220
  7.0 3.8 %collective-permute-start.4 = (f32[8,512]{1,0:T(8,128)S(1)}, f32[8,512]{1,0:T(8,128)S(1)}, u32[]{:S(2)}, u32[]{:S(2)}) collective-permute-start(f32[8,512]{1,0:T(8,128)S(1)} %get-tuple-element.36), channel_id=1, source_target_pairs={{0,1},{1,0},{2,3},{3,2},{4,5},{5,4},{6,7},{7,6},{8,9},{9,8},{10,11... | collective-permute-start | bytes 49160 | tf_op jit(solution)/shard_map/faces_in/ppermute | solution.py:39
  8.6 2.3 %copy-start.10 = (f32[40,128]{1,0:T(8,128)S(1)}, f32[40,128]{1,0:T(8,128)}, u32[]{:S(2)}) copy-start(f32[40,128]{1,0:T(8,128)} %constant.24.clone.rim) | copy-start | bytes 61444
  8.6 2.3 %copy-start.11 = (bf16[32,256]{1,0:T(8,128)(2,1)S(1)}, bf16[32,256]{1,0:T(8,128)(2,1)}, u32[]{:S(2)}) copy-start(bf16[32,256]{1,0:T(8,128)(2,1)} %constant.26.clone.out_ends) | copy-start | bytes 49156
  8.6 2.3 %copy-start.12 = (bf16[48,128]{1,0:T(8,128)(2,1)S(1)}, bf16[48,128]{1,0:T(8,128)(2,1)}, u32[]{:S(2)}) copy-start(bf16[48,128]{1,0:T(8,128)(2,1)} %constant.21.clone.one) | copy-start | bytes 36868
  8.6 2.3 %copy-start.13 = (f32[8,256]{1,0:T(8,128)S(1)}, f32[8,256]{1,0:T(8,128)}, u32[]{:S(2)}) copy-start(f32[8,256]{1,0:T(8,128)} %constant.22.clone.row_ends) | copy-start | bytes 24580
  12.4 6.2 %collective-permute-start.6 = (f32[3,32,128]{2,1,0:T(8,128)S(1)}, f32[3,32,128]{2,1,0:T(8,128)S(1)}, u32[]{:S(2)}, u32[]{:S(2)}) collective-permute-start(f32[3,32,128]{2,1,0:T(8,128)S(1)} %get-tuple-element.43.tx1), channel_id=1, source_target_pairs={{0,24},{1,25},{2,26},{3,27},{4,28},{5,29},{6,30},{7,31},{8,16},{9,... | collective-permute-start | bytes 147464 | tf_op jit(solution)/shard_map/faces_out/ppermute | solution.py:39
  12.4 6.2 %collective-permute-start.7 = (f32[6,16,128]{2,1,0:T(8,128)S(1)}, f32[6,16,128]{2,1,0:T(8,128)S(1)}, u32[]{:S(2)}, u32[]{:S(2)}) collective-permute-start(f32[6,16,128]{2,1,0:T(8,128)S(1)} %get-tuple-element.44.ty0), channel_id=1, source_target_pairs={{0,2},{1,3},{2,0},{3,1},{4,6},{5,7},{6,4},{7,5},{8,10},{9,11},{10,... | collective-permute-start | bytes 147464 | tf_op jit(solution)/shard_map/faces_out/ppermute | solution.py:39
  15.5 3.1 %collective-permute-start.8 = (f32[6,16,128]{2,1,0:T(8,128)S(1)}, f32[6,16,128]{2,1,0:T(8,128)S(1)}, u32[]{:S(2)}, u32[]{:S(2)}) collective-permute-start(f32[6,16,128]{2,1,0:T(8,128)S(1)} %get-tuple-element.45.ty1), channel_id=1, source_target_pairs={{0,8},{1,9},{2,4},{3,5},{4,2},{5,3},{6,14},{7,15},{8,0},{9,1},{10,... | collective-permute-start | bytes 147464 | tf_op jit(solution)/shard_map/faces_out/ppermute | solution.py:39
  15.8 4.1 %collective-permute-start.9 = (f32[24,512]{1,0:T(8,128)S(1)}, f32[24,512]{1,0:T(8,128)S(1)}, u32[]{:S(2)}, u32[]{:S(2)}) collective-permute-start(f32[24,512]{1,0:T(8,128)S(1)} %get-tuple-element.46.tz), channel_id=1, source_target_pairs={{0,1},{1,0},{2,3},{3,2},{4,5},{5,4},{6,7},{7,6},{8,9},{9,8},{10,11... | collective-permute-start | bytes 147464 | tf_op jit(solution)/shard_map/faces_out/ppermute | solution.py:39
  17.4 1.2 %collective-permute-start.5 = (f32[2,32,128]{2,1,0:T(8,128)S(1)}, f32[2,32,128]{2,1,0:T(8,128)S(1)}, u32[]{:S(2)}, u32[]{:S(2)}) collective-permute-start(f32[2,32,128]{2,1,0:T(8,128)S(1)} %get-tuple-element.42.tx0), channel_id=1, source_target_pairs={{0,8},{1,9},{2,10},{3,11},{4,12},{5,13},{6,14},{7,15},{8,0},{9,1},... | collective-permute-start | bytes 98312 | tf_op jit(solution)/shard_map/faces_out/ppermute | solution.py:39
  19.9 10.9 %copy-start.2 = (f32[16,32,128]{2,1,0:T(8,128)S(1)}, f32[16,32,128]{2,1,0:T(8,128)}, u32[]{:S(2)}) copy-start(f32[16,32,128]{2,1,0:T(8,128)} %res.1) | copy-start | bytes 786436
  19.9 10.9 %copy-start.5 = (f32[16,32,128]{2,1,0:T(8,128)S(1)}, f32[16,32,128]{2,1,0:T(8,128)}, u32[]{:S(2)}) copy-start(f32[16,32,128]{2,1,0:T(8,128)} %iterate.1) | copy-start | bytes 786436

commit v7 on v6

--- a/solution.py
+++ b/solution.py
@@ -18,6 +18,7 @@
 LANES = 256
 GROUP = 6
 FOUR = 4
+FILL = {"gx": 2, "gy": 0}
 
 
 def swaps(axis, turn):
@@ -27,8 +28,8 @@
     for source in np.ndindex(*counts):
         target = list(source)
         step = 1 if (source[dim] + turn) % 2 == 0 else -1
-        if axis == "gy" and not 0 <= source[dim] + step < counts[dim]:
-            target[0] ^= 1
+        if not 0 <= source[dim] + step < counts[dim] and axis in FILL:
+            target[FILL[axis]] ^= 1
         else:
             target[dim] = (source[dim] + step) % counts[dim]
         pairs.append(tuple(int(np.ravel_multi_index(where, counts)) for where in (source, target)))

time: 32.3 us -> 31.9 us (0.988)
  blocking collectives: 10.2 us -> 9.64 us
    all_to_all x1, blocking collectives: 10.2 us -> 9.64 us  [shards(): sums = lax.all_to_all(sums, AXES, 0, 0, tiled=True)]
where the time goes in v7:
time: 31.9 us; the launch traced here: 31.7 us
  starting transfers between devices  11.3 us (35%)
  blocking collectives  9.64 us (30%)
  Pallas kernels  4.76 us (15%)
  waiting for transfers between devices  3.28 us (10%)
  between operations  1.48 us (5%)
  other arithmetic  1.14 us (4%)
    ppermute x10, starting transfers between devices, swap(): return lax.ppermute(block, AXES, swaps(axis, turn))  11.3 us
    all_to_all x1, blocking collectives, shards(): sums = lax.all_to_all(sums, AXES, 0, 0, tiled=True)  9.64 us
    pallas_call x6, Pallas kernels, call(): pl.pallas_call(kernel, out_shape=outs, in_specs=specs or [VMEM] * len(arg...  4.76 us
    ppermute x10, waiting for transfers between devices, swap(): return lax.ppermute(block, AXES, swaps(axis, turn))  3.28 us
    mul x1, other arithmetic, shards(): masked = unfixed_node_mask.astype(F32) * residual  1.14 us
  transfers between devices with their start and end apart: 10, of which 2 were waited for; matrix products, arithmetic and copies ran while one was open for 0% of the time, Pallas kernels for 3%

profile of v7, /device:TPU:0, one launch (start us, length us, event | category | flops | bytes accessed | tf_op | source)
XLA Modules:
  0.0 31.7 jit_solution(1612257410281513904)
XLA Ops:
  0.7 1.1 %convert_multiply_fusion.masked = f32[16,32,128]{2,1,0:T(8,128)S(1)} fusion(f32[16,32,128]{2,1,0:T(8,128)} %res.1, s32[16,32,128]{2,1,0:T(8,128)} %msk.3), kind=kLoop, calls=%fused_computation | loop fusion | flops 131072 | bytes 786432 | tf_op jit(solution)/shard_map/masks/mul | solution.py:474
  1.8 0.0 copy-done.1
  1.8 0.1 copy-done.3
  1.9 0.4 %pack.1 = (f32[4,32,128]{2,1,0:T(8,128)S(1)}, f32[4,32,128]{2,1,0:T(8,128)S(1)}, f32[4,16,128]{2,1,0:T(8,128)S(1)}, f32[4,16,128]{2,1,0:T(8,128)S(1)}, f32[8,512]{1,0:T(8,128)S(1)}) custom-call(f32[16,32,128]{2,1,0:T(8,128)S(1)} %convert_multiply_fusion.masked, s32[16,32,128]{2,1,0:T(8,128)S(1)} %copy-done, f32[16,32,128]{2,1,0:T(8,128)S(1)} %copy-done.3, ...), custom_call_target="tpu_custom_call" | custom-call | bytes 1048576 | tf_op jit(solution)/shard_map/pack/pallas_call | solution.py:437
  2.3 0.5 %collective-permute-start = (f32[4,32,128]{2,1,0:T(8,128)S(1)}, f32[4,32,128]{2,1,0:T(8,128)S(1)}, u32[]{:S(2)}, u32[]{:S(2)}) collective-permute-start(f32[4,32,128]{2,1,0:T(8,128)S(1)} %get-tuple-element.32), channel_id=1, source_target_pairs={{0,8},{1,9},{2,10},{3,11},{4,12},{5,13},{6,14},{7,15},{8,0},{9,1},... | collective-permute-start | bytes 196616 | tf_op jit(solution)/shard_map/faces_in/ppermute | solution.py:40
  2.8 2.5 %collective-permute-start.1 = (f32[4,32,128]{2,1,0:T(8,128)S(1)}, f32[4,32,128]{2,1,0:T(8,128)S(1)}, u32[]{:S(2)}, u32[]{:S(2)}) collective-permute-start(f32[4,32,128]{2,1,0:T(8,128)S(1)} %get-tuple-element.33), channel_id=1, source_target_pairs={{0,1},{1,0},{2,3},{3,2},{4,5},{5,4},{6,7},{7,6},{8,16},{9,17},{10,... | collective-permute-start | bytes 196616 | tf_op jit(solution)/shard_map/faces_in/ppermute | solution.py:40
  5.3 1.6 %collective-permute-start.2 = (f32[4,16,128]{2,1,0:T(8,128)S(1)}, f32[4,16,128]{2,1,0:T(8,128)S(1)}, u32[]{:S(2)}, u32[]{:S(2)}) collective-permute-start(f32[4,16,128]{2,1,0:T(8,128)S(1)} %get-tuple-element.34), channel_id=1, source_target_pairs={{0,2},{1,3},{2,0},{3,1},{4,6},{5,7},{6,4},{7,5},{8,10},{9,11},{10,... | collective-permute-start | bytes 98312 | tf_op jit(solution)/shard_map/faces_in/ppermute | solution.py:40
  6.9 0.0 collective-permute-start.3
  6.9 1.3 %collective-permute-start.4 = (f32[8,512]{1,0:T(8,128)S(1)}, f32[8,512]{1,0:T(8,128)S(1)}, u32[]{:S(2)}, u32[]{:S(2)}) collective-permute-start(f32[8,512]{1,0:T(8,128)S(1)} %get-tuple-element.36), channel_id=1, source_target_pairs={{0,1},{1,0},{2,3},{3,2},{4,5},{5,4},{6,7},{7,6},{8,9},{9,8},{10,11... | collective-permute-start | bytes 49160 | tf_op jit(solution)/shard_map/faces_in/ppermute | solution.py:40
  8.3 0.0 copy-start.12
  8.3 0.0 copy-start.13
  8.3 0.3 %own_part.1 = (f32[640,128]{1,0:T(8,128)S(1)}, f32[16,32,128]{2,1,0:T(8,128)S(1)}, f32[16,32,128]{2,1,0:T(8,128)S(1)}, f32[720,256]{1,0:T(8,128)S(1)}, f32[8,128]{1,0:T(8,128)S(1)}) custom-call(f32[16,32,128]{2,1,0:T(8,128)S(1)} %convert_multiply_fusion.masked, s32[16,32,128]{2,1,0:T(8,128)S(1)} %copy-done, f32[16,32,128]{2,1,0:T(8,128)S(1)} %copy-done.3, ...), custom_call_target="tpu_custom_call" | custom-call | bytes 1048576 | tf_op jit(solution)/shard_map/own_part/pallas_call | solution.py:437
  8.6 2.1 %collective-permute-done.4.rz = f32[8,512]{1,0:T(8,128)S(1)} collective-permute-done((f32[8,512]{1,0:T(8,128)S(1)}, f32[8,512]{1,0:T(8,128)S(1)}, u32[]{:S(2)}, u32[]{:S(2)}) %collective-permute-start.4) | collective-permute-done | bytes 16416 | tf_op jit(solution)/shard_map/faces_in/ppermute | solution.py:40
  10.7 0.0 collective-permute-done.2.ry0
  10.7 0.0 collective-permute-done.3.ry1
  10.7 0.0 collective-permute-done.rx0
  10.7 0.0 collective-permute-done.1.rx1
  10.8 1.5 %solve.1 = (f32[16,32,128]{2,1,0:T(8,128)S(1)}, f32[2,32,128]{2,1,0:T(8,128)S(1)}, f32[3,32,128]{2,1,0:T(8,128)S(1)}, f32[6,16,128]{2,1,0:T(8,128)S(1)}, f32[6,1...) custom-call(f32[640,128]{1,0:T(8,128)S(1)} %get-tuple-element.38.modes, f32[720,256]{1,0:T(8,128)S(1)} %get-tuple-element.39.factors, ...), custom_call_target="tpu_custom_call" | custom-call | bytes 1048576 | tf_op jit(solution)/shard_map/solve/pallas_call | solution.py:437
  12.3 1.3 %collective-permute-start.6 = (f32[3,32,128]{2,1,0:T(8,128)S(1)}, f32[3,32,128]{2,1,0:T(8,128)S(1)}, u32[]{:S(2)}, u32[]{:S(2)}) collective-permute-start(f32[3,32,128]{2,1,0:T(8,128)S(1)} %get-tuple-element.43.tx1), channel_id=1, source_target_pairs={{0,1},{1,0},{2,3},{3,2},{4,5},{5,4},{6,7},{7,6},{8,16},{9,17},{10,... | collective-permute-start | bytes 147464 | tf_op jit(solution)/shard_map/faces_out/ppermute | solution.py:40
  13.6 2.3 %collective-permute-start.7 = (f32[6,16,128]{2,1,0:T(8,128)S(1)}, f32[6,16,128]{2,1,0:T(8,128)S(1)}, u32[]{:S(2)}, u32[]{:S(2)}) collective-permute-start(f32[6,16,128]{2,1,0:T(8,128)S(1)} %get-tuple-element.44.ty0), channel_id=1, source_target_pairs={{0,2},{1,3},{2,0},{3,1},{4,6},{5,7},{6,4},{7,5},{8,10},{9,11},{10,... | collective-permute-start | bytes 147464 | tf_op jit(solution)/shard_map/faces_out/ppermute | solution.py:40
  15.9 0.0 collective-permute-start.8
  15.9 1.5 %collective-permute-start.9 = (f32[24,512]{1,0:T(8,128)S(1)}, f32[24,512]{1,0:T(8,128)S(1)}, u32[]{:S(2)}, u32[]{:S(2)}) collective-permute-start(f32[24,512]{1,0:T(8,128)S(1)} %get-tuple-element.46.tz), channel_id=1, source_target_pairs={{0,1},{1,0},{2,3},{3,2},{4,5},{5,4},{6,7},{7,6},{8,9},{9,8},{10,11... | collective-permute-start | bytes 147464 | tf_op jit(solution)/shard_map/faces_out/ppermute | solution.py:40
  17.4 0.2 collective-permute-start.5
  18.3 0.6 %links.1 = (f32[16,32,128]{2,1,0:T(8,128)S(1)}, f32[17,32,128]{2,1,0:T(8,128)S(1)}, f32[16,32,128]{2,1,0:T(8,128)S(1)}, f32[16,128]{1,0:T(8,128)S(1)}, f32[16,32...) custom-call(f32[1]{0:T(128)S(6)} %copy.18.rz_prev, ...), custom_call_target="tpu_custom_call" | custom-call | bytes 1048576 | tf_op jit(solution)/shard_map/links/pallas_call | solution.py:437
  18.9 0.0 collective-permute-done.5.qx0
  18.9 0.0 collective-permute-done.6.qx1
  18.9 0.0 collective-permute-done.7.qy0
  18.9 0.0 collective-permute-done.8.qy1
  18.9 1.1 %collective-permute-done.9.qz = f32[24,512]{1,0:T(8,128)S(1)} collective-permute-done((f32[24,512]{1,0:T(8,128)S(1)}, f32[24,512]{1,0:T(8,128)S(1)}, u32[]{:S(2)}, u32[]{:S(2)}) %collective-permute-start.9) | collective-permute-done | bytes 49184 | tf_op jit(solution)/shard_map/faces_out/ppermute | solution.py:40
  20.1 0.7 %image.1 = (f32[16,32,128]{2,1,0:T(8,128)S(1)}, f32[16,32,128]{2,1,0:T(8,128)S(1)}, f32[32,1,128]{2,1,0:T(1,128)S(1)}) custom-call(f32[16,32,128]{2,1,0:T(8,128)S(1)} %convert_multiply_fusion.masked, f32[16,32,128]{2,1,0:T(8,128)S(1)} %get-tuple-element.30.mask, f32[16,32,128]{2,1,0:T(8,128)S(1)} %get-tuple-element.31.d, ...), custom_call_target="tpu_custom_call" | custom-call | bytes 1048576 | tf_op jit(solution)/shard_map/image/pallas_call | solution.py:437
  20.8 9.6 %all_to_all.5.sums = f32[32,1,128]{2,1,0:T(1,128)S(1)} all-to-all(f32[32,1,128]{2,1,0:T(1,128)S(1)} %get-tuple-element.54), channel_id=1, replica_groups=mesh['gx'=4,'gy'=4,'gz'=2] {'gx','gy','gz'}, dimensions={0} | all-to-all | bytes 32768 | tf_op jit(solution)/shard_map/sums/all_to_all | solution.py:495
  30.4 1.3 %update.1 = (f32[16,32,128]{2,1,0:T(8,128)}, f32[16,32,128]{2,1,0:T(8,128)}, f32[16,32,128]{2,1,0:T(8,128)}) custom-call(f32[1,128]{1,0:T(1,128)S(1)} %get-tuple-element.37.rz_line, f32[32,1,128]{2,1,0:T(1,128)S(1)} %all_to_all.5.sums, f32[16,32,128]{2,1,0:T(8,128)S(1)} %copy-done.5, f32[16,32,128]{2,1,0:T(8,128)S(1)} %copy-done.2, ...), custom_call_target="tpu_custom_call" | custom-call | bytes 1048576 | tf_op jit(solution)/shard_map/update/pallas_call | solution.py:437
  (24 shorter events, 0.0 us)
Async XLA Ops:
  0.6 1.2 %copy-start = (s32[16,32,128]{2,1,0:T(8,128)S(1)}, s32[16,32,128]{2,1,0:T(8,128)}, u32[]{:S(2)}) copy-start(s32[16,32,128]{2,1,0:T(8,128)} %msk.3) | copy-start | bytes 786436
  0.6 1.2 %copy-start.1 = (f32[16,32,128]{2,1,0:T(8,128)S(1)}, f32[16,32,128]{2,1,0:T(8,128)}, u32[]{:S(2)}) copy-start(f32[16,32,128]{2,1,0:T(8,128)} %mu.5) | copy-start | bytes 786436
  0.7 1.2 %copy-start.3 = (f32[16,32,128]{2,1,0:T(8,128)S(1)}, f32[16,32,128]{2,1,0:T(8,128)}, u32[]{:S(2)}) copy-start(f32[16,32,128]{2,1,0:T(8,128)} %direction.3) | copy-start | bytes 786436
  1.9 6.3 %copy-start.4 = (bf16[160,256]{1,0:T(8,128)(2,1)S(1)}, bf16[160,256]{1,0:T(8,128)(2,1)}, u32[]{:S(2)}) copy-start(bf16[160,256]{1,0:T(8,128)(2,1)} %constant.20.clone.into) | copy-start | bytes 245764
  1.9 6.3 %copy-start.9 = (f32[40,256]{1,0:T(8,128)S(1)}, f32[40,256]{1,0:T(8,128)}, u32[]{:S(2)}) copy-start(f32[40,256]{1,0:T(8,128)} %constant.19.clone.middle) | copy-start | bytes 122884
  2.3 8.4 %collective-permute-start = (f32[4,32,128]{2,1,0:T(8,128)S(1)}, f32[4,32,128]{2,1,0:T(8,128)S(1)}, u32[]{:S(2)}, u32[]{:S(2)}) collective-permute-start(f32[4,32,128]{2,1,0:T(8,128)S(1)} %get-tuple-element.32), channel_id=1, source_target_pairs={{0,8},{1,9},{2,10},{3,11},{4,12},{5,13},{6,14},{7,15},{8,0},{9,1},... | collective-permute-start | bytes 196616 | tf_op jit(solution)/shard_map/faces_in/ppermute | solution.py:40
  2.8 7.9 %collective-permute-start.1 = (f32[4,32,128]{2,1,0:T(8,128)S(1)}, f32[4,32,128]{2,1,0:T(8,128)S(1)}, u32[]{:S(2)}, u32[]{:S(2)}) collective-permute-start(f32[4,32,128]{2,1,0:T(8,128)S(1)} %get-tuple-element.33), channel_id=1, source_target_pairs={{0,1},{1,0},{2,3},{3,2},{4,5},{5,4},{6,7},{7,6},{8,16},{9,17},{10,... | collective-permute-start | bytes 196616 | tf_op jit(solution)/shard_map/faces_in/ppermute | solution.py:40
  5.3 5.4 %collective-permute-start.2 = (f32[4,16,128]{2,1,0:T(8,128)S(1)}, f32[4,16,128]{2,1,0:T(8,128)S(1)}, u32[]{:S(2)}, u32[]{:S(2)}) collective-permute-start(f32[4,16,128]{2,1,0:T(8,128)S(1)} %get-tuple-element.34), channel_id=1, source_target_pairs={{0,2},{1,3},{2,0},{3,1},{4,6},{5,7},{6,4},{7,5},{8,10},{9,11},{10,... | collective-permute-start | bytes 98312 | tf_op jit(solution)/shard_map/faces_in/ppermute | solution.py:40
  6.9 3.8 %collective-permute-start.3 = (f32[4,16,128]{2,1,0:T(8,128)S(1)}, f32[4,16,128]{2,1,0:T(8,128)S(1)}, u32[]{:S(2)}, u32[]{:S(2)}) collective-permute-start(f32[4,16,128]{2,1,0:T(8,128)S(1)} %get-tuple-element.35), channel_id=1, source_target_pairs={{0,8},{1,9},{2,4},{3,5},{4,2},{5,3},{6,14},{7,15},{8,0},{9,1},{10,... | collective-permute-start | bytes 98312 | tf_op jit(solution)/shard_map/faces_in/ppermute | solution.py:40
  6.9 3.8 %copy-start.6 = (bf16[384,256]{1,0:T(8,128)(2,1)S(1)}, bf16[384,256]{1,0:T(8,128)(2,1)}, u32[]{:S(2)}) copy-start(bf16[384,256]{1,0:T(8,128)(2,1)} %constant.23.clone.back) | copy-start | bytes 589828
  6.9 3.9 %copy-start.7 = (bf16[256,256]{1,0:T(8,128)(2,1)S(1)}, bf16[256,256]{1,0:T(8,128)(2,1)}, u32[]{:S(2)}) copy-start(bf16[256,256]{1,0:T(8,128)(2,1)} %constant.25.clone.out) | copy-start | bytes 393220
  6.9 3.9 %copy-start.8 = (bf16[256,256]{1,0:T(8,128)(2,1)S(1)}, bf16[256,256]{1,0:T(8,128)(2,1)}, u32[]{:S(2)}) copy-start(bf16[256,256]{1,0:T(8,128)(2,1)} %constant.18.clone.fwd) | copy-start | bytes 393220
  6.9 3.8 %collective-permute-start.4 = (f32[8,512]{1,0:T(8,128)S(1)}, f32[8,512]{1,0:T(8,128)S(1)}, u32[]{:S(2)}, u32[]{:S(2)}) collective-permute-start(f32[8,512]{1,0:T(8,128)S(1)} %get-tuple-element.36), channel_id=1, source_target_pairs={{0,1},{1,0},{2,3},{3,2},{4,5},{5,4},{6,7},{7,6},{8,9},{9,8},{10,11... | collective-permute-start | bytes 49160 | tf_op jit(solution)/shard_map/faces_in/ppermute | solution.py:40
  8.2 2.5 %copy-start.10 = (f32[40,128]{1,0:T(8,128)S(1)}, f32[40,128]{1,0:T(8,128)}, u32[]{:S(2)}) copy-start(f32[40,128]{1,0:T(8,128)} %constant.24.clone.rim) | copy-start | bytes 61444
  8.2 2.5 %copy-start.11 = (bf16[32,256]{1,0:T(8,128)(2,1)S(1)}, bf16[32,256]{1,0:T(8,128)(2,1)}, u32[]{:S(2)}) copy-start(bf16[32,256]{1,0:T(8,128)(2,1)} %constant.26.clone.out_ends) | copy-start | bytes 49156
  8.3 2.5 %copy-start.12 = (bf16[48,128]{1,0:T(8,128)(2,1)S(1)}, bf16[48,128]{1,0:T(8,128)(2,1)}, u32[]{:S(2)}) copy-start(bf16[48,128]{1,0:T(8,128)(2,1)} %constant.21.clone.one) | copy-start | bytes 36868
  8.3 2.5 %copy-start.13 = (f32[8,256]{1,0:T(8,128)S(1)}, f32[8,256]{1,0:T(8,128)}, u32[]{:S(2)}) copy-start(f32[8,256]{1,0:T(8,128)} %constant.22.clone.row_ends) | copy-start | bytes 24580
  12.3 6.6 %collective-permute-start.6 = (f32[3,32,128]{2,1,0:T(8,128)S(1)}, f32[3,32,128]{2,1,0:T(8,128)S(1)}, u32[]{:S(2)}, u32[]{:S(2)}) collective-permute-start(f32[3,32,128]{2,1,0:T(8,128)S(1)} %get-tuple-element.43.tx1), channel_id=1, source_target_pairs={{0,1},{1,0},{2,3},{3,2},{4,5},{5,4},{6,7},{7,6},{8,16},{9,17},{10,... | collective-permute-start | bytes 147464 | tf_op jit(solution)/shard_map/faces_out/ppermute | solution.py:40
  13.6 5.3 %collective-permute-start.7 = (f32[6,16,128]{2,1,0:T(8,128)S(1)}, f32[6,16,128]{2,1,0:T(8,128)S(1)}, u32[]{:S(2)}, u32[]{:S(2)}) collective-permute-start(f32[6,16,128]{2,1,0:T(8,128)S(1)} %get-tuple-element.44.ty0), channel_id=1, source_target_pairs={{0,2},{1,3},{2,0},{3,1},{4,6},{5,7},{6,4},{7,5},{8,10},{9,11},{10,... | collective-permute-start | bytes 147464 | tf_op jit(solution)/shard_map/faces_out/ppermute | solution.py:40
  15.9 3.0 %collective-permute-start.8 = (f32[6,16,128]{2,1,0:T(8,128)S(1)}, f32[6,16,128]{2,1,0:T(8,128)S(1)}, u32[]{:S(2)}, u32[]{:S(2)}) collective-permute-start(f32[6,16,128]{2,1,0:T(8,128)S(1)} %get-tuple-element.45.ty1), channel_id=1, source_target_pairs={{0,8},{1,9},{2,4},{3,5},{4,2},{5,3},{6,14},{7,15},{8,0},{9,1},{10,... | collective-permute-start | bytes 147464 | tf_op jit(solution)/shard_map/faces_out/ppermute | solution.py:40
  15.9 4.2 %collective-permute-start.9 = (f32[24,512]{1,0:T(8,128)S(1)}, f32[24,512]{1,0:T(8,128)S(1)}, u32[]{:S(2)}, u32[]{:S(2)}) collective-permute-start(f32[24,512]{1,0:T(8,128)S(1)} %get-tuple-element.46.tz), channel_id=1, source_target_pairs={{0,1},{1,0},{2,3},{3,2},{4,5},{5,4},{6,7},{7,6},{8,9},{9,8},{10,11... | collective-permute-start | bytes 147464 | tf_op jit(solution)/shard_map/faces_out/ppermute | solution.py:40
  17.4 1.4 %collective-permute-start.5 = (f32[2,32,128]{2,1,0:T(8,128)S(1)}, f32[2,32,128]{2,1,0:T(8,128)S(1)}, u32[]{:S(2)}, u32[]{:S(2)}) collective-permute-start(f32[2,32,128]{2,1,0:T(8,128)S(1)} %get-tuple-element.42.tx0), channel_id=1, source_target_pairs={{0,8},{1,9},{2,10},{3,11},{4,12},{5,13},{6,14},{7,15},{8,0},{9,1},... | collective-permute-start | bytes 98312 | tf_op jit(solution)/shard_map/faces_out/ppermute | solution.py:40
  20.1 10.4 %copy-start.2 = (f32[16,32,128]{2,1,0:T(8,128)S(1)}, f32[16,32,128]{2,1,0:T(8,128)}, u32[]{:S(2)}) copy-start(f32[16,32,128]{2,1,0:T(8,128)} %res.1) | copy-start | bytes 786436
  20.1 10.4 %copy-start.5 = (f32[16,32,128]{2,1,0:T(8,128)S(1)}, f32[16,32,128]{2,1,0:T(8,128)}, u32[]{:S(2)}) copy-start(f32[16,32,128]{2,1,0:T(8,128)} %iterate.1) | copy-start | bytes 786436

commit v8 on v7

--- a/solution.py
+++ b/solution.py
@@ -95,9 +95,11 @@
     ends = np.zeros((2, LANES))
     ends[:, :nz] = qz[[0, -1]]
     fh, fl = np_halves(forward)
-    eh, el = np_halves(ends)
+    last = np.zeros((4, LANES))
+    last[:, :nz] = qz[[1, -2, 0, -1]]
+    oh, ol = np_halves(last)
     out_ends = np.zeros((32, LANES), ml_dtypes.bfloat16)
-    out_ends[0:2], out_ends[16:18] = eh, el
+    out_ends[0:4], out_ends[16:20] = oh, ol
     into = np.zeros((FOUR * pad, FOUR * size_y))
     for s in range(FOUR):
         into[s * pad : s * pad + ny, s * size_y : (s + 1) * size_y] = qy[1:-1].T
@@ -172,7 +174,15 @@
         sy0[f] = jnp.where(even_y, high, low)
         sy1[f] = jnp.where(even_y, low, high)
     flat = [field.reshape(size_x * size_y, size_z) for field in fields(every)]
-    sz[...] = lane_rows(flat, jnp.where(even_z, size_z - 1, 0))
+    lane = jnp.where(even_z, size_z - 1, 0)
+    pick = jnp.where((iota((16, 2 * size_z), 1) % size_z == lane) & (iota((16, 2 * size_z), 0) < 1), 1.0, 0.0).astype(BF16)
+    lines = [dot_lanes(pick, jnp.concatenate(halves(field), axis=1))[0:1] for field in (flat[0], flat[2], flat[3])]
+    lines.insert(1, dot_lanes(pick[:, :size_z], flat[1].astype(BF16))[0:1])
+    at = iota((8, size_x * size_y), 0)
+    total = jnp.zeros(at.shape, F32)
+    for f, line in enumerate(lines):
+        total = jnp.where(at == f, line, total)
+    sz[...] = total
 
 
 def along_z(rows, fwd, size_z):
@@ -208,7 +218,7 @@
 
 
 def solve_kernel(
-    modes, factors, scale, mask, rx0, rx1, ry0, ry1, rz, fwd, into, one, row_ends, back, rim, out, out_ends,
+    modes, factors, scale, mask, sz, rx0, rx1, ry0, ry1, rz, fwd, into, one, row_ends, back, rim, out, out_ends,
     own, tx0, tx1, ty0, ty1, tz,
 ):
     size_x, size_y, size_z = mask.shape
@@ -305,11 +315,11 @@
     ty0[1] = jnp.where(even, g_high, g_low)
     ty1[0] = jnp.where(even, low, high)
     ty1[1] = jnp.where(even, g_low, g_high)
-    mine = lane_rows([own_flat], jnp.where(even_z, size_z - 1, 0))
+    mine = jnp.where(even_z, face[1:2], face[0:1]) * sz[1:2]
     ids = iota((1, rows), 1)
     x_at, y_at = ids // size_y, ids % size_y
     kept = (x_at >= 1) & (x_at <= size_x - 2) & (y_at >= 1) & (y_at <= size_y - 2)
-    ghost = jnp.where(kept, jnp.where(even_z, face[1:2], face[0:1]) * rz[1:2], 0.0)
+    ghost = jnp.where(kept, jnp.where(even_z, face[3:4], face[2:3]) * rz[1:2], 0.0)
     for unused in (tx1, ty0, ty1):
         unused[2:] = jnp.zeros((unused.shape[0] - 2, *unused.shape[1:]), F32)
     tz[8:] = jnp.zeros((tz.shape[0] - 8, rows), F32)
@@ -483,7 +493,7 @@
         outs = [(size_x * pad, size_z), box, box, ((size_x + 2) * pad, LANES), (8, size_z)]
         modes, mask, d, *part = call(own_kernel, args, outs)
     with jax.named_scope("solve"):
-        own, *made = call(solve_kernel, (modes, *part, mask, *near, fwd, into, *tables), [box] + made_faces)
+        own, *made = call(solve_kernel, (modes, *part, mask, sent[-1], *near, fwd, into, *tables), [box] + made_faces)
     with jax.named_scope("faces_out"):
         got = exchange(*made)
     with jax.named_scope("links"):

time: 31.9 us -> 31.8 us (level)
  no operation moved by 1% of the time
where the time goes in v8:
time: 31.8 us; the launch traced here: 31.7 us
  starting transfers between devices  11.3 us (36%)
  blocking collectives  9.64 us (30%)
  Pallas kernels  4.66 us (15%)
  waiting for transfers between devices  3.28 us (10%)
  between operations  1.48 us (5%)
  other arithmetic  1.14 us (4%)
    ppermute x10, starting transfers between devices, swap(): return lax.ppermute(block, AXES, swaps(axis, turn))  11.3 us
    all_to_all x1, blocking collectives, shards(): sums = lax.all_to_all(sums, AXES, 0, 0, tiled=True)  9.64 us
    pallas_call x6, Pallas kernels, call(): pl.pallas_call(kernel, out_shape=outs, in_specs=specs or [VMEM] * len(arg...  4.66 us
    ppermute x10, waiting for transfers between devices, swap(): return lax.ppermute(block, AXES, swaps(axis, turn))  3.28 us
    mul x1, other arithmetic, shards(): masked = unfixed_node_mask.astype(F32) * residual  1.14 us
  transfers between devices with their start and end apart: 10, of which 2 were waited for; matrix products, arithmetic and copies ran while one was open for 0% of the time, Pallas kernels for 3%

profile of v8, /device:TPU:0, one launch (start us, length us, event | category | flops | bytes accessed | tf_op | source)
XLA Modules:
  0.0 31.7 jit_solution(18073270176263978084)
XLA Ops:
  0.7 1.1 %convert_multiply_fusion.masked = f32[16,32,128]{2,1,0:T(8,128)S(1)} fusion(f32[16,32,128]{2,1,0:T(8,128)} %res.1, s32[16,32,128]{2,1,0:T(8,128)} %msk.3), kind=kLoop, calls=%fused_computation | loop fusion | flops 131072 | bytes 786432 | tf_op jit(solution)/shard_map/masks/mul | solution.py:484
  1.8 0.0 copy-done.1
  1.8 0.1 copy-done.3
  1.9 0.4 %pack.1 = (f32[4,32,128]{2,1,0:T(8,128)S(1)}, f32[4,32,128]{2,1,0:T(8,128)S(1)}, f32[4,16,128]{2,1,0:T(8,128)S(1)}, f32[4,16,128]{2,1,0:T(8,128)S(1)}, f32[8,512]{1,0:T(8,128)S(1)}) custom-call(f32[16,32,128]{2,1,0:T(8,128)S(1)} %convert_multiply_fusion.masked, s32[16,32,128]{2,1,0:T(8,128)S(1)} %copy-done, f32[16,32,128]{2,1,0:T(8,128)S(1)} %copy-done.3, ...), custom_call_target="tpu_custom_call" | custom-call | bytes 1048576 | tf_op jit(solution)/shard_map/pack/pallas_call | solution.py:447
  2.3 0.5 %collective-permute-start = (f32[4,32,128]{2,1,0:T(8,128)S(1)}, f32[4,32,128]{2,1,0:T(8,128)S(1)}, u32[]{:S(2)}, u32[]{:S(2)}) collective-permute-start(f32[4,32,128]{2,1,0:T(8,128)S(1)} %get-tuple-element.32), channel_id=1, source_target_pairs={{0,8},{1,9},{2,10},{3,11},{4,12},{5,13},{6,14},{7,15},{8,0},{9,1},... | collective-permute-start | bytes 196616 | tf_op jit(solution)/shard_map/faces_in/ppermute | solution.py:40
  2.8 2.6 %collective-permute-start.1 = (f32[4,32,128]{2,1,0:T(8,128)S(1)}, f32[4,32,128]{2,1,0:T(8,128)S(1)}, u32[]{:S(2)}, u32[]{:S(2)}) collective-permute-start(f32[4,32,128]{2,1,0:T(8,128)S(1)} %get-tuple-element.33), channel_id=1, source_target_pairs={{0,1},{1,0},{2,3},{3,2},{4,5},{5,4},{6,7},{7,6},{8,16},{9,17},{10,... | collective-permute-start | bytes 196616 | tf_op jit(solution)/shard_map/faces_in/ppermute | solution.py:40
  5.3 1.6 %collective-permute-start.2 = (f32[4,16,128]{2,1,0:T(8,128)S(1)}, f32[4,16,128]{2,1,0:T(8,128)S(1)}, u32[]{:S(2)}, u32[]{:S(2)}) collective-permute-start(f32[4,16,128]{2,1,0:T(8,128)S(1)} %get-tuple-element.34), channel_id=1, source_target_pairs={{0,2},{1,3},{2,0},{3,1},{4,6},{5,7},{6,4},{7,5},{8,10},{9,11},{10,... | collective-permute-start | bytes 98312 | tf_op jit(solution)/shard_map/faces_in/ppermute | solution.py:40
  6.9 0.0 collective-permute-start.3
  6.9 1.3 %collective-permute-start.4 = (f32[8,512]{1,0:T(8,128)S(1)}, f32[8,512]{1,0:T(8,128)S(1)}, u32[]{:S(2)}, u32[]{:S(2)}) collective-permute-start(f32[8,512]{1,0:T(8,128)S(1)} %get-tuple-element.36.sz), channel_id=1, source_target_pairs={{0,1},{1,0},{2,3},{3,2},{4,5},{5,4},{6,7},{7,6},{8,9},{9,8},{10,11... | collective-permute-start | bytes 49160 | tf_op jit(solution)/shard_map/faces_in/ppermute | solution.py:40
  8.3 0.0 copy-start.12
  8.3 0.0 copy-start.13
  8.3 0.3 %own_part.1 = (f32[640,128]{1,0:T(8,128)S(1)}, f32[16,32,128]{2,1,0:T(8,128)S(1)}, f32[16,32,128]{2,1,0:T(8,128)S(1)}, f32[720,256]{1,0:T(8,128)S(1)}, f32[8,128]{1,0:T(8,128)S(1)}) custom-call(f32[16,32,128]{2,1,0:T(8,128)S(1)} %convert_multiply_fusion.masked, s32[16,32,128]{2,1,0:T(8,128)S(1)} %copy-done, f32[16,32,128]{2,1,0:T(8,128)S(1)} %copy-done.3, ...), custom_call_target="tpu_custom_call" | custom-call | bytes 1048576 | tf_op jit(solution)/shard_map/own_part/pallas_call | solution.py:447
  8.6 2.1 %collective-permute-done.4.rz = f32[8,512]{1,0:T(8,128)S(1)} collective-permute-done((f32[8,512]{1,0:T(8,128)S(1)}, f32[8,512]{1,0:T(8,128)S(1)}, u32[]{:S(2)}, u32[]{:S(2)}) %collective-permute-start.4) | collective-permute-done | bytes 16416 | tf_op jit(solution)/shard_map/faces_in/ppermute | solution.py:40
  10.7 0.0 collective-permute-done.2.ry0
  10.7 0.0 collective-permute-done.3.ry1
  10.7 0.0 collective-permute-done.rx0
  10.7 0.0 collective-permute-done.1.rx1
  10.8 1.4 %solve.1 = (f32[16,32,128]{2,1,0:T(8,128)S(1)}, f32[2,32,128]{2,1,0:T(8,128)S(1)}, f32[3,32,128]{2,1,0:T(8,128)S(1)}, f32[6,16,128]{2,1,0:T(8,128)S(1)}, f32[6,1...) custom-call(f32[640,128]{1,0:T(8,128)S(1)} %get-tuple-element.38.modes, f32[720,256]{1,0:T(8,128)S(1)} %get-tuple-element.39.factors, ...), custom_call_target="tpu_custom_call" | custom-call | bytes 1048576 | tf_op jit(solution)/shard_map/solve/pallas_call | solution.py:447
  12.2 1.3 %collective-permute-start.6 = (f32[3,32,128]{2,1,0:T(8,128)S(1)}, f32[3,32,128]{2,1,0:T(8,128)S(1)}, u32[]{:S(2)}, u32[]{:S(2)}) collective-permute-start(f32[3,32,128]{2,1,0:T(8,128)S(1)} %get-tuple-element.43.tx1), channel_id=1, source_target_pairs={{0,1},{1,0},{2,3},{3,2},{4,5},{5,4},{6,7},{7,6},{8,16},{9,17},{10,... | collective-permute-start | bytes 147464 | tf_op jit(solution)/shard_map/faces_out/ppermute | solution.py:40
  13.5 2.3 %collective-permute-start.7 = (f32[6,16,128]{2,1,0:T(8,128)S(1)}, f32[6,16,128]{2,1,0:T(8,128)S(1)}, u32[]{:S(2)}, u32[]{:S(2)}) collective-permute-start(f32[6,16,128]{2,1,0:T(8,128)S(1)} %get-tuple-element.44.ty0), channel_id=1, source_target_pairs={{0,2},{1,3},{2,0},{3,1},{4,6},{5,7},{6,4},{7,5},{8,10},{9,11},{10,... | collective-permute-start | bytes 147464 | tf_op jit(solution)/shard_map/faces_out/ppermute | solution.py:40
  15.9 0.0 collective-permute-start.8
  15.9 1.5 %collective-permute-start.9 = (f32[24,512]{1,0:T(8,128)S(1)}, f32[24,512]{1,0:T(8,128)S(1)}, u32[]{:S(2)}, u32[]{:S(2)}) collective-permute-start(f32[24,512]{1,0:T(8,128)S(1)} %get-tuple-element.46.tz), channel_id=1, source_target_pairs={{0,1},{1,0},{2,3},{3,2},{4,5},{5,4},{6,7},{7,6},{8,9},{9,8},{10,11... | collective-permute-start | bytes 147464 | tf_op jit(solution)/shard_map/faces_out/ppermute | solution.py:40
  17.4 0.2 collective-permute-start.5
  18.3 0.6 %links.1 = (f32[16,32,128]{2,1,0:T(8,128)S(1)}, f32[17,32,128]{2,1,0:T(8,128)S(1)}, f32[16,32,128]{2,1,0:T(8,128)S(1)}, f32[16,128]{1,0:T(8,128)S(1)}, f32[16,32...) custom-call(f32[1]{0:T(128)S(6)} %copy.18.rz_prev, ...), custom_call_target="tpu_custom_call" | custom-call | bytes 1048576 | tf_op jit(solution)/shard_map/links/pallas_call | solution.py:447
  18.8 0.0 collective-permute-done.5.qx0
  18.9 0.0 collective-permute-done.6.qx1
  18.9 0.0 collective-permute-done.7.qy0
  18.9 0.0 collective-permute-done.8.qy1
  18.9 1.1 %collective-permute-done.9.qz = f32[24,512]{1,0:T(8,128)S(1)} collective-permute-done((f32[24,512]{1,0:T(8,128)S(1)}, f32[24,512]{1,0:T(8,128)S(1)}, u32[]{:S(2)}, u32[]{:S(2)}) %collective-permute-start.9) | collective-permute-done | bytes 49184 | tf_op jit(solution)/shard_map/faces_out/ppermute | solution.py:40
  20.0 0.7 %image.1 = (f32[16,32,128]{2,1,0:T(8,128)S(1)}, f32[16,32,128]{2,1,0:T(8,128)S(1)}, f32[32,1,128]{2,1,0:T(1,128)S(1)}) custom-call(f32[16,32,128]{2,1,0:T(8,128)S(1)} %convert_multiply_fusion.masked, f32[16,32,128]{2,1,0:T(8,128)S(1)} %get-tuple-element.30.mask, f32[16,32,128]{2,1,0:T(8,128)S(1)} %get-tuple-element.31.d, ...), custom_call_target="tpu_custom_call" | custom-call | bytes 1048576 | tf_op jit(solution)/shard_map/image/pallas_call | solution.py:447
  20.8 9.6 %all_to_all.5.sums = f32[32,1,128]{2,1,0:T(1,128)S(1)} all-to-all(f32[32,1,128]{2,1,0:T(1,128)S(1)} %get-tuple-element.54), channel_id=1, replica_groups=mesh['gx'=4,'gy'=4,'gz'=2] {'gx','gy','gz'}, dimensions={0} | all-to-all | bytes 32768 | tf_op jit(solution)/shard_map/sums/all_to_all | solution.py:505
  30.4 1.3 %update.1 = (f32[16,32,128]{2,1,0:T(8,128)}, f32[16,32,128]{2,1,0:T(8,128)}, f32[16,32,128]{2,1,0:T(8,128)}) custom-call(f32[1,128]{1,0:T(1,128)S(1)} %get-tuple-element.37.rz_line, f32[32,1,128]{2,1,0:T(1,128)S(1)} %all_to_all.5.sums, f32[16,32,128]{2,1,0:T(8,128)S(1)} %copy-done.5, f32[16,32,128]{2,1,0:T(8,128)S(1)} %copy-done.2, ...), custom_call_target="tpu_custom_call" | custom-call | bytes 1048576 | tf_op jit(solution)/shard_map/update/pallas_call | solution.py:447
  (24 shorter events, 0.0 us)
Async XLA Ops:
  0.6 1.2 %copy-start = (s32[16,32,128]{2,1,0:T(8,128)S(1)}, s32[16,32,128]{2,1,0:T(8,128)}, u32[]{:S(2)}) copy-start(s32[16,32,128]{2,1,0:T(8,128)} %msk.3) | copy-start | bytes 786436
  0.6 1.2 %copy-start.1 = (f32[16,32,128]{2,1,0:T(8,128)S(1)}, f32[16,32,128]{2,1,0:T(8,128)}, u32[]{:S(2)}) copy-start(f32[16,32,128]{2,1,0:T(8,128)} %mu.5) | copy-start | bytes 786436
  0.7 1.2 %copy-start.3 = (f32[16,32,128]{2,1,0:T(8,128)S(1)}, f32[16,32,128]{2,1,0:T(8,128)}, u32[]{:S(2)}) copy-start(f32[16,32,128]{2,1,0:T(8,128)} %direction.3) | copy-start | bytes 786436
  1.9 6.3 %copy-start.4 = (bf16[160,256]{1,0:T(8,128)(2,1)S(1)}, bf16[160,256]{1,0:T(8,128)(2,1)}, u32[]{:S(2)}) copy-start(bf16[160,256]{1,0:T(8,128)(2,1)} %constant.20.clone.into) | copy-start | bytes 245764
  1.9 6.3 %copy-start.9 = (f32[40,256]{1,0:T(8,128)S(1)}, f32[40,256]{1,0:T(8,128)}, u32[]{:S(2)}) copy-start(f32[40,256]{1,0:T(8,128)} %constant.19.clone.middle) | copy-start | bytes 122884
  2.3 8.4 %collective-permute-start = (f32[4,32,128]{2,1,0:T(8,128)S(1)}, f32[4,32,128]{2,1,0:T(8,128)S(1)}, u32[]{:S(2)}, u32[]{:S(2)}) collective-permute-start(f32[4,32,128]{2,1,0:T(8,128)S(1)} %get-tuple-element.32), channel_id=1, source_target_pairs={{0,8},{1,9},{2,10},{3,11},{4,12},{5,13},{6,14},{7,15},{8,0},{9,1},... | collective-permute-start | bytes 196616 | tf_op jit(solution)/shard_map/faces_in/ppermute | solution.py:40
  2.8 8.0 %collective-permute-start.1 = (f32[4,32,128]{2,1,0:T(8,128)S(1)}, f32[4,32,128]{2,1,0:T(8,128)S(1)}, u32[]{:S(2)}, u32[]{:S(2)}) collective-permute-start(f32[4,32,128]{2,1,0:T(8,128)S(1)} %get-tuple-element.33), channel_id=1, source_target_pairs={{0,1},{1,0},{2,3},{3,2},{4,5},{5,4},{6,7},{7,6},{8,16},{9,17},{10,... | collective-permute-start | bytes 196616 | tf_op jit(solution)/shard_map/faces_in/ppermute | solution.py:40
  5.3 5.4 %collective-permute-start.2 = (f32[4,16,128]{2,1,0:T(8,128)S(1)}, f32[4,16,128]{2,1,0:T(8,128)S(1)}, u32[]{:S(2)}, u32[]{:S(2)}) collective-permute-start(f32[4,16,128]{2,1,0:T(8,128)S(1)} %get-tuple-element.34), channel_id=1, source_target_pairs={{0,2},{1,3},{2,0},{3,1},{4,6},{5,7},{6,4},{7,5},{8,10},{9,11},{10,... | collective-permute-start | bytes 98312 | tf_op jit(solution)/shard_map/faces_in/ppermute | solution.py:40
  6.9 3.8 %collective-permute-start.3 = (f32[4,16,128]{2,1,0:T(8,128)S(1)}, f32[4,16,128]{2,1,0:T(8,128)S(1)}, u32[]{:S(2)}, u32[]{:S(2)}) collective-permute-start(f32[4,16,128]{2,1,0:T(8,128)S(1)} %get-tuple-element.35), channel_id=1, source_target_pairs={{0,8},{1,9},{2,4},{3,5},{4,2},{5,3},{6,14},{7,15},{8,0},{9,1},{10,... | collective-permute-start | bytes 98312 | tf_op jit(solution)/shard_map/faces_in/ppermute | solution.py:40
  6.9 3.8 %copy-start.6 = (bf16[384,256]{1,0:T(8,128)(2,1)S(1)}, bf16[384,256]{1,0:T(8,128)(2,1)}, u32[]{:S(2)}) copy-start(bf16[384,256]{1,0:T(8,128)(2,1)} %constant.23.clone.back) | copy-start | bytes 589828
  6.9 3.9 %copy-start.7 = (bf16[256,256]{1,0:T(8,128)(2,1)S(1)}, bf16[256,256]{1,0:T(8,128)(2,1)}, u32[]{:S(2)}) copy-start(bf16[256,256]{1,0:T(8,128)(2,1)} %constant.25.clone.out) | copy-start | bytes 393220
  6.9 3.9 %copy-start.8 = (bf16[256,256]{1,0:T(8,128)(2,1)S(1)}, bf16[256,256]{1,0:T(8,128)(2,1)}, u32[]{:S(2)}) copy-start(bf16[256,256]{1,0:T(8,128)(2,1)} %constant.18.clone.fwd) | copy-start | bytes 393220
  6.9 3.8 %collective-permute-start.4 = (f32[8,512]{1,0:T(8,128)S(1)}, f32[8,512]{1,0:T(8,128)S(1)}, u32[]{:S(2)}, u32[]{:S(2)}) collective-permute-start(f32[8,512]{1,0:T(8,128)S(1)} %get-tuple-element.36.sz), channel_id=1, source_target_pairs={{0,1},{1,0},{2,3},{3,2},{4,5},{5,4},{6,7},{7,6},{8,9},{9,8},{10,11... | collective-permute-start | bytes 49160 | tf_op jit(solution)/shard_map/faces_in/ppermute | solution.py:40
  8.2 2.5 %copy-start.10 = (f32[40,128]{1,0:T(8,128)S(1)}, f32[40,128]{1,0:T(8,128)}, u32[]{:S(2)}) copy-start(f32[40,128]{1,0:T(8,128)} %constant.24.clone.rim) | copy-start | bytes 61444
  8.2 2.5 %copy-start.11 = (bf16[32,256]{1,0:T(8,128)(2,1)S(1)}, bf16[32,256]{1,0:T(8,128)(2,1)}, u32[]{:S(2)}) copy-start(bf16[32,256]{1,0:T(8,128)(2,1)} %constant.26.clone.out_ends) | copy-start | bytes 49156
  8.3 2.5 %copy-start.12 = (bf16[48,128]{1,0:T(8,128)(2,1)S(1)}, bf16[48,128]{1,0:T(8,128)(2,1)}, u32[]{:S(2)}) copy-start(bf16[48,128]{1,0:T(8,128)(2,1)} %constant.21.clone.one) | copy-start | bytes 36868
  8.3 2.5 %copy-start.13 = (f32[8,256]{1,0:T(8,128)S(1)}, f32[8,256]{1,0:T(8,128)}, u32[]{:S(2)}) copy-start(f32[8,256]{1,0:T(8,128)} %constant.22.clone.row_ends) | copy-start | bytes 24580
  12.2 6.6 %collective-permute-start.6 = (f32[3,32,128]{2,1,0:T(8,128)S(1)}, f32[3,32,128]{2,1,0:T(8,128)S(1)}, u32[]{:S(2)}, u32[]{:S(2)}) collective-permute-start(f32[3,32,128]{2,1,0:T(8,128)S(1)} %get-tuple-element.43.tx1), channel_id=1, source_target_pairs={{0,1},{1,0},{2,3},{3,2},{4,5},{5,4},{6,7},{7,6},{8,16},{9,17},{10,... | collective-permute-start | bytes 147464 | tf_op jit(solution)/shard_map/faces_out/ppermute | solution.py:40
  13.5 5.3 %collective-permute-start.7 = (f32[6,16,128]{2,1,0:T(8,128)S(1)}, f32[6,16,128]{2,1,0:T(8,128)S(1)}, u32[]{:S(2)}, u32[]{:S(2)}) collective-permute-start(f32[6,16,128]{2,1,0:T(8,128)S(1)} %get-tuple-element.44.ty0), channel_id=1, source_target_pairs={{0,2},{1,3},{2,0},{3,1},{4,6},{5,7},{6,4},{7,5},{8,10},{9,11},{10,... | collective-permute-start | bytes 147464 | tf_op jit(solution)/shard_map/faces_out/ppermute | solution.py:40
  15.9 3.0 %collective-permute-start.8 = (f32[6,16,128]{2,1,0:T(8,128)S(1)}, f32[6,16,128]{2,1,0:T(8,128)S(1)}, u32[]{:S(2)}, u32[]{:S(2)}) collective-permute-start(f32[6,16,128]{2,1,0:T(8,128)S(1)} %get-tuple-element.45.ty1), channel_id=1, source_target_pairs={{0,8},{1,9},{2,4},{3,5},{4,2},{5,3},{6,14},{7,15},{8,0},{9,1},{10,... | collective-permute-start | bytes 147464 | tf_op jit(solution)/shard_map/faces_out/ppermute | solution.py:40
  15.9 4.2 %collective-permute-start.9 = (f32[24,512]{1,0:T(8,128)S(1)}, f32[24,512]{1,0:T(8,128)S(1)}, u32[]{:S(2)}, u32[]{:S(2)}) collective-permute-start(f32[24,512]{1,0:T(8,128)S(1)} %get-tuple-element.46.tz), channel_id=1, source_target_pairs={{0,1},{1,0},{2,3},{3,2},{4,5},{5,4},{6,7},{7,6},{8,9},{9,8},{10,11... | collective-permute-start | bytes 147464 | tf_op jit(solution)/shard_map/faces_out/ppermute | solution.py:40
  17.4 1.4 %collective-permute-start.5 = (f32[2,32,128]{2,1,0:T(8,128)S(1)}, f32[2,32,128]{2,1,0:T(8,128)S(1)}, u32[]{:S(2)}, u32[]{:S(2)}) collective-permute-start(f32[2,32,128]{2,1,0:T(8,128)S(1)} %get-tuple-element.42.tx0), channel_id=1, source_target_pairs={{0,8},{1,9},{2,10},{3,11},{4,12},{5,13},{6,14},{7,15},{8,0},{9,1},... | collective-permute-start | bytes 98312 | tf_op jit(solution)/shard_map/faces_out/ppermute | solution.py:40
  20.0 10.4 %copy-start.2 = (f32[16,32,128]{2,1,0:T(8,128)S(1)}, f32[16,32,128]{2,1,0:T(8,128)}, u32[]{:S(2)}) copy-start(f32[16,32,128]{2,1,0:T(8,128)} %res.1) | copy-start | bytes 786436
  20.0 10.4 %copy-start.5 = (f32[16,32,128]{2,1,0:T(8,128)S(1)}, f32[16,32,128]{2,1,0:T(8,128)}, u32[]{:S(2)}) copy-start(f32[16,32,128]{2,1,0:T(8,128)} %iterate.1) | copy-start | bytes 786436

commit v9 on v8

--- a/solution.py
+++ b/solution.py
@@ -176,8 +176,9 @@
     flat = [field.reshape(size_x * size_y, size_z) for field in fields(every)]
     lane = jnp.where(even_z, size_z - 1, 0)
     pick = jnp.where((iota((16, 2 * size_z), 1) % size_z == lane) & (iota((16, 2 * size_z), 0) < 1), 1.0, 0.0).astype(BF16)
-    lines = [dot_lanes(pick, jnp.concatenate(halves(field), axis=1))[0:1] for field in (flat[0], flat[2], flat[3])]
+    lines = [dot_lanes(pick, jnp.concatenate(halves(field), axis=1))[0:1] for field in (flat[0], flat[3])]
     lines.insert(1, dot_lanes(pick[:, :size_z], flat[1].astype(BF16))[0:1])
+    lines.insert(2, jnp.transpose(pltpu.roll(flat[2], jnp.where(even_z, 1, 0), 1))[0:1])
     at = iota((8, size_x * size_y), 0)
     total = jnp.zeros(at.shape, F32)
     for f, line in enumerate(lines):

time: 31.8 us -> 31.8 us (level)
  no operation moved by 1% of the time
where the time goes in v9:
time: 31.8 us; the launch traced here: 31.7 us
  starting transfers between devices  11.4 us (36%)
  blocking collectives  9.64 us (30%)
  Pallas kernels  4.6 us (14%)
  waiting for transfers between devices  3.28 us (10%)
  between operations  1.48 us (5%)
  other arithmetic  1.14 us (4%)
    ppermute x10, starting transfers between devices, swap(): return lax.ppermute(block, AXES, swaps(axis, turn))  11.4 us
    all_to_all x1, blocking collectives, shards(): sums = lax.all_to_all(sums, AXES, 0, 0, tiled=True)  9.64 us
    pallas_call x6, Pallas kernels, call(): pl.pallas_call(kernel, out_shape=outs, in_specs=specs or [VMEM] * len(arg...  4.6 us
    ppermute x10, waiting for transfers between devices, swap(): return lax.ppermute(block, AXES, swaps(axis, turn))  3.28 us
    mul x1, other arithmetic, shards(): masked = unfixed_node_mask.astype(F32) * residual  1.14 us
  transfers between devices with their start and end apart: 10, of which 2 were waited for; matrix products, arithmetic and copies ran while one was open for 0% of the time, Pallas kernels for 3%

profile of v9, /device:TPU:0, one launch (start us, length us, event | category | flops | bytes accessed | tf_op | source)
XLA Modules:
  0.0 31.7 jit_solution(5569696531100767757)
XLA Ops:
  0.7 1.1 %convert_multiply_fusion.masked = f32[16,32,128]{2,1,0:T(8,128)S(1)} fusion(f32[16,32,128]{2,1,0:T(8,128)} %res.1, s32[16,32,128]{2,1,0:T(8,128)} %msk.3), kind=kLoop, calls=%fused_computation | loop fusion | flops 131072 | bytes 786432 | tf_op jit(solution)/shard_map/masks/mul | solution.py:485
  1.8 0.0 copy-done.1
  1.8 0.1 copy-done.3
  1.9 0.3 %pack.1 = (f32[4,32,128]{2,1,0:T(8,128)S(1)}, f32[4,32,128]{2,1,0:T(8,128)S(1)}, f32[4,16,128]{2,1,0:T(8,128)S(1)}, f32[4,16,128]{2,1,0:T(8,128)S(1)}, f32[8,512]{1,0:T(8,128)S(1)}) custom-call(f32[16,32,128]{2,1,0:T(8,128)S(1)} %convert_multiply_fusion.masked, s32[16,32,128]{2,1,0:T(8,128)S(1)} %copy-done, f32[16,32,128]{2,1,0:T(8,128)S(1)} %copy-done.3, ...), custom_call_target="tpu_custom_call" | custom-call | bytes 1048576 | tf_op jit(solution)/shard_map/pack/pallas_call | solution.py:448
  2.2 0.5 %collective-permute-start = (f32[4,32,128]{2,1,0:T(8,128)S(1)}, f32[4,32,128]{2,1,0:T(8,128)S(1)}, u32[]{:S(2)}, u32[]{:S(2)}) collective-permute-start(f32[4,32,128]{2,1,0:T(8,128)S(1)} %get-tuple-element.32), channel_id=1, source_target_pairs={{0,8},{1,9},{2,10},{3,11},{4,12},{5,13},{6,14},{7,15},{8,0},{9,1},... | collective-permute-start | bytes 196616 | tf_op jit(solution)/shard_map/faces_in/ppermute | solution.py:40
  2.7 2.6 %collective-permute-start.1 = (f32[4,32,128]{2,1,0:T(8,128)S(1)}, f32[4,32,128]{2,1,0:T(8,128)S(1)}, u32[]{:S(2)}, u32[]{:S(2)}) collective-permute-start(f32[4,32,128]{2,1,0:T(8,128)S(1)} %get-tuple-element.33), channel_id=1, source_target_pairs={{0,1},{1,0},{2,3},{3,2},{4,5},{5,4},{6,7},{7,6},{8,16},{9,17},{10,... | collective-permute-start | bytes 196616 | tf_op jit(solution)/shard_map/faces_in/ppermute | solution.py:40
  5.3 1.6 %collective-permute-start.2 = (f32[4,16,128]{2,1,0:T(8,128)S(1)}, f32[4,16,128]{2,1,0:T(8,128)S(1)}, u32[]{:S(2)}, u32[]{:S(2)}) collective-permute-start(f32[4,16,128]{2,1,0:T(8,128)S(1)} %get-tuple-element.34), channel_id=1, source_target_pairs={{0,2},{1,3},{2,0},{3,1},{4,6},{5,7},{6,4},{7,5},{8,10},{9,11},{10,... | collective-permute-start | bytes 98312 | tf_op jit(solution)/shard_map/faces_in/ppermute | solution.py:40
  6.9 0.0 collective-permute-start.3
  6.9 1.3 %collective-permute-start.4 = (f32[8,512]{1,0:T(8,128)S(1)}, f32[8,512]{1,0:T(8,128)S(1)}, u32[]{:S(2)}, u32[]{:S(2)}) collective-permute-start(f32[8,512]{1,0:T(8,128)S(1)} %get-tuple-element.36.sz), channel_id=1, source_target_pairs={{0,1},{1,0},{2,3},{3,2},{4,5},{5,4},{6,7},{7,6},{8,9},{9,8},{10,11... | collective-permute-start | bytes 49160 | tf_op jit(solution)/shard_map/faces_in/ppermute | solution.py:40
  8.2 0.0 copy-start.12
  8.3 0.0 copy-start.13
  8.3 0.3 %own_part.1 = (f32[640,128]{1,0:T(8,128)S(1)}, f32[16,32,128]{2,1,0:T(8,128)S(1)}, f32[16,32,128]{2,1,0:T(8,128)S(1)}, f32[720,256]{1,0:T(8,128)S(1)}, f32[8,128]{1,0:T(8,128)S(1)}) custom-call(f32[16,32,128]{2,1,0:T(8,128)S(1)} %convert_multiply_fusion.masked, s32[16,32,128]{2,1,0:T(8,128)S(1)} %copy-done, f32[16,32,128]{2,1,0:T(8,128)S(1)} %copy-done.3, ...), custom_call_target="tpu_custom_call" | custom-call | bytes 1048576 | tf_op jit(solution)/shard_map/own_part/pallas_call | solution.py:448
  8.6 2.1 %collective-permute-done.4.rz = f32[8,512]{1,0:T(8,128)S(1)} collective-permute-done((f32[8,512]{1,0:T(8,128)S(1)}, f32[8,512]{1,0:T(8,128)S(1)}, u32[]{:S(2)}, u32[]{:S(2)}) %collective-permute-start.4) | collective-permute-done | bytes 16416 | tf_op jit(solution)/shard_map/faces_in/ppermute | solution.py:40
  10.7 0.0 collective-permute-done.2.ry0
  10.7 0.0 collective-permute-done.3.ry1
  10.7 0.0 collective-permute-done.rx0
  10.7 0.0 collective-permute-done.1.rx1
  10.8 1.4 %solve.1 = (f32[16,32,128]{2,1,0:T(8,128)S(1)}, f32[2,32,128]{2,1,0:T(8,128)S(1)}, f32[3,32,128]{2,1,0:T(8,128)S(1)}, f32[6,16,128]{2,1,0:T(8,128)S(1)}, f32[6,1...) custom-call(f32[640,128]{1,0:T(8,128)S(1)} %get-tuple-element.38.modes, f32[720,256]{1,0:T(8,128)S(1)} %get-tuple-element.39.factors, ...), custom_call_target="tpu_custom_call" | custom-call | bytes 1048576 | tf_op jit(solution)/shard_map/solve/pallas_call | solution.py:448
  12.2 1.3 %collective-permute-start.6 = (f32[3,32,128]{2,1,0:T(8,128)S(1)}, f32[3,32,128]{2,1,0:T(8,128)S(1)}, u32[]{:S(2)}, u32[]{:S(2)}) collective-permute-start(f32[3,32,128]{2,1,0:T(8,128)S(1)} %get-tuple-element.43.tx1), channel_id=1, source_target_pairs={{0,1},{1,0},{2,3},{3,2},{4,5},{5,4},{6,7},{7,6},{8,16},{9,17},{10,... | collective-permute-start | bytes 147464 | tf_op jit(solution)/shard_map/faces_out/ppermute | solution.py:40
  13.5 2.3 %collective-permute-start.7 = (f32[6,16,128]{2,1,0:T(8,128)S(1)}, f32[6,16,128]{2,1,0:T(8,128)S(1)}, u32[]{:S(2)}, u32[]{:S(2)}) collective-permute-start(f32[6,16,128]{2,1,0:T(8,128)S(1)} %get-tuple-element.44.ty0), channel_id=1, source_target_pairs={{0,2},{1,3},{2,0},{3,1},{4,6},{5,7},{6,4},{7,5},{8,10},{9,11},{10,... | collective-permute-start | bytes 147464 | tf_op jit(solution)/shard_map/faces_out/ppermute | solution.py:40
  15.9 0.0 collective-permute-start.8
  15.9 1.5 %collective-permute-start.9 = (f32[24,512]{1,0:T(8,128)S(1)}, f32[24,512]{1,0:T(8,128)S(1)}, u32[]{:S(2)}, u32[]{:S(2)}) collective-permute-start(f32[24,512]{1,0:T(8,128)S(1)} %get-tuple-element.46.tz), channel_id=1, source_target_pairs={{0,1},{1,0},{2,3},{3,2},{4,5},{5,4},{6,7},{7,6},{8,9},{9,8},{10,11... | collective-permute-start | bytes 147464 | tf_op jit(solution)/shard_map/faces_out/ppermute | solution.py:40
  17.4 0.2 collective-permute-start.5
  18.3 0.6 %links.1 = (f32[16,32,128]{2,1,0:T(8,128)S(1)}, f32[17,32,128]{2,1,0:T(8,128)S(1)}, f32[16,32,128]{2,1,0:T(8,128)S(1)}, f32[16,128]{1,0:T(8,128)S(1)}, f32[16,32...) custom-call(f32[1]{0:T(128)S(6)} %copy.18.rz_prev, ...), custom_call_target="tpu_custom_call" | custom-call | bytes 1048576 | tf_op jit(solution)/shard_map/links/pallas_call | solution.py:448
  18.8 0.0 collective-permute-done.5.qx0
  18.9 0.0 collective-permute-done.6.qx1
  18.9 0.0 collective-permute-done.7.qy0
  18.9 0.0 collective-permute-done.8.qy1
  18.9 1.1 %collective-permute-done.9.qz = f32[24,512]{1,0:T(8,128)S(1)} collective-permute-done((f32[24,512]{1,0:T(8,128)S(1)}, f32[24,512]{1,0:T(8,128)S(1)}, u32[]{:S(2)}, u32[]{:S(2)}) %collective-permute-start.9) | collective-permute-done | bytes 49184 | tf_op jit(solution)/shard_map/faces_out/ppermute | solution.py:40
  20.0 0.7 %image.1 = (f32[16,32,128]{2,1,0:T(8,128)S(1)}, f32[16,32,128]{2,1,0:T(8,128)S(1)}, f32[32,1,128]{2,1,0:T(1,128)S(1)}) custom-call(f32[16,32,128]{2,1,0:T(8,128)S(1)} %convert_multiply_fusion.masked, f32[16,32,128]{2,1,0:T(8,128)S(1)} %get-tuple-element.30.mask, f32[16,32,128]{2,1,0:T(8,128)S(1)} %get-tuple-element.31.d, ...), custom_call_target="tpu_custom_call" | custom-call | bytes 1048576 | tf_op jit(solution)/shard_map/image/pallas_call | solution.py:448
  20.7 9.6 %all_to_all.5.sums = f32[32,1,128]{2,1,0:T(1,128)S(1)} all-to-all(f32[32,1,128]{2,1,0:T(1,128)S(1)} %get-tuple-element.54), channel_id=1, replica_groups=mesh['gx'=4,'gy'=4,'gz'=2] {'gx','gy','gz'}, dimensions={0} | all-to-all | bytes 32768 | tf_op jit(solution)/shard_map/sums/all_to_all | solution.py:506
  30.4 1.3 %update.1 = (f32[16,32,128]{2,1,0:T(8,128)}, f32[16,32,128]{2,1,0:T(8,128)}, f32[16,32,128]{2,1,0:T(8,128)}) custom-call(f32[1,128]{1,0:T(1,128)S(1)} %get-tuple-element.37.rz_line, f32[32,1,128]{2,1,0:T(1,128)S(1)} %all_to_all.5.sums, f32[16,32,128]{2,1,0:T(8,128)S(1)} %copy-done.5, f32[16,32,128]{2,1,0:T(8,128)S(1)} %copy-done.2, ...), custom_call_target="tpu_custom_call" | custom-call | bytes 1048576 | tf_op jit(solution)/shard_map/update/pallas_call | solution.py:448
  (24 shorter events, 0.0 us)
Async XLA Ops:
  0.6 1.2 %copy-start = (s32[16,32,128]{2,1,0:T(8,128)S(1)}, s32[16,32,128]{2,1,0:T(8,128)}, u32[]{:S(2)}) copy-start(s32[16,32,128]{2,1,0:T(8,128)} %msk.3) | copy-start | bytes 786436
  0.6 1.2 %copy-start.1 = (f32[16,32,128]{2,1,0:T(8,128)S(1)}, f32[16,32,128]{2,1,0:T(8,128)}, u32[]{:S(2)}) copy-start(f32[16,32,128]{2,1,0:T(8,128)} %mu.5) | copy-start | bytes 786436
  0.7 1.2 %copy-start.3 = (f32[16,32,128]{2,1,0:T(8,128)S(1)}, f32[16,32,128]{2,1,0:T(8,128)}, u32[]{:S(2)}) copy-start(f32[16,32,128]{2,1,0:T(8,128)} %direction.3) | copy-start | bytes 786436
  1.9 6.3 %copy-start.4 = (bf16[160,256]{1,0:T(8,128)(2,1)S(1)}, bf16[160,256]{1,0:T(8,128)(2,1)}, u32[]{:S(2)}) copy-start(bf16[160,256]{1,0:T(8,128)(2,1)} %constant.20.clone.into) | copy-start | bytes 245764
  1.9 6.3 %copy-start.9 = (f32[40,256]{1,0:T(8,128)S(1)}, f32[40,256]{1,0:T(8,128)}, u32[]{:S(2)}) copy-start(f32[40,256]{1,0:T(8,128)} %constant.19.clone.middle) | copy-start | bytes 122884
  2.2 8.5 %collective-permute-start = (f32[4,32,128]{2,1,0:T(8,128)S(1)}, f32[4,32,128]{2,1,0:T(8,128)S(1)}, u32[]{:S(2)}, u32[]{:S(2)}) collective-permute-start(f32[4,32,128]{2,1,0:T(8,128)S(1)} %get-tuple-element.32), channel_id=1, source_target_pairs={{0,8},{1,9},{2,10},{3,11},{4,12},{5,13},{6,14},{7,15},{8,0},{9,1},... | collective-permute-start | bytes 196616 | tf_op jit(solution)/shard_map/faces_in/ppermute | solution.py:40
  2.7 8.0 %collective-permute-start.1 = (f32[4,32,128]{2,1,0:T(8,128)S(1)}, f32[4,32,128]{2,1,0:T(8,128)S(1)}, u32[]{:S(2)}, u32[]{:S(2)}) collective-permute-start(f32[4,32,128]{2,1,0:T(8,128)S(1)} %get-tuple-element.33), channel_id=1, source_target_pairs={{0,1},{1,0},{2,3},{3,2},{4,5},{5,4},{6,7},{7,6},{8,16},{9,17},{10,... | collective-permute-start | bytes 196616 | tf_op jit(solution)/shard_map/faces_in/ppermute | solution.py:40
  5.3 5.4 %collective-permute-start.2 = (f32[4,16,128]{2,1,0:T(8,128)S(1)}, f32[4,16,128]{2,1,0:T(8,128)S(1)}, u32[]{:S(2)}, u32[]{:S(2)}) collective-permute-start(f32[4,16,128]{2,1,0:T(8,128)S(1)} %get-tuple-element.34), channel_id=1, source_target_pairs={{0,2},{1,3},{2,0},{3,1},{4,6},{5,7},{6,4},{7,5},{8,10},{9,11},{10,... | collective-permute-start | bytes 98312 | tf_op jit(solution)/shard_map/faces_in/ppermute | solution.py:40
  6.9 3.8 %collective-permute-start.3 = (f32[4,16,128]{2,1,0:T(8,128)S(1)}, f32[4,16,128]{2,1,0:T(8,128)S(1)}, u32[]{:S(2)}, u32[]{:S(2)}) collective-permute-start(f32[4,16,128]{2,1,0:T(8,128)S(1)} %get-tuple-element.35), channel_id=1, source_target_pairs={{0,8},{1,9},{2,4},{3,5},{4,2},{5,3},{6,14},{7,15},{8,0},{9,1},{10,... | collective-permute-start | bytes 98312 | tf_op jit(solution)/shard_map/faces_in/ppermute | solution.py:40
  6.9 3.8 %copy-start.6 = (bf16[384,256]{1,0:T(8,128)(2,1)S(1)}, bf16[384,256]{1,0:T(8,128)(2,1)}, u32[]{:S(2)}) copy-start(bf16[384,256]{1,0:T(8,128)(2,1)} %constant.23.clone.back) | copy-start | bytes 589828
  6.9 3.9 %copy-start.7 = (bf16[256,256]{1,0:T(8,128)(2,1)S(1)}, bf16[256,256]{1,0:T(8,128)(2,1)}, u32[]{:S(2)}) copy-start(bf16[256,256]{1,0:T(8,128)(2,1)} %constant.25.clone.out) | copy-start | bytes 393220
  6.9 3.9 %copy-start.8 = (bf16[256,256]{1,0:T(8,128)(2,1)S(1)}, bf16[256,256]{1,0:T(8,128)(2,1)}, u32[]{:S(2)}) copy-start(bf16[256,256]{1,0:T(8,128)(2,1)} %constant.18.clone.fwd) | copy-start | bytes 393220
  6.9 3.8 %collective-permute-start.4 = (f32[8,512]{1,0:T(8,128)S(1)}, f32[8,512]{1,0:T(8,128)S(1)}, u32[]{:S(2)}, u32[]{:S(2)}) collective-permute-start(f32[8,512]{1,0:T(8,128)S(1)} %get-tuple-element.36.sz), channel_id=1, source_target_pairs={{0,1},{1,0},{2,3},{3,2},{4,5},{5,4},{6,7},{7,6},{8,9},{9,8},{10,11... | collective-permute-start | bytes 49160 | tf_op jit(solution)/shard_map/faces_in/ppermute | solution.py:40
  8.2 2.5 %copy-start.10 = (f32[40,128]{1,0:T(8,128)S(1)}, f32[40,128]{1,0:T(8,128)}, u32[]{:S(2)}) copy-start(f32[40,128]{1,0:T(8,128)} %constant.24.clone.rim) | copy-start | bytes 61444
  8.2 2.5 %copy-start.11 = (bf16[32,256]{1,0:T(8,128)(2,1)S(1)}, bf16[32,256]{1,0:T(8,128)(2,1)}, u32[]{:S(2)}) copy-start(bf16[32,256]{1,0:T(8,128)(2,1)} %constant.26.clone.out_ends) | copy-start | bytes 49156
  8.2 2.5 %copy-start.12 = (bf16[48,128]{1,0:T(8,128)(2,1)S(1)}, bf16[48,128]{1,0:T(8,128)(2,1)}, u32[]{:S(2)}) copy-start(bf16[48,128]{1,0:T(8,128)(2,1)} %constant.21.clone.one) | copy-start | bytes 36868
  8.3 2.5 %copy-start.13 = (f32[8,256]{1,0:T(8,128)S(1)}, f32[8,256]{1,0:T(8,128)}, u32[]{:S(2)}) copy-start(f32[8,256]{1,0:T(8,128)} %constant.22.clone.row_ends) | copy-start | bytes 24580
  12.2 6.6 %collective-permute-start.6 = (f32[3,32,128]{2,1,0:T(8,128)S(1)}, f32[3,32,128]{2,1,0:T(8,128)S(1)}, u32[]{:S(2)}, u32[]{:S(2)}) collective-permute-start(f32[3,32,128]{2,1,0:T(8,128)S(1)} %get-tuple-element.43.tx1), channel_id=1, source_target_pairs={{0,1},{1,0},{2,3},{3,2},{4,5},{5,4},{6,7},{7,6},{8,16},{9,17},{10,... | collective-permute-start | bytes 147464 | tf_op jit(solution)/shard_map/faces_out/ppermute | solution.py:40
  13.5 5.3 %collective-permute-start.7 = (f32[6,16,128]{2,1,0:T(8,128)S(1)}, f32[6,16,128]{2,1,0:T(8,128)S(1)}, u32[]{:S(2)}, u32[]{:S(2)}) collective-permute-start(f32[6,16,128]{2,1,0:T(8,128)S(1)} %get-tuple-element.44.ty0), channel_id=1, source_target_pairs={{0,2},{1,3},{2,0},{3,1},{4,6},{5,7},{6,4},{7,5},{8,10},{9,11},{10,... | collective-permute-start | bytes 147464 | tf_op jit(solution)/shard_map/faces_out/ppermute | solution.py:40
  15.9 3.0 %collective-permute-start.8 = (f32[6,16,128]{2,1,0:T(8,128)S(1)}, f32[6,16,128]{2,1,0:T(8,128)S(1)}, u32[]{:S(2)}, u32[]{:S(2)}) collective-permute-start(f32[6,16,128]{2,1,0:T(8,128)S(1)} %get-tuple-element.45.ty1), channel_id=1, source_target_pairs={{0,8},{1,9},{2,4},{3,5},{4,2},{5,3},{6,14},{7,15},{8,0},{9,1},{10,... | collective-permute-start | bytes 147464 | tf_op jit(solution)/shard_map/faces_out/ppermute | solution.py:40
  15.9 4.2 %collective-permute-start.9 = (f32[24,512]{1,0:T(8,128)S(1)}, f32[24,512]{1,0:T(8,128)S(1)}, u32[]{:S(2)}, u32[]{:S(2)}) collective-permute-start(f32[24,512]{1,0:T(8,128)S(1)} %get-tuple-element.46.tz), channel_id=1, source_target_pairs={{0,1},{1,0},{2,3},{3,2},{4,5},{5,4},{6,7},{7,6},{8,9},{9,8},{10,11... | collective-permute-start | bytes 147464 | tf_op jit(solution)/shard_map/faces_out/ppermute | solution.py:40
  17.4 1.4 %collective-permute-start.5 = (f32[2,32,128]{2,1,0:T(8,128)S(1)}, f32[2,32,128]{2,1,0:T(8,128)S(1)}, u32[]{:S(2)}, u32[]{:S(2)}) collective-permute-start(f32[2,32,128]{2,1,0:T(8,128)S(1)} %get-tuple-element.42.tx0), channel_id=1, source_target_pairs={{0,8},{1,9},{2,10},{3,11},{4,12},{5,13},{6,14},{7,15},{8,0},{9,1},... | collective-permute-start | bytes 98312 | tf_op jit(solution)/shard_map/faces_out/ppermute | solution.py:40
  20.0 10.4 %copy-start.2 = (f32[16,32,128]{2,1,0:T(8,128)S(1)}, f32[16,32,128]{2,1,0:T(8,128)}, u32[]{:S(2)}) copy-start(f32[16,32,128]{2,1,0:T(8,128)} %res.1) | copy-start | bytes 786436
  20.0 10.4 %copy-start.5 = (f32[16,32,128]{2,1,0:T(8,128)S(1)}, f32[16,32,128]{2,1,0:T(8,128)}, u32[]{:S(2)}) copy-start(f32[16,32,128]{2,1,0:T(8,128)} %iterate.1) | copy-start | bytes 786436

commit v10 on v8

--- a/solution.py
+++ b/solution.py
@@ -412,7 +412,7 @@
         az_out[i] = image
         rz = rz + masked[i] * value
         zaz = zaz + value * image
-        zad = zad + (value * ad[i] + d[i] * image)
+        zad = zad + 2.0 * (value * ad[i])
     at = iota(sums.shape, 2)
     line = jnp.zeros(sums.shape, F32)
     for k, part in enumerate((rz, zaz, zad, dad[...])):

time: 31.8 us -> 31.8 us (level)
  no operation moved by 1% of the time
where the time goes in v10:
time: 31.8 us; the launch traced here: 31.6 us
  starting transfers between devices  11.3 us (36%)
  blocking collectives  9.64 us (30%)
  Pallas kernels  4.63 us (15%)
  waiting for transfers between devices  3.28 us (10%)
  between operations  1.48 us (5%)
  other arithmetic  1.14 us (4%)
    ppermute x10, starting transfers between devices, swap(): return lax.ppermute(block, AXES, swaps(axis, turn))  11.3 us
    all_to_all x1, blocking collectives, shards(): sums = lax.all_to_all(sums, AXES, 0, 0, tiled=True)  9.64 us
    pallas_call x6, Pallas kernels, call(): pl.pallas_call(kernel, out_shape=outs, in_specs=specs or [VMEM] * len(arg...  4.63 us
    ppermute x10, waiting for transfers between devices, swap(): return lax.ppermute(block, AXES, swaps(axis, turn))  3.28 us
    mul x1, other arithmetic, shards(): masked = unfixed_node_mask.astype(F32) * residual  1.14 us
  transfers between devices with their start and end apart: 10, of which 2 were waited for; matrix products, arithmetic and copies ran while one was open for 0% of the time, Pallas kernels for 3%

profile of v10, /device:TPU:0, one launch (start us, length us, event | category | flops | bytes accessed | tf_op | source)
XLA Modules:
  0.0 31.6 jit_solution(8130598356854261138)
XLA Ops:
  0.7 1.1 %convert_multiply_fusion.masked = f32[16,32,128]{2,1,0:T(8,128)S(1)} fusion(f32[16,32,128]{2,1,0:T(8,128)} %res.1, s32[16,32,128]{2,1,0:T(8,128)} %msk.3), kind=kLoop, calls=%fused_computation | loop fusion | flops 131072 | bytes 786432 | tf_op jit(solution)/shard_map/masks/mul | solution.py:484
  1.8 0.0 copy-done.1
  1.8 0.1 copy-done.3
  1.9 0.4 %pack.1 = (f32[4,32,128]{2,1,0:T(8,128)S(1)}, f32[4,32,128]{2,1,0:T(8,128)S(1)}, f32[4,16,128]{2,1,0:T(8,128)S(1)}, f32[4,16,128]{2,1,0:T(8,128)S(1)}, f32[8,512]{1,0:T(8,128)S(1)}) custom-call(f32[16,32,128]{2,1,0:T(8,128)S(1)} %convert_multiply_fusion.masked, s32[16,32,128]{2,1,0:T(8,128)S(1)} %copy-done, f32[16,32,128]{2,1,0:T(8,128)S(1)} %copy-done.3, ...), custom_call_target="tpu_custom_call" | custom-call | bytes 1048576 | tf_op jit(solution)/shard_map/pack/pallas_call | solution.py:447
  2.3 0.5 %collective-permute-start = (f32[4,32,128]{2,1,0:T(8,128)S(1)}, f32[4,32,128]{2,1,0:T(8,128)S(1)}, u32[]{:S(2)}, u32[]{:S(2)}) collective-permute-start(f32[4,32,128]{2,1,0:T(8,128)S(1)} %get-tuple-element.32), channel_id=1, source_target_pairs={{0,8},{1,9},{2,10},{3,11},{4,12},{5,13},{6,14},{7,15},{8,0},{9,1},... | collective-permute-start | bytes 196616 | tf_op jit(solution)/shard_map/faces_in/ppermute | solution.py:40
  2.8 2.6 %collective-permute-start.1 = (f32[4,32,128]{2,1,0:T(8,128)S(1)}, f32[4,32,128]{2,1,0:T(8,128)S(1)}, u32[]{:S(2)}, u32[]{:S(2)}) collective-permute-start(f32[4,32,128]{2,1,0:T(8,128)S(1)} %get-tuple-element.33), channel_id=1, source_target_pairs={{0,1},{1,0},{2,3},{3,2},{4,5},{5,4},{6,7},{7,6},{8,16},{9,17},{10,... | collective-permute-start | bytes 196616 | tf_op jit(solution)/shard_map/faces_in/ppermute | solution.py:40
  5.3 1.6 %collective-permute-start.2 = (f32[4,16,128]{2,1,0:T(8,128)S(1)}, f32[4,16,128]{2,1,0:T(8,128)S(1)}, u32[]{:S(2)}, u32[]{:S(2)}) collective-permute-start(f32[4,16,128]{2,1,0:T(8,128)S(1)} %get-tuple-element.34), channel_id=1, source_target_pairs={{0,2},{1,3},{2,0},{3,1},{4,6},{5,7},{6,4},{7,5},{8,10},{9,11},{10,... | collective-permute-start | bytes 98312 | tf_op jit(solution)/shard_map/faces_in/ppermute | solution.py:40
  6.9 0.0 collective-permute-start.3
  6.9 1.3 %collective-permute-start.4 = (f32[8,512]{1,0:T(8,128)S(1)}, f32[8,512]{1,0:T(8,128)S(1)}, u32[]{:S(2)}, u32[]{:S(2)}) collective-permute-start(f32[8,512]{1,0:T(8,128)S(1)} %get-tuple-element.36.sz), channel_id=1, source_target_pairs={{0,1},{1,0},{2,3},{3,2},{4,5},{5,4},{6,7},{7,6},{8,9},{9,8},{10,11... | collective-permute-start | bytes 49160 | tf_op jit(solution)/shard_map/faces_in/ppermute | solution.py:40
  8.3 0.0 copy-start.12
  8.3 0.0 copy-start.13
  8.3 0.3 %own_part.1 = (f32[640,128]{1,0:T(8,128)S(1)}, f32[16,32,128]{2,1,0:T(8,128)S(1)}, f32[16,32,128]{2,1,0:T(8,128)S(1)}, f32[720,256]{1,0:T(8,128)S(1)}, f32[8,128]{1,0:T(8,128)S(1)}) custom-call(f32[16,32,128]{2,1,0:T(8,128)S(1)} %convert_multiply_fusion.masked, s32[16,32,128]{2,1,0:T(8,128)S(1)} %copy-done, f32[16,32,128]{2,1,0:T(8,128)S(1)} %copy-done.3, ...), custom_call_target="tpu_custom_call" | custom-call | bytes 1048576 | tf_op jit(solution)/shard_map/own_part/pallas_call | solution.py:447
  8.6 2.1 %collective-permute-done.4.rz = f32[8,512]{1,0:T(8,128)S(1)} collective-permute-done((f32[8,512]{1,0:T(8,128)S(1)}, f32[8,512]{1,0:T(8,128)S(1)}, u32[]{:S(2)}, u32[]{:S(2)}) %collective-permute-start.4) | collective-permute-done | bytes 16416 | tf_op jit(solution)/shard_map/faces_in/ppermute | solution.py:40
  10.7 0.0 collective-permute-done.2.ry0
  10.7 0.0 collective-permute-done.3.ry1
  10.7 0.0 collective-permute-done.rx0
  10.7 0.0 collective-permute-done.1.rx1
  10.8 1.4 %solve.1 = (f32[16,32,128]{2,1,0:T(8,128)S(1)}, f32[2,32,128]{2,1,0:T(8,128)S(1)}, f32[3,32,128]{2,1,0:T(8,128)S(1)}, f32[6,16,128]{2,1,0:T(8,128)S(1)}, f32[6,1...) custom-call(f32[640,128]{1,0:T(8,128)S(1)} %get-tuple-element.38.modes, f32[720,256]{1,0:T(8,128)S(1)} %get-tuple-element.39.factors, ...), custom_call_target="tpu_custom_call" | custom-call | bytes 1048576 | tf_op jit(solution)/shard_map/solve/pallas_call | solution.py:447
  12.2 1.3 %collective-permute-start.6 = (f32[3,32,128]{2,1,0:T(8,128)S(1)}, f32[3,32,128]{2,1,0:T(8,128)S(1)}, u32[]{:S(2)}, u32[]{:S(2)}) collective-permute-start(f32[3,32,128]{2,1,0:T(8,128)S(1)} %get-tuple-element.43.tx1), channel_id=1, source_target_pairs={{0,1},{1,0},{2,3},{3,2},{4,5},{5,4},{6,7},{7,6},{8,16},{9,17},{10,... | collective-permute-start | bytes 147464 | tf_op jit(solution)/shard_map/faces_out/ppermute | solution.py:40
  13.5 2.3 %collective-permute-start.7 = (f32[6,16,128]{2,1,0:T(8,128)S(1)}, f32[6,16,128]{2,1,0:T(8,128)S(1)}, u32[]{:S(2)}, u32[]{:S(2)}) collective-permute-start(f32[6,16,128]{2,1,0:T(8,128)S(1)} %get-tuple-element.44.ty0), channel_id=1, source_target_pairs={{0,2},{1,3},{2,0},{3,1},{4,6},{5,7},{6,4},{7,5},{8,10},{9,11},{10,... | collective-permute-start | bytes 147464 | tf_op jit(solution)/shard_map/faces_out/ppermute | solution.py:40
  15.9 0.0 collective-permute-start.8
  15.9 1.5 %collective-permute-start.9 = (f32[24,512]{1,0:T(8,128)S(1)}, f32[24,512]{1,0:T(8,128)S(1)}, u32[]{:S(2)}, u32[]{:S(2)}) collective-permute-start(f32[24,512]{1,0:T(8,128)S(1)} %get-tuple-element.46.tz), channel_id=1, source_target_pairs={{0,1},{1,0},{2,3},{3,2},{4,5},{5,4},{6,7},{7,6},{8,9},{9,8},{10,11... | collective-permute-start | bytes 147464 | tf_op jit(solution)/shard_map/faces_out/ppermute | solution.py:40
  17.4 0.2 collective-permute-start.5
  18.3 0.6 %links.1 = (f32[16,32,128]{2,1,0:T(8,128)S(1)}, f32[17,32,128]{2,1,0:T(8,128)S(1)}, f32[16,32,128]{2,1,0:T(8,128)S(1)}, f32[16,128]{1,0:T(8,128)S(1)}, f32[16,32...) custom-call(f32[1]{0:T(128)S(6)} %copy.18.rz_prev, ...), custom_call_target="tpu_custom_call" | custom-call | bytes 1048576 | tf_op jit(solution)/shard_map/links/pallas_call | solution.py:447
  18.8 0.0 collective-permute-done.5.qx0
  18.9 0.0 collective-permute-done.6.qx1
  18.9 0.0 collective-permute-done.7.qy0
  18.9 0.0 collective-permute-done.8.qy1
  18.9 1.1 %collective-permute-done.9.qz = f32[24,512]{1,0:T(8,128)S(1)} collective-permute-done((f32[24,512]{1,0:T(8,128)S(1)}, f32[24,512]{1,0:T(8,128)S(1)}, u32[]{:S(2)}, u32[]{:S(2)}) %collective-permute-start.9) | collective-permute-done | bytes 49184 | tf_op jit(solution)/shard_map/faces_out/ppermute | solution.py:40
  20.0 0.7 %image.1 = (f32[16,32,128]{2,1,0:T(8,128)S(1)}, f32[16,32,128]{2,1,0:T(8,128)S(1)}, f32[32,1,128]{2,1,0:T(1,128)S(1)}) custom-call(f32[16,32,128]{2,1,0:T(8,128)S(1)} %convert_multiply_fusion.masked, f32[16,32,128]{2,1,0:T(8,128)S(1)} %get-tuple-element.30.mask, f32[16,32,128]{2,1,0:T(8,128)S(1)} %get-tuple-element.31.d, ...), custom_call_target="tpu_custom_call" | custom-call | bytes 1048576 | tf_op jit(solution)/shard_map/image/pallas_call | solution.py:447
  20.7 9.6 %all_to_all.5.sums = f32[32,1,128]{2,1,0:T(1,128)S(1)} all-to-all(f32[32,1,128]{2,1,0:T(1,128)S(1)} %get-tuple-element.54), channel_id=1, replica_groups=mesh['gx'=4,'gy'=4,'gz'=2] {'gx','gy','gz'}, dimensions={0} | all-to-all | bytes 32768 | tf_op jit(solution)/shard_map/sums/all_to_all | solution.py:505
  30.4 1.3 %update.1 = (f32[16,32,128]{2,1,0:T(8,128)}, f32[16,32,128]{2,1,0:T(8,128)}, f32[16,32,128]{2,1,0:T(8,128)}) custom-call(f32[1,128]{1,0:T(1,128)S(1)} %get-tuple-element.37.rz_line, f32[32,1,128]{2,1,0:T(1,128)S(1)} %all_to_all.5.sums, f32[16,32,128]{2,1,0:T(8,128)S(1)} %copy-done.5, f32[16,32,128]{2,1,0:T(8,128)S(1)} %copy-done.2, ...), custom_call_target="tpu_custom_call" | custom-call | bytes 1048576 | tf_op jit(solution)/shard_map/update/pallas_call | solution.py:447
  (24 shorter events, 0.0 us)
Async XLA Ops:
  0.6 1.2 %copy-start = (s32[16,32,128]{2,1,0:T(8,128)S(1)}, s32[16,32,128]{2,1,0:T(8,128)}, u32[]{:S(2)}) copy-start(s32[16,32,128]{2,1,0:T(8,128)} %msk.3) | copy-start | bytes 786436
  0.6 1.2 %copy-start.1 = (f32[16,32,128]{2,1,0:T(8,128)S(1)}, f32[16,32,128]{2,1,0:T(8,128)}, u32[]{:S(2)}) copy-start(f32[16,32,128]{2,1,0:T(8,128)} %mu.5) | copy-start | bytes 786436
  0.7 1.2 %copy-start.3 = (f32[16,32,128]{2,1,0:T(8,128)S(1)}, f32[16,32,128]{2,1,0:T(8,128)}, u32[]{:S(2)}) copy-start(f32[16,32,128]{2,1,0:T(8,128)} %direction.3) | copy-start | bytes 786436
  1.9 6.3 %copy-start.4 = (bf16[160,256]{1,0:T(8,128)(2,1)S(1)}, bf16[160,256]{1,0:T(8,128)(2,1)}, u32[]{:S(2)}) copy-start(bf16[160,256]{1,0:T(8,128)(2,1)} %constant.20.clone.into) | copy-start | bytes 245764
  1.9 6.3 %copy-start.9 = (f32[40,256]{1,0:T(8,128)S(1)}, f32[40,256]{1,0:T(8,128)}, u32[]{:S(2)}) copy-start(f32[40,256]{1,0:T(8,128)} %constant.19.clone.middle) | copy-start | bytes 122884
  2.3 8.4 %collective-permute-start = (f32[4,32,128]{2,1,0:T(8,128)S(1)}, f32[4,32,128]{2,1,0:T(8,128)S(1)}, u32[]{:S(2)}, u32[]{:S(2)}) collective-permute-start(f32[4,32,128]{2,1,0:T(8,128)S(1)} %get-tuple-element.32), channel_id=1, source_target_pairs={{0,8},{1,9},{2,10},{3,11},{4,12},{5,13},{6,14},{7,15},{8,0},{9,1},... | collective-permute-start | bytes 196616 | tf_op jit(solution)/shard_map/faces_in/ppermute | solution.py:40
  2.8 8.0 %collective-permute-start.1 = (f32[4,32,128]{2,1,0:T(8,128)S(1)}, f32[4,32,128]{2,1,0:T(8,128)S(1)}, u32[]{:S(2)}, u32[]{:S(2)}) collective-permute-start(f32[4,32,128]{2,1,0:T(8,128)S(1)} %get-tuple-element.33), channel_id=1, source_target_pairs={{0,1},{1,0},{2,3},{3,2},{4,5},{5,4},{6,7},{7,6},{8,16},{9,17},{10,... | collective-permute-start | bytes 196616 | tf_op jit(solution)/shard_map/faces_in/ppermute | solution.py:40
  5.3 5.4 %collective-permute-start.2 = (f32[4,16,128]{2,1,0:T(8,128)S(1)}, f32[4,16,128]{2,1,0:T(8,128)S(1)}, u32[]{:S(2)}, u32[]{:S(2)}) collective-permute-start(f32[4,16,128]{2,1,0:T(8,128)S(1)} %get-tuple-element.34), channel_id=1, source_target_pairs={{0,2},{1,3},{2,0},{3,1},{4,6},{5,7},{6,4},{7,5},{8,10},{9,11},{10,... | collective-permute-start | bytes 98312 | tf_op jit(solution)/shard_map/faces_in/ppermute | solution.py:40
  6.9 3.8 %collective-permute-start.3 = (f32[4,16,128]{2,1,0:T(8,128)S(1)}, f32[4,16,128]{2,1,0:T(8,128)S(1)}, u32[]{:S(2)}, u32[]{:S(2)}) collective-permute-start(f32[4,16,128]{2,1,0:T(8,128)S(1)} %get-tuple-element.35), channel_id=1, source_target_pairs={{0,8},{1,9},{2,4},{3,5},{4,2},{5,3},{6,14},{7,15},{8,0},{9,1},{10,... | collective-permute-start | bytes 98312 | tf_op jit(solution)/shard_map/faces_in/ppermute | solution.py:40
  6.9 3.8 %copy-start.6 = (bf16[384,256]{1,0:T(8,128)(2,1)S(1)}, bf16[384,256]{1,0:T(8,128)(2,1)}, u32[]{:S(2)}) copy-start(bf16[384,256]{1,0:T(8,128)(2,1)} %constant.23.clone.back) | copy-start | bytes 589828
  6.9 3.9 %copy-start.7 = (bf16[256,256]{1,0:T(8,128)(2,1)S(1)}, bf16[256,256]{1,0:T(8,128)(2,1)}, u32[]{:S(2)}) copy-start(bf16[256,256]{1,0:T(8,128)(2,1)} %constant.25.clone.out) | copy-start | bytes 393220
  6.9 3.9 %copy-start.8 = (bf16[256,256]{1,0:T(8,128)(2,1)S(1)}, bf16[256,256]{1,0:T(8,128)(2,1)}, u32[]{:S(2)}) copy-start(bf16[256,256]{1,0:T(8,128)(2,1)} %constant.18.clone.fwd) | copy-start | bytes 393220
  6.9 3.8 %collective-permute-start.4 = (f32[8,512]{1,0:T(8,128)S(1)}, f32[8,512]{1,0:T(8,128)S(1)}, u32[]{:S(2)}, u32[]{:S(2)}) collective-permute-start(f32[8,512]{1,0:T(8,128)S(1)} %get-tuple-element.36.sz), channel_id=1, source_target_pairs={{0,1},{1,0},{2,3},{3,2},{4,5},{5,4},{6,7},{7,6},{8,9},{9,8},{10,11... | collective-permute-start | bytes 49160 | tf_op jit(solution)/shard_map/faces_in/ppermute | solution.py:40
  8.2 2.5 %copy-start.10 = (f32[40,128]{1,0:T(8,128)S(1)}, f32[40,128]{1,0:T(8,128)}, u32[]{:S(2)}) copy-start(f32[40,128]{1,0:T(8,128)} %constant.24.clone.rim) | copy-start | bytes 61444
  8.2 2.5 %copy-start.11 = (bf16[32,256]{1,0:T(8,128)(2,1)S(1)}, bf16[32,256]{1,0:T(8,128)(2,1)}, u32[]{:S(2)}) copy-start(bf16[32,256]{1,0:T(8,128)(2,1)} %constant.26.clone.out_ends) | copy-start | bytes 49156
  8.3 2.5 %copy-start.12 = (bf16[48,128]{1,0:T(8,128)(2,1)S(1)}, bf16[48,128]{1,0:T(8,128)(2,1)}, u32[]{:S(2)}) copy-start(bf16[48,128]{1,0:T(8,128)(2,1)} %constant.21.clone.one) | copy-start | bytes 36868
  8.3 2.5 %copy-start.13 = (f32[8,256]{1,0:T(8,128)S(1)}, f32[8,256]{1,0:T(8,128)}, u32[]{:S(2)}) copy-start(f32[8,256]{1,0:T(8,128)} %constant.22.clone.row_ends) | copy-start | bytes 24580
  12.2 6.6 %collective-permute-start.6 = (f32[3,32,128]{2,1,0:T(8,128)S(1)}, f32[3,32,128]{2,1,0:T(8,128)S(1)}, u32[]{:S(2)}, u32[]{:S(2)}) collective-permute-start(f32[3,32,128]{2,1,0:T(8,128)S(1)} %get-tuple-element.43.tx1), channel_id=1, source_target_pairs={{0,1},{1,0},{2,3},{3,2},{4,5},{5,4},{6,7},{7,6},{8,16},{9,17},{10,... | collective-permute-start | bytes 147464 | tf_op jit(solution)/shard_map/faces_out/ppermute | solution.py:40
  13.5 5.3 %collective-permute-start.7 = (f32[6,16,128]{2,1,0:T(8,128)S(1)}, f32[6,16,128]{2,1,0:T(8,128)S(1)}, u32[]{:S(2)}, u32[]{:S(2)}) collective-permute-start(f32[6,16,128]{2,1,0:T(8,128)S(1)} %get-tuple-element.44.ty0), channel_id=1, source_target_pairs={{0,2},{1,3},{2,0},{3,1},{4,6},{5,7},{6,4},{7,5},{8,10},{9,11},{10,... | collective-permute-start | bytes 147464 | tf_op jit(solution)/shard_map/faces_out/ppermute | solution.py:40
  15.9 3.0 %collective-permute-start.8 = (f32[6,16,128]{2,1,0:T(8,128)S(1)}, f32[6,16,128]{2,1,0:T(8,128)S(1)}, u32[]{:S(2)}, u32[]{:S(2)}) collective-permute-start(f32[6,16,128]{2,1,0:T(8,128)S(1)} %get-tuple-element.45.ty1), channel_id=1, source_target_pairs={{0,8},{1,9},{2,4},{3,5},{4,2},{5,3},{6,14},{7,15},{8,0},{9,1},{10,... | collective-permute-start | bytes 147464 | tf_op jit(solution)/shard_map/faces_out/ppermute | solution.py:40
  15.9 4.2 %collective-permute-start.9 = (f32[24,512]{1,0:T(8,128)S(1)}, f32[24,512]{1,0:T(8,128)S(1)}, u32[]{:S(2)}, u32[]{:S(2)}) collective-permute-start(f32[24,512]{1,0:T(8,128)S(1)} %get-tuple-element.46.tz), channel_id=1, source_target_pairs={{0,1},{1,0},{2,3},{3,2},{4,5},{5,4},{6,7},{7,6},{8,9},{9,8},{10,11... | collective-permute-start | bytes 147464 | tf_op jit(solution)/shard_map/faces_out/ppermute | solution.py:40
  17.4 1.4 %collective-permute-start.5 = (f32[2,32,128]{2,1,0:T(8,128)S(1)}, f32[2,32,128]{2,1,0:T(8,128)S(1)}, u32[]{:S(2)}, u32[]{:S(2)}) collective-permute-start(f32[2,32,128]{2,1,0:T(8,128)S(1)} %get-tuple-element.42.tx0), channel_id=1, source_target_pairs={{0,8},{1,9},{2,10},{3,11},{4,12},{5,13},{6,14},{7,15},{8,0},{9,1},... | collective-permute-start | bytes 98312 | tf_op jit(solution)/shard_map/faces_out/ppermute | solution.py:40
  20.0 10.3 %copy-start.2 = (f32[16,32,128]{2,1,0:T(8,128)S(1)}, f32[16,32,128]{2,1,0:T(8,128)}, u32[]{:S(2)}) copy-start(f32[16,32,128]{2,1,0:T(8,128)} %res.1) | copy-start | bytes 786436
  20.0 10.3 %copy-start.5 = (f32[16,32,128]{2,1,0:T(8,128)S(1)}, f32[16,32,128]{2,1,0:T(8,128)}, u32[]{:S(2)}) copy-start(f32[16,32,128]{2,1,0:T(8,128)} %iterate.1) | copy-start | bytes 786436
